TPU v7x, 512 devices: a whole 4x4x16 slice. The times are simulated.
512 devices in a mesh: dp: 16 (over x, z_hi), row: 4 (over z_lo), col: 8 (over y, core).
Axes of the slice: x: 4, y: 4, z: 16 (z_hi: 4, z_lo: 4; z = z_hi * 4 + z_lo), core: 2. Of those that a mesh axis runs over, the one named last changes fastest.
Arguments:
- queries: bfloat16 [16, 48, 128, 1024], P('dp', 'row', 'col'), may hold values from -6 to 6
- keyvals: bfloat16 [16, 2, 48, 128, 1024], P('dp', None, 'row', 'col'), may hold values from -6 to 6
- out_weight: bfloat16 [16, 1024, 2048], P('dp', ('row', 'col')), may hold values from -0.75 to 0.75
- gate_weight: bfloat16 [16, 2048, 2048], P('dp', ('row', 'col')), may hold values from -0.125 to 0.125
- class_table: bfloat16 [16, 1000, 2048], P('dp', None, ('row', 'col')), may hold values from -5 to 5
- labels: int32 [16], P('dp'), may hold values from 0 to 999
- timesteps: int32 [16], P('dp'), may hold values from 0 to 999
- round_index: int32 [1], replicated, may hold values from 0 to 996
Outputs:
- update: bfloat16 [16, 48, 128, 2048], P('dp', 'row', 'col')
All inputs are finite; a program needn't handle non-finite values.
Results may differ from a plain program's by a relative error of at most 0.0081.
Values may be sent and summed in bfloat16 or wider, within the bound.
No kernel may reach another device: no remote copies, remote signals or barrier semaphores. Data moves between devices by JAX's collectives and lax.ppermute only.
A program may use at most 64 MiB of HBM per device.

v0:
```python
from functools import partial
import math

import jax
import jax.numpy as jnp
from jax import lax
from jax.sharding import PartitionSpec as P

HDIM = 128
RADIUS = 3


def shortened(value):

    def short(part):
        return part.astype(jnp.bfloat16) if part.dtype == jnp.float32 else part

    return jax.tree.map(short, value)


def from_behind(value, axis, steps):
    count = lax.axis_size(axis)
    pairs = [(source, (source + steps) % count) for source in range(count)]
    return lax.ppermute(value, axis, pairs)


def padded(value, sides, width):
    for axis, dim in sides:
        size, length = (lax.axis_size(axis), value.shape[dim])
        up = [(i, (i + 1) % size) for i in range(size - 1)]
        down = [(j, i) for i, j in up]
        last = lax.slice_in_dim(value, length - width, length, axis=dim)
        leading = lax.slice_in_dim(value, 0, width, axis=dim)
        before = lax.ppermute(last, axis, up)
        after = lax.ppermute(leading, axis, down)
        value = jnp.concatenate([before, value, after], axis=dim)
    return value


def gossip_from(packed, distance):
    return jax.tree.map(
        lambda part, own: part.astype(own.dtype),
        from_behind(shortened(packed), "dp", distance),
        packed,
    )


def local(queries, keyvals, out_weight, gate_weight, class_table, labels, timesteps, round_index):
    bit_count = lax.axis_size("dp").bit_length() - 1
    shard_inner = out_weight.shape[1]
    model_width = out_weight.shape[2]
    shard_width = gate_weight.shape[1]
    class_count = class_table.shape[1]
    packed = jnp.concatenate(
        [out_weight.reshape(-1), gate_weight.reshape(-1), class_table.reshape(-1)]
    )
    branches = [partial(gossip_from, distance=2**power) for power in range(bit_count)]
    peer_params = lax.switch(round_index[0] % bit_count, branches, packed)
    mixed = (0.5 * (packed.astype(jnp.float32) + peer_params.astype(jnp.float32))).astype(
        jnp.bfloat16
    )
    out_size = shard_inner * model_width
    gate_size = shard_width * model_width
    out_mixed = mixed[:out_size].reshape(shard_inner, model_width)
    gate_mixed = mixed[out_size : out_size + gate_size].reshape(shard_width, model_width)
    table_mixed = mixed[out_size + gate_size :].reshape(class_count, shard_width)
    half_width = model_width // 2
    positions = lax.axis_index(("row", "col")) * shard_width + jnp.arange(shard_width)
    freq_index = (positions % half_width).astype(jnp.float32)
    frequency = jnp.exp(-math.log(10000.0) * freq_index / half_width)
    angle_value = timesteps[0].astype(jnp.float32) * frequency
    embed = jnp.where(positions < half_width, jnp.cos(angle_value), jnp.sin(angle_value))
    class_row = lax.dynamic_index_in_dim(table_mixed, labels[0], 0, keepdims=False)
    cond = jax.nn.silu(class_row.astype(jnp.float32) + embed).astype(jnp.bfloat16)
    partial_gate = jnp.dot(cond[None, :], gate_mixed, preferred_element_type=jnp.float32)[0]
    gate = lax.psum(partial_gate, ("row", "col"))
    tile_rows = queries.shape[1]
    tile_cols = queries.shape[2]
    inner_width = queries.shape[3]
    head_count = inner_width // HDIM
    window = 2 * RADIUS + 1
    ext_cols = tile_cols + 2 * RADIUS
    local_kv = keyvals[0]
    extended = padded(local_kv, (("row", 1), ("col", 2)), RADIUS)
    banded = jnp.stack(
        [extended[:, offset : offset + tile_rows] for offset in range(window)], axis=2
    )
    banded = banded.reshape(2, tile_rows, window * ext_cols, head_count, HDIM)
    query_heads = queries[0].reshape(tile_rows, tile_cols, head_count, HDIM)
    score_scale = 1.0 / math.sqrt(HDIM)
    scores = (
        jnp.einsum("ijhd,ikhd->ihjk", query_heads, banded[0], preferred_element_type=jnp.float32)
        * score_scale
    )
    row_global = lax.axis_index("row") * tile_rows + jnp.arange(tile_rows + 2 * RADIUS) - RADIUS
    row_valid = (row_global >= 0) & (row_global < tile_rows * lax.axis_size("row"))
    row_band = jnp.stack(
        [row_valid[offset : offset + tile_rows] for offset in range(window)], axis=1
    )
    col_global = lax.axis_index("col") * tile_cols + jnp.arange(ext_cols) - RADIUS
    col_valid = (col_global >= 0) & (col_global < tile_cols * lax.axis_size("col"))
    reach = (
        jnp.abs(jnp.arange(ext_cols)[None, :] - jnp.arange(tile_cols)[:, None] - RADIUS) <= RADIUS
    )
    allowed = (
        row_band[:, None, None, :, None]
        & col_valid[None, None, None, None, :]
        & reach[None, None, :, None, :]
    )
    allowed = allowed.reshape(tile_rows, 1, tile_cols, window * ext_cols)
    scores = jnp.where(allowed, scores, jnp.float32(-1e30))
    row_max = jnp.max(scores, axis=-1, keepdims=True)
    exponent = jnp.exp(scores - row_max)
    probs = (exponent / jnp.sum(exponent, axis=-1, keepdims=True)).astype(jnp.bfloat16)
    attended = jnp.einsum("ihjk,ikhd->ijhd", probs, banded[1], preferred_element_type=jnp.float32)
    attended = attended.astype(jnp.bfloat16).reshape(tile_rows * tile_cols, inner_width)
    projected = jnp.dot(
        attended,
        lax.all_gather(out_mixed, ("row", "col"), axis=0, tiled=True),
        preferred_element_type=jnp.float32,
    )
    result = (gate[None, :] * projected).astype(jnp.bfloat16)
    return result.reshape(1, tile_rows, tile_cols, model_width)


def solution(mesh):
    placed = (
        P("dp", "row", "col", None),
        P("dp", None, "row", "col", None),
        P("dp", ("row", "col"), None),
        P("dp", ("row", "col"), None),
        P("dp", None, ("row", "col")),
        P("dp"),
        P("dp"),
        P(),
    )
    return jax.shard_map(
        local, mesh=mesh, in_specs=placed, out_specs=P("dp", "row", "col", None), check_vma=False
    )
```

profile of v0, /device:TPU:1, one launch (start us, length us, event | category | flops | bytes accessed | tf_op | source)
XLA Modules:
  0.0 165.4 jit_solution(17559823692384981982)
XLA Ops:
  7.3 0.9 copy.19
  8.3 1.0 copy.20
  9.2 1.1 copy.11
  10.4 0.2 reshape.152
  10.6 13.6 %conditional.4 = (bf16[260608]{0:T(1024)(128)(2,1)}) conditional(s32[]{:T(128)} %clamp.3, bf16[260608]{0:T(1024)(128)(2,1)S(1)} %constant_dynamic-update-slice_fusion.1, bf16[260608]{0:T(1024)(128)(2,1)S(1)} %constant_dynamic-update-slice_fusion.1, ...), branch_computations={%region_0.1_spmd, %region_1.2_spmd, %region_2.3_spmd, %region_3.4_... | conditional | bytes 2084912
  10.6 5.5 %collective-permute-start.3 = (bf16[260608]{0:T(1024)(128)(2,1)S(1)}, bf16[260608]{0:T(1024)(128)(2,1)}, u32[]{:S(2)}, u32[]{:S(2)}) collective-permute-start(bf16[260608]{0:T(1024)(128)(2,1)S(1)} %param.3), channel_id=1, source_target_pairs={{0,256},{32,288},{64,320},{96,352},{128,384},{160,416},{192,448},{... | collective-permute-start | bytes 1563656 | tf_op jit(solution)/shard_map/cond/branch_3_fun/ppermute | solution.py:24
  16.1 8.1 %collective-permute-done.3 = bf16[260608]{0:T(1024)(128)(2,1)} collective-permute-done((bf16[260608]{0:T(1024)(128)(2,1)S(1)}, bf16[260608]{0:T(1024)(128)(2,1)}, u32[]{:S(2)}, u32[]{:S(2)}) %collective-permute-start.3) | collective-permute-done | bytes 521248 | tf_op jit(solution)/shard_map/cond/branch_3_fun/ppermute | solution.py:24
  24.2 1.2 multiply_convert_fusion
  25.4 0.7 reshape.156
  26.1 0.0 all-gather.2.cloned.1.call-update
  26.2 7.1 %collective-permute-start.4 = (bf16[2,3,16,1024]{3,2,1,0:T(8,128)(2,1)S(1)}, bf16[2,3,16,1024]{3,2,1,0:T(8,128)(2,1)S(1)}, u32[]{:S(2)}, u32[]{:S(2)}) collective-permute-start(bf16[2,3,16,1024]{3,2,1,0:T(8,128)(2,1)S(1)} %get-tuple-element.24), channel_id=1, source_target_pairs={{0,8},{8,16},{16,24},{1,9},{9,17},{17,25},{2,10},{10,18},{18,26},{... | collective-permute-start | bytes 589832 | tf_op jit(solution)/shard_map/ppermute | solution.py:34
  33.3 1.3 collective-permute-start.5
  34.6 0.1 slice_bitcast_fusion.7
  34.8 0.1 copy.13
  34.9 0.1 and.85
  35.0 0.1 and.86
  35.1 0.1 and.89
  35.2 0.1 and.94
  35.3 0.1 copy.21
  35.4 0.1 reshape.154
  35.5 0.1 slice.82
  37.0 0.2 fusion.33
  37.2 72.2 %psum.7 = f32[2048]{0:T(1024)S(1)} all-reduce(f32[2048]{0:T(1024)S(1)} %bitcast.90), channel_id=1, replica_groups=mesh['dp'=16,'row'=4,'col'=8] {'row','col'}, use_global_device_ids=true, to_apply=%region_4.5 | all-reduce | flops 2048 | bytes 16384 | tf_op jit(solution)/shard_map/psum | solution.py:76
  109.5 0.0 collective-permute-done.4
  109.5 0.0 collective-permute-done.5
  109.5 0.3 pad_maximum_fusion.3
  109.7 1.9 %collective-permute-start.6 = (bf16[2,18,3,1024]{3,2,1,0:T(4,128)(2,1)S(1)}, bf16[2,18,3,1024]{3,2,1,0:T(4,128)(2,1)S(1)}, u32[]{:S(2)}, u32[]{:S(2)}) collective-permute-start(bf16[2,18,3,1024]{3,2,1,0:T(4,128)(2,1)S(1)} %get-tuple-element.22), channel_id=1, source_target_pairs={{0,1},{1,2},{2,3},{3,4},{4,5},{5,6},{6,7},{8,9},{9,10},{10,11},{11... | collective-permute-start | bytes 663560 | tf_op jit(solution)/shard_map/ppermute | solution.py:34
  111.7 5.6 %collective-permute-start.7 = (bf16[2,18,3,1024]{3,2,1,0:T(4,128)(2,1)S(1)}, bf16[2,18,3,1024]{3,2,1,0:T(4,128)(2,1)S(1)}, u32[]{:S(2)}, u32[]{:S(2)}) collective-permute-start(bf16[2,18,3,1024]{3,2,1,0:T(4,128)(2,1)S(1)} %get-tuple-element.23), channel_id=1, source_target_pairs={{1,0},{2,1},{3,2},{4,3},{5,4},{6,5},{7,6},{9,8},{10,9},{11,10},{12... | collective-permute-start | bytes 663560 | tf_op jit(solution)/shard_map/ppermute | solution.py:35
  117.3 0.0 collective-permute-done.6
  117.3 2.4 %collective-permute-done.7 = bf16[2,18,3,1024]{3,2,1,0:T(4,128)(2,1)S(1)} collective-permute-done((bf16[2,18,3,1024]{3,2,1,0:T(4,128)(2,1)S(1)}, bf16[2,18,3,1024]{3,2,1,0:T(4,128)(2,1)S(1)}, u32[]{:S(2)}, u32[]{:S(2)}) %collective-permute-start.7) | collective-permute-done | bytes 221216 | tf_op jit(solution)/shard_map/ppermute | solution.py:35
  119.7 0.9 pad_maximum_fusion
  120.7 0.1 fusion.22
  120.7 0.1 fusion.21
  120.8 0.1 fusion.20
  120.9 0.1 fusion.19
  121.0 0.1 fusion.18
  121.1 0.1 fusion.17
  121.2 0.1 fusion.16
  121.3 2.5 %fusion.58 = (bf16[1,12,7,22,1024]{4,3,1,0,2:T(8,128)(2,1)S(1)}, bf16[1,12,7,22,1024]{4,3,1,0,2:T(8,128)(2,1)}) fusion(bf16[2,12,7,22,1024]{4,3,1,0,2:T(8,128)(2,1)S(1)} %fusion.16), kind=kLoop, calls=%fused_computation.85 | loop fusion | bytes 15138816 | tf_op jit(solution)/shard_map/slice | solution.py:92
  123.8 2.4 %copy.14 = bf16[1,12,7,22,1024]{4,3,2,1,0:T(8,128)(2,1)} copy(bf16[1,12,7,22,1024]{4,3,1,0,2:T(8,128)(2,1)S(1)} %get-tuple-element.20) | data formatting | bytes 7569408 | tf_op jit(solution)/shard_map/slice | solution.py:92
  126.1 7.2 %squeeze.23 = bf16[12,154,8,128]{3,2,1,0:T(8,128)(2,1)} reshape(bf16[1,12,7,22,1024]{4,3,2,1,0:T(8,128)(2,1)} %copy.14) | data formatting | bytes 7569408 | tf_op jit(solution)/shard_map/squeeze | solution.py:92
  133.3 4.6 %copy.12 = bf16[1,12,7,22,1024]{4,3,2,1,0:T(8,128)(2,1)} copy(bf16[1,12,7,22,1024]{4,3,1,0,2:T(8,128)(2,1)} %get-tuple-element.21) | data formatting | bytes 7569408 | tf_op jit(solution)/shard_map/slice | solution.py:115
  137.9 7.2 %squeeze.22 = bf16[12,154,8,128]{3,2,1,0:T(8,128)(2,1)} reshape(bf16[1,12,7,22,1024]{4,3,2,1,0:T(8,128)(2,1)} %copy.12) | data formatting | bytes 7569408 | tf_op jit(solution)/shard_map/squeeze | solution.py:115
  145.0 5.6 %fusion.60 = (f32[12,8,16]{2,1,0:T(8,128)S(1)}, f32[12,8,16,154]{3,2,1,0:T(8,128)}) fusion(bf16[12,154,8,128]{3,2,1,0:T(8,128)(2,1)} %squeeze.23, pred[12,16,154]{2,1,0:T(8,128)(4,1)S(1)} %broadcast_and_fusion, bf16[12,16,8,128]{3,2,1,0:T(8,128)(2,1)S(1)} %bitcast.86), kind=kOutput, calls=%fused_computation.87 | convolution fusion | flops 61501592 | bytes 5159808 | tf_op jit(solution)/shard_map/sub | solution.py:113
  150.6 3.7 %fusion.13 = bf16[12,16,8,128]{3,1,2,0:T(8,128)(2,1)S(1)} fusion(bf16[12,154,8,128]{3,2,1,0:T(8,128)(2,1)} %squeeze.22, f32[12,8,16,154]{3,2,1,0:T(8,128)} %get-tuple-element.34, f32[12,8,16]{2,1,0:T(8,128)S(1)} %get-tuple-element.33), kind=kOutput, calls=%fused_computation.13 | convolution fusion | flops 61224960 | bytes 5130240 | tf_op jit(solution)/shard_map/ihjk,ikhd->ijhd/dot_general | solution.py:115
  154.3 0.1 copy.18
  154.4 0.0 all-gather.2.cloned.1.call-done
  154.5 4.1 %fusion.5 = bf16[192,2048]{1,0:T(8,128)(2,1)} fusion(bf16[1024,2048]{1,0:T(8,128)(2,1)} %all-gather.2.cloned.1.call-done, f32[2048]{0:T(1024)S(1)} %psum.7, bf16[24,8,8,128]{3,2,1,0:T(8,128)(2,1)S(1)} %bitcast.87), kind=kOutput, calls=%fused_computation.6 | convolution fusion | flops 806092800 | bytes 5382144 | tf_op jit(solution)/shard_map/dot_general | solution.py:117
  (20 shorter events, 0.2 us)
Async XLA Ops:
  6.5 19.6 %copy-start = (bf16[1,2,12,16,1024]{4,3,2,1,0:T(8,128)(2,1)S(1)}, bf16[1,2,12,16,1024]{4,3,2,1,0:T(8,128)(2,1)}, u32[]{:S(2)}) copy-start(bf16[1,2,12,16,1024]{4,3,2,1,0:T(8,128)(2,1)} %param.13) | copy-start | bytes 2359300
  6.5 28.8 %copy-start.1 = (bf16[1,12,16,1024]{3,2,1,0:T(8,128)(2,1)S(1)}, bf16[1,12,16,1024]{3,2,1,0:T(8,128)(2,1)}, u32[]{:S(2)}) copy-start(bf16[1,12,16,1024]{3,2,1,0:T(8,128)(2,1)} %param.12) | copy-start | bytes 1179652
  6.5 147.9 %all-gather.2.cloned.1.call-start = ((), (), s32[]{:S(2)}) async-start(), calls=%async_computation | async-start | bytes 4325376 | tf_op jit(solution)/shard_map/all_gather | solution.py:119
  10.6 13.6 %collective-permute-start.3 = (bf16[260608]{0:T(1024)(128)(2,1)S(1)}, bf16[260608]{0:T(1024)(128)(2,1)}, u32[]{:S(2)}, u32[]{:S(2)}) collective-permute-start(bf16[260608]{0:T(1024)(128)(2,1)S(1)} %param.3), channel_id=1, source_target_pairs={{0,256},{32,288},{64,320},{96,352},{128,384},{160,416},{192,448},{... | collective-permute-start | bytes 1563656 | tf_op jit(solution)/shard_map/cond/branch_3_fun/ppermute | solution.py:24
  26.2 83.3 %collective-permute-start.4 = (bf16[2,3,16,1024]{3,2,1,0:T(8,128)(2,1)S(1)}, bf16[2,3,16,1024]{3,2,1,0:T(8,128)(2,1)S(1)}, u32[]{:S(2)}, u32[]{:S(2)}) collective-permute-start(bf16[2,3,16,1024]{3,2,1,0:T(8,128)(2,1)S(1)} %get-tuple-element.24), channel_id=1, source_target_pairs={{0,8},{8,16},{16,24},{1,9},{9,17},{17,25},{2,10},{10,18},{18,26},{... | collective-permute-start | bytes 589832 | tf_op jit(solution)/shard_map/ppermute | solution.py:34
  33.3 76.2 %collective-permute-start.5 = (bf16[2,3,16,1024]{3,2,1,0:T(8,128)(2,1)S(1)}, bf16[2,3,16,1024]{3,2,1,0:T(8,128)(2,1)S(1)}, u32[]{:S(2)}, u32[]{:S(2)}) collective-permute-start(bf16[2,3,16,1024]{3,2,1,0:T(8,128)(2,1)S(1)} %get-tuple-element.25), channel_id=1, source_target_pairs={{8,0},{16,8},{24,16},{9,1},{17,9},{25,17},{10,2},{18,10},{26,18},{... | collective-permute-start | bytes 589832 | tf_op jit(solution)/shard_map/ppermute | solution.py:35
  109.7 7.6 %collective-permute-start.6 = (bf16[2,18,3,1024]{3,2,1,0:T(4,128)(2,1)S(1)}, bf16[2,18,3,1024]{3,2,1,0:T(4,128)(2,1)S(1)}, u32[]{:S(2)}, u32[]{:S(2)}) collective-permute-start(bf16[2,18,3,1024]{3,2,1,0:T(4,128)(2,1)S(1)} %get-tuple-element.22), channel_id=1, source_target_pairs={{0,1},{1,2},{2,3},{3,4},{4,5},{5,6},{6,7},{8,9},{9,10},{10,11},{11... | collective-permute-start | bytes 663560 | tf_op jit(solution)/shard_map/ppermute | solution.py:34
  111.7 8.0 %collective-permute-start.7 = (bf16[2,18,3,1024]{3,2,1,0:T(4,128)(2,1)S(1)}, bf16[2,18,3,1024]{3,2,1,0:T(4,128)(2,1)S(1)}, u32[]{:S(2)}, u32[]{:S(2)}) collective-permute-start(bf16[2,18,3,1024]{3,2,1,0:T(4,128)(2,1)S(1)} %get-tuple-element.23), channel_id=1, source_target_pairs={{1,0},{2,1},{3,2},{4,3},{5,4},{6,5},{7,6},{9,8},{10,9},{11,10},{12... | collective-permute-start | bytes 663560 | tf_op jit(solution)/shard_map/ppermute | solution.py:35
Sparse Core Ops, SparseCore 0:
  26.3 77.2 all-gather.1
where the time goes:
time: 166 us; the launch traced here: 165 us
  blocking collectives  72.2 us (43%)
  local copies, waits for them, and re-layouts  29.4 us (18%)
  starting transfers between devices  21.4 us (13%)
  between operations  15.8 us (10%)
  matrix products  13.6 us (8%)
  waiting for transfers between devices  10.5 us (6%)
  other arithmetic  2.46 us (1%)
    psum x1, blocking collectives, local(): gate = lax.psum(partial_gate, ('row', 'col'))  72.2 us
    ppermute x2, starting transfers between devices, padded(): before = lax.ppermute(last, axis, up)  8.98 us
    ppermute x1, waiting for transfers between devices, from_behind(): return lax.ppermute(value, axis, pairs)  8.11 us
    squeeze x1, local copies, waits for them, and re-layouts, local(): banded[0]  7.17 us
    squeeze x1, local copies, waits for them, and re-layouts, local(): banded[1]  7.17 us
    ppermute x2, starting transfers between devices, padded(): after = lax.ppermute(leading, axis, down)  6.9 us
    sub x1, matrix products, local(): exponent = jnp.exp(scores - row_max)  5.56 us
    ppermute x1, starting transfers between devices, from_behind(): return lax.ppermute(value, axis, pairs)  5.48 us
  transfers between devices with their start and end apart: 6, of which 2 were waited for; matrix products, arithmetic and copies ran while one was open for 22% of the time, Pallas kernels for 0%

commit v1 on v0

v1 whole, which is shorter than its diff:
```python
import math

import jax
import jax.numpy as jnp
from jax import lax
from jax.experimental import pallas as pl
from jax.experimental.pallas import tpu as pltpu
from jax.sharding import PartitionSpec as P

HDIM = 128
RADIUS = 3
F32 = jnp.float32
BF16 = jnp.bfloat16
GROUP = 4
EDGE = 4
PAD_ROWS = 2


def attend_kernel(q_ref, kv_ref, up_ref, down_ref, near_ref, far_ref, out_ref):
    rows, cols = 12, 16
    inner = q_ref.shape[1]
    row0 = lax.axis_index("row") * rows
    col_index = lax.axis_index("col")
    col0 = col_index * cols
    core = lax.rem(col_index, 2)
    near_base = jnp.where(core == 0, cols, -EDGE)
    far_base = jnp.where(core == 0, -EDGE, cols)
    queries = GROUP * cols
    band = (GROUP + 2 * RADIUS) * cols
    side = (GROUP + 2 * RADIUS + PAD_ROWS) * EDGE
    keys = band + 2 * side
    halo = RADIUS * cols
    factor = math.log2(math.e) / math.sqrt(HDIM)
    q_id = lax.broadcasted_iota(jnp.int32, (queries, keys), 0)
    k_id = lax.broadcasted_iota(jnp.int32, (queries, keys), 1)
    q_row, q_col = q_id // cols, q_id % cols
    side_id = jnp.where(k_id < band + side, k_id - band, k_id - band - side)
    k_row = jnp.where(k_id < band, k_id // cols, side_id // EDGE)
    base = jnp.where(k_id < band + side, near_base, far_base)
    k_col = jnp.where(k_id < band, k_id % cols, base + side_id % EDGE)
    d_row, d_col = k_row - q_row, k_col - q_col
    reach = (d_row >= 0) & (d_row <= 2 * RADIUS) & (d_col >= -RADIUS) & (d_col <= RADIUS)
    k_gcol = col0 + k_col
    reach = reach & (k_gcol >= 0) & (k_gcol < cols * lax.axis_size("col"))
    ones = jnp.ones((keys, HDIM), BF16)
    for group in range(rows // GROUP):
        k_grow = row0 + GROUP * group - RADIUS + k_row
        allowed = reach & (k_grow >= 0) & (k_grow < rows * lax.axis_size("row"))
        bias = jnp.where(allowed, F32(0.0), F32(-1e30))
        first = (GROUP * group - RADIUS) * cols
        last = first + band
        for head in range(inner // HDIM):
            lanes = slice(head * HDIM, (head + 1) * HDIM)

            def gathered(which):
                parts = []
                if first < 0:
                    parts.append(up_ref[which, halo + first : halo, lanes])
                parts.append(kv_ref[which, max(first, 0) : min(last, rows * cols), lanes])
                if last > rows * cols:
                    parts.append(down_ref[which, 0 : last - rows * cols, lanes])
                span = slice(GROUP * group * EDGE, GROUP * group * EDGE + side)
                parts.append(near_ref[which, span, lanes])
                parts.append(far_ref[which, span, lanes])
                return jnp.concatenate(parts, axis=0)

            q = q_ref[group * queries : (group + 1) * queries, lanes]
            scores = lax.dot_general(
                q, gathered(0), (((1,), (1,)), ((), ())), preferred_element_type=F32
            )
            scores = scores + bias
            top = jnp.max(scores, axis=-1, keepdims=True)
            weight = jnp.exp2((scores - top) * factor).astype(BF16)
            values = jnp.concatenate([gathered(1), ones], axis=1)
            both = jnp.dot(weight, values, preferred_element_type=F32)
            out_ref[group * queries : (group + 1) * queries, lanes] = (
                both[:, :HDIM] / both[:, HDIM:]
            ).astype(BF16)


def attend(q, kv, up, down, near, far):
    tokens, inner = q.shape
    return pl.pallas_call(
        attend_kernel,
        out_shape=jax.ShapeDtypeStruct((tokens, inner), BF16),
        in_specs=[pl.BlockSpec(memory_space=pltpu.VMEM)] * 6,
        out_specs=pl.BlockSpec(memory_space=pltpu.VMEM),
        compiler_params=pltpu.CompilerParams(vmem_limit_bytes=20 * 2**20),
        cost_estimate=pl.CostEstimate(flops=1_200_000_000, bytes_accessed=3_000_000, transcendentals=400_000),
        name="attend",
    )(q, kv, up, down, near, far)


def project_kernel(a_ref, gate_ref, *refs):
    pieces, (out_ref, w_ref, sems) = refs[:8], refs[8:]
    row, col = lax.axis_index("row"), lax.axis_index("col")
    core, place = lax.rem(col, 2), lax.div(col, 2)
    shard = 32
    copies = []
    for plane in range(2):
        owner_core = core if plane == 0 else 1 - core
        for step in range(4):
            owner_place = lax.rem(place + 4 - step, 4)
            for back in range(4):
                owner_row = lax.rem(row + 4 - back, 4)
                start = ((owner_row * 4 + owner_place) * 2 + owner_core) * shard
                copy = pltpu.make_async_copy(
                    pieces[plane * 4 + step].at[pl.ds(back * shard, shard), :],
                    w_ref.at[pl.ds(pl.multiple_of(start, shard), shard), :],
                    sems.at[(plane * 4 + step) * 4 + back],
                )
                copy.start()
                copies.append(copy)
    for copy in copies:
        copy.wait()
    width = 512
    for part in range(out_ref.shape[1] // width):
        lanes = slice(part * width, (part + 1) * width)
        total = jnp.dot(a_ref[...], w_ref[:, lanes], preferred_element_type=F32)
        out_ref[:, lanes] = (gate_ref[:, lanes] * total).astype(BF16)


def project(a, gate, pieces):
    tokens, inner = a.shape
    width = gate.shape[1]
    return pl.pallas_call(
        project_kernel,
        out_shape=jax.ShapeDtypeStruct((tokens, width), BF16),
        in_specs=[pl.BlockSpec(memory_space=pltpu.VMEM)] * 2 + [pl.BlockSpec(memory_space=pl.ANY)] * 8,
        out_specs=pl.BlockSpec(memory_space=pltpu.VMEM),
        scratch_shapes=[pltpu.VMEM((inner, width), BF16), pltpu.SemaphoreType.DMA((32,))],
        compiler_params=pltpu.CompilerParams(vmem_limit_bytes=24 * 2**20),
        cost_estimate=pl.CostEstimate(flops=810_000_000, bytes_accessed=6_000_000, transcendentals=0),
        name="project",
    )(a, gate, *pieces)


def two_rows(value):
    high = lax.reduce_precision(value, 8, 7)
    return jnp.stack([high, value - high]).astype(BF16)


def summed(rows):
    return rows[0].astype(F32) + rows[1].astype(F32)


def cond_shard(row_a, row_b, step, positions, half_width):
    mixed = lax.reduce_precision(0.5 * (row_a + row_b), 8, 7)
    freq_index = (positions % half_width).astype(F32)
    frequency = jnp.exp(-math.log(10000.0) * freq_index / half_width)
    angle = step * frequency
    embed = jnp.where(positions < half_width, jnp.cos(angle), jnp.sin(angle))
    return jax.nn.silu(mixed + embed).astype(BF16)


def body(distance, queries, keyvals, out_weight, gate_weight, class_table, label, step):
    dp_count, row_count, col_count = (lax.axis_size(a) for a in ("dp", "row", "col"))
    ahead = [(i, (i + distance) % dp_count) for i in range(dp_count)]
    behind = [(j, i) for i, j in ahead]
    model_width = gate_weight.shape[1]
    shard_width = gate_weight.shape[0]
    half_width = model_width // 2
    tile_rows, tile_cols, inner = queries.shape
    core = lax.axis_index("col") % 2

    peer_out = lax.ppermute(out_weight, "dp", ahead)

    positions = lax.axis_index(("row", "col")) * shard_width + jnp.arange(shard_width)
    own_row = lax.dynamic_index_in_dim(class_table, label, 0, keepdims=False).astype(F32)
    scalars = jnp.stack([label.astype(F32), step.astype(F32)])
    ask = jnp.concatenate([own_row, scalars, jnp.zeros((62,), F32)])[None]
    asked = lax.ppermute(ask, "dp", behind)[0]
    their_label = asked[shard_width].astype(jnp.int32)
    row_for_them = lax.dynamic_index_in_dim(class_table, their_label, 0, keepdims=False).astype(F32)
    their_cond = cond_shard(asked[:shard_width], row_for_them, asked[shard_width + 1], positions, half_width)
    their_part = jnp.dot(their_cond[None], gate_weight, preferred_element_type=F32)[0]
    answer = jnp.concatenate([their_part, row_for_them, jnp.zeros((64,), F32)]).reshape(17, 128)
    answered = lax.ppermute(answer, "dp", ahead).reshape(-1)
    peer_row = answered[model_width : model_width + shard_width]
    cond = cond_shard(own_row, peer_row, step.astype(F32), positions, half_width)
    own_part = jnp.dot(cond[None], gate_weight, preferred_element_type=F32)[0]
    gate_part = 0.5 * (own_part + answered[:model_width])

    up_pairs = [(i, i + 1) for i in range(row_count - 1)]
    down_pairs = [(j, i) for i, j in up_pairs]
    up = lax.ppermute(keyvals[:, tile_rows - RADIUS :], "row", up_pairs)
    down = lax.ppermute(keyvals[:, :RADIUS], "row", down_pairs)
    near_pairs = [(i, i ^ 1) for i in range(col_count)]
    far_pairs = [(i, i + 1) for i in range(1, col_count - 1, 2)]
    far_pairs = far_pairs + [(j, i) for i, j in far_pairs]

    def edge(lead):
        def cut(array):
            right, left = array[:, :, tile_cols - EDGE :], array[:, :, :EDGE]
            return jnp.where(lead, right, left)

        parts = [cut(up), cut(keyvals), cut(down)]
        parts.append(jnp.zeros((2, PAD_ROWS, EDGE, inner), BF16))
        return jnp.concatenate(parts, axis=1).reshape(2, -1, inner)

    near = lax.ppermute(edge(core == 0), "col", near_pairs)
    far = lax.ppermute(edge(core == 1), "col", far_pairs)
    attended = attend(
        queries.reshape(-1, inner),
        keyvals.reshape(2, -1, inner),
        up.reshape(2, -1, inner),
        down.reshape(2, -1, inner),
        near,
        far,
    )

    mixed = (0.5 * (out_weight.astype(F32) + peer_out.astype(F32))).astype(BF16)
    shard = mixed.shape[0]
    sent = jnp.concatenate([mixed, two_rows(gate_part), jnp.zeros((6, model_width), BF16)], axis=0)
    got = [sent] + [
        lax.ppermute(sent, "row", [(i, (i + k) % row_count) for i in range(row_count)])
        for k in range(1, row_count)
    ]
    gate_rows = sum(summed(part[shard : shard + 2]) for part in got)
    stack = jnp.concatenate(
        [part[:shard] for part in got] + [two_rows(gate_rows), jnp.zeros((6, model_width), BF16)],
        axis=0,
    )
    places = [stack] + [
        lax.ppermute(stack, "col", [(i, (i + 2 * k) % col_count) for i in range(col_count)])
        for k in range(1, col_count // 2)
    ]
    siblings = [lax.ppermute(part, "col", near_pairs) for part in places]
    pieces = places + siblings
    height = shard * row_count
    gate = sum(summed(part[height : height + 2]) for part in pieces)
    result = project(attended, gate[None], pieces)
    return result.reshape(1, tile_rows, tile_cols, model_width)


def local(queries, keyvals, out_weight, gate_weight, class_table, labels, timesteps, round_index):
    bit_count = lax.axis_size("dp").bit_length() - 1

    def branch(power):
        return lambda *args: body(2**power, *args)

    return lax.switch(
        round_index[0] % bit_count,
        [branch(power) for power in range(bit_count)],
        queries[0],
        keyvals[0],
        out_weight[0],
        gate_weight[0],
        class_table[0],
        labels[0],
        timesteps[0],
    )


def solution(mesh):
    placed = (
        P("dp", "row", "col", None),
        P("dp", None, "row", "col", None),
        P("dp", ("row", "col"), None),
        P("dp", ("row", "col"), None),
        P("dp", None, ("row", "col")),
        P("dp"),
        P("dp"),
        P(),
    )
    return jax.shard_map(
        local, mesh=mesh, in_specs=placed, out_specs=P("dp", "row", "col", None), check_vma=False
    )
```

time: 166 us -> 134 us (0.81)
  blocking collectives: 72.2 us -> 0 us
  starting transfers between devices: 21.4 us -> 77.7 us
  local copies, waits for them, and re-layouts: 29.4 us -> 10.3 us
  waiting for transfers between devices: 10.5 us -> 26.7 us
  between operations: 15.8 us -> 0.69 us
  matrix products: 13.6 us -> 1.03 us
  Pallas kernels: 0 us -> 8.76 us
  loops' own time: 0.03 us -> 4.59 us
    psum x1 -> x0, blocking collectives: 72.2 us -> none  [local(): gate = lax.psum(partial_gate, ('row', 'col'))]
    ppermute x5 -> x17, starting transfers between devices: 21.4 us -> 77.7 us  [the longest x4 19.1 us: body(): siblings = [lax.ppermute(part, 'col', near_pairs) for part in places]]
    ppermute x5 -> x17, waiting for transfers between devices: 10.5 us -> 26.7 us  [the longest x3 10 us: body(): lax.ppermute(sent, 'row', [(i, (i + k) % row_count) for i in range(row_co...]
    squeeze x2 -> x0, local copies, waits for them, and re-layouts: 14.3 us -> none  [the longest x1 7.17 us: local(): banded[0]]
    pallas_call x0 -> x2, Pallas kernels: none -> 8.76 us  [the longest x1 6.04 us: project(): pl.pallas_call(project_kernel, out_shape=jax.ShapeDtypeStruct((tokens, wi...]
    dot_general x3 -> x2, matrix products: 8 us -> 1.03 us  [the longest x1 0.82 us: body(): jnp.dot(their_cond[None], gate_weight, preferred_element_type=F32)[0]]
    slice x8 -> x7, local copies, waits for them, and re-layouts: 9.6 us -> 3.36 us  [the longest x1 1.78 us: body(): down = lax.ppermute(keyvals[:, :RADIUS], 'row', down_pairs)]
    sub x1 -> x0, matrix products: 5.56 us -> none  [local(): exponent = jnp.exp(scores - row_max)]
  transfers between devices with their start and end apart: 6 -> 17, of which waited for: 2 -> 5; matrix products, arithmetic and copies ran while one was open for 22% -> 7% of each run, Pallas kernels for 0% -> 2%
where the time goes in v1:
time: 134 us; the launch traced here: 133 us
  starting transfers between devices  77.7 us (58%)
  waiting for transfers between devices  26.7 us (20%)
  local copies, waits for them, and re-layouts  10.3 us (8%)
  Pallas kernels  8.76 us (7%)
  loops' own time  4.59 us (3%)
  other arithmetic  3.38 us (3%)
    ppermute x4, starting transfers between devices, body(): siblings = [lax.ppermute(part, 'col', near_pairs) for part in places]  19.1 us
    ppermute x1, starting transfers between devices, body(): peer_out = lax.ppermute(out_weight, 'dp', ahead)  16.4 us
    ppermute x3, waiting for transfers between devices, body(): lax.ppermute(sent, 'row', [(i, (i + k) % row_count) for i in range(row_co...  10 us
    ppermute x3, starting transfers between devices, body(): lax.ppermute(stack, 'col', [(i, (i + 2 * k) % col_count) for i in range(c...  9.63 us
    ppermute x3, starting transfers between devices, body(): lax.ppermute(sent, 'row', [(i, (i + k) % row_count) for i in range(row_co...  8.38 us
    ppermute x1, starting transfers between devices, body(): answered = lax.ppermute(answer, 'dp', ahead).reshape(-1)  8.05 us
    ppermute x1, waiting for transfers between devices, body(): answered = lax.ppermute(answer, 'dp', ahead).reshape(-1)  6.88 us
    ppermute x1, waiting for transfers between devices, body(): far = lax.ppermute(edge(core == 1), 'col', far_pairs)  6.68 us
  transfers between devices with their start and end apart: 17, of which 5 were waited for; matrix products, arithmetic and copies ran while one was open for 7% of the time, Pallas kernels for 2%

profile of v1, /device:TPU:1, one launch (start us, length us, event | category | flops | bytes accessed | tf_op | source)
XLA Modules:
  0.0 133.2 jit_solution(10324876713358953863)
XLA Ops:
  0.7 131.7 %conditional.1 = (bf16[1,12,16,2048]{3,2,1,0:T(8,128)(2,1)S(1)}) conditional(s32[]{:T(128)} %clamp.3, (bf16[1,12,16,1024]{3,2,1,0:T(8,128)(2,1)}, bf16[1,2,12,16,1024]{4,3,2,1,0:T(8,128)(2,1)}, bf16[1,2,12,16,1024]{4,3,2,1,0:T(8,128)(2,1)}, s32[1]{0:T(128)}, bf16[1,1000,64]{1,2,0:T(8,128)(2,1)}, ...), branch_computations={%region_0.1_spmd, %region_1.2_spmd, %region_2.3_spmd, %region_3.4_... | conditional | flops 2012913920 | bytes 47736540 | solution.py:242
  0.7 16.4 %collective-permute-start.23 = (bf16[32,2048]{1,0:T(8,128)(2,1)}, bf16[32,2048]{1,0:T(8,128)(2,1)S(1)}, u32[]{:S(2)}, u32[]{:S(2)}) collective-permute-start(bf16[32,2048]{1,0:T(8,128)(2,1)} %bitcast.253), channel_id=1, source_target_pairs={{0,64},{32,96},{64,128},{96,160},{128,192},{160,224},{192,256},{22... | collective-permute-start | bytes 393224 | tf_op jit(solution)/shard_map/cond/branch_1_fun/ppermute | solution.py:166
  19.7 1.1 copy.38
  21.5 0.1 maximum_bitcast_fusion.1
  21.6 4.1 %collective-permute-start.21 = (f32[1,128]{1,0:T(1,128)S(1)}, f32[1,128]{1,0:T(1,128)S(1)}, u32[]{:S(2)}, u32[]{:S(2)}) collective-permute-start(f32[1,128]{1,0:T(1,128)S(1)} %maximum_bitcast_fusion.1), channel_id=1, source_target_pairs={{64,0},{96,32},{128,64},{160,96},{192,128},{224,160},{256,192},{28... | collective-permute-start | bytes 1544 | tf_op jit(solution)/shard_map/cond/branch_1_fun/ppermute | solution.py:172
  25.7 1.8 %fusion.374 = (bf16[2,3,16,1024]{3,2,1,0:T(8,128)(2,1)S(1)}, bf16[2,3,16,1024]{3,2,1,0:T(8,128)(2,1)}) fusion(bf16[2,12,16,1024]{3,2,1,0:T(8,128)(2,1)} %bitcast.243), kind=kLoop, calls=%fused_computation.554 | loop fusion | bytes 786432 | tf_op jit(solution)/shard_map/cond/branch_1_fun/slice | solution.py:187
  27.5 1.3 collective-permute-start.18
  28.8 4.0 %collective-permute-start.17 = (bf16[2,3,16,1024]{3,2,1,0:T(8,128)(2,1)}, bf16[2,3,16,1024]{3,2,1,0:T(8,128)(2,1)S(1)}, u32[]{:S(2)}, u32[]{:S(2)}) collective-permute-start(bf16[2,3,16,1024]{3,2,1,0:T(8,128)(2,1)} %get-tuple-element.236), channel_id=1, source_target_pairs={{0,8},{8,16},{16,24},{1,9},{9,17},{17,25},{2,10},{10,18},{18,26},{... | collective-permute-start | bytes 589832 | tf_op jit(solution)/shard_map/cond/branch_1_fun/ppermute | solution.py:186
  32.8 1.8 %collective-permute-done.21 = f32[1,128]{1,0:T(1,128)S(1)} collective-permute-done((f32[1,128]{1,0:T(1,128)S(1)}, f32[1,128]{1,0:T(1,128)S(1)}, u32[]{:S(2)}, u32[]{:S(2)}) %collective-permute-start.21) | collective-permute-done | bytes 544 | tf_op jit(solution)/shard_map/cond/branch_1_fun/ppermute | solution.py:172
  34.6 0.6 fusion.375
  35.9 0.8 fusion.94
  36.7 0.1 concatenate.65
  36.8 8.1 %collective-permute-start.22 = (f32[17,128]{1,0:T(8,128)S(1)}, f32[17,128]{1,0:T(8,128)S(1)}, u32[]{:S(2)}, u32[]{:S(2)}) collective-permute-start(f32[17,128]{1,0:T(8,128)S(1)} %bitcast.273), channel_id=1, source_target_pairs={{0,64},{32,96},{64,128},{96,160},{128,192},{160,224},{192,256},{22... | collective-permute-start | bytes 26120 | tf_op jit(solution)/shard_map/cond/branch_1_fun/ppermute | solution.py:178
  44.9 0.2 broadcast_select_fusion.6
  45.1 0.1 pad.31.clone
  45.2 6.9 %collective-permute-done.22 = f32[17,128]{1,0:T(8,128)S(1)} collective-permute-done((f32[17,128]{1,0:T(8,128)S(1)}, f32[17,128]{1,0:T(8,128)S(1)}, u32[]{:S(2)}, u32[]{:S(2)}) %collective-permute-start.22) | collective-permute-done | bytes 8736 | tf_op jit(solution)/shard_map/cond/branch_1_fun/ppermute | solution.py:178
  52.1 0.2 fusion.92
  52.4 0.6 copy-done.17
  53.1 3.5 %collective-permute-start.26 = (bf16[40,2048]{1,0:T(8,128)(2,1)S(1)}, bf16[40,2048]{1,0:T(8,128)(2,1)S(1)}, u32[]{:S(2)}, u32[]{:S(2)}) collective-permute-start(bf16[40,2048]{1,0:T(8,128)(2,1)S(1)} %pad_maximum_fusion.1), channel_id=1, source_target_pairs={{0,24},{8,0},{16,8},{24,16},{1,25},{9,1},{17,9},{25,17},{2,26},{10... | collective-permute-start | bytes 491528 | tf_op jit(solution)/shard_map/cond/branch_1_fun/ppermute | solution.py:216
  56.6 2.2 %collective-permute-start.25 = (bf16[40,2048]{1,0:T(8,128)(2,1)S(1)}, bf16[40,2048]{1,0:T(8,128)(2,1)S(1)}, u32[]{:S(2)}, u32[]{:S(2)}) collective-permute-start(bf16[40,2048]{1,0:T(8,128)(2,1)S(1)} %pad_maximum_fusion.1), channel_id=1, source_target_pairs={{0,16},{8,24},{16,0},{24,8},{1,17},{9,25},{17,1},{25,9},{2,18},{10... | collective-permute-start | bytes 491528 | tf_op jit(solution)/shard_map/cond/branch_1_fun/ppermute | solution.py:216
  58.8 2.7 %collective-permute-start.24 = (bf16[40,2048]{1,0:T(8,128)(2,1)S(1)}, bf16[40,2048]{1,0:T(8,128)(2,1)S(1)}, u32[]{:S(2)}, u32[]{:S(2)}) collective-permute-start(bf16[40,2048]{1,0:T(8,128)(2,1)S(1)} %pad_maximum_fusion.1), channel_id=1, source_target_pairs={{0,8},{8,16},{16,24},{24,0},{1,9},{9,17},{17,25},{25,1},{2,10},{10... | collective-permute-start | bytes 491528 | tf_op jit(solution)/shard_map/cond/branch_1_fun/ppermute | solution.py:216
  61.5 0.7 broadcast_select_fusion.8
  62.2 10.0 %collective-permute-done.25 = bf16[40,2048]{1,0:T(8,128)(2,1)S(1)} collective-permute-done((bf16[40,2048]{1,0:T(8,128)(2,1)S(1)}, bf16[40,2048]{1,0:T(8,128)(2,1)S(1)}, u32[]{:S(2)}, u32[]{:S(2)}) %collective-permute-start.25) | collective-permute-done | bytes 163872 | tf_op jit(solution)/shard_map/cond/branch_1_fun/ppermute | solution.py:216
  72.2 0.1 fusion.96
  72.3 0.6 copy-done.26
  72.9 0.9 slice-done.1
  73.8 0.1 slice-done.5
  73.9 0.1 concatenate.67.refs_0_
  74.0 4.8 %collective-permute-start.29 = (bf16[136,2048]{1,0:T(8,128)(2,1)S(1)}, bf16[136,2048]{1,0:T(8,128)(2,1)S(1)}, u32[]{:S(2)}, u32[]{:S(2)}) collective-permute-start(bf16[136,2048]{1,0:T(8,128)(2,1)S(1)} %concatenate.67.refs_0_), channel_id=1, source_target_pairs={{0,6},{1,7},{2,0},{3,1},{4,2},{5,3},{6,4},{7,5},{8,14},{9,15},{10,... | collective-permute-start | bytes 1671176 | tf_op jit(solution)/shard_map/cond/branch_1_fun/ppermute | solution.py:225
  78.7 2.3 %collective-permute-start.28 = (bf16[136,2048]{1,0:T(8,128)(2,1)S(1)}, bf16[136,2048]{1,0:T(8,128)(2,1)S(1)}, u32[]{:S(2)}, u32[]{:S(2)}) collective-permute-start(bf16[136,2048]{1,0:T(8,128)(2,1)S(1)} %concatenate.67.refs_0_), channel_id=1, source_target_pairs={{0,4},{1,5},{2,6},{3,7},{4,0},{5,1},{6,2},{7,3},{8,12},{9,13},{10,... | collective-permute-start | bytes 1671176 | tf_op jit(solution)/shard_map/cond/branch_1_fun/ppermute | solution.py:225
  81.0 2.6 %collective-permute-start.27 = (bf16[136,2048]{1,0:T(8,128)(2,1)S(1)}, bf16[136,2048]{1,0:T(8,128)(2,1)S(1)}, u32[]{:S(2)}, u32[]{:S(2)}) collective-permute-start(bf16[136,2048]{1,0:T(8,128)(2,1)S(1)} %concatenate.67.refs_0_), channel_id=1, source_target_pairs={{0,2},{1,3},{2,4},{3,5},{4,6},{5,7},{6,0},{7,1},{8,10},{9,11},{10,... | collective-permute-start | bytes 1671176 | tf_op jit(solution)/shard_map/cond/branch_1_fun/ppermute | solution.py:225
  83.6 0.1 broadcast_select_fusion.9
  83.7 1.2 maximum_maximum_fusion.3
  84.9 0.8 reshape.442
  85.7 4.9 %collective-permute-start.19 = (bf16[2,80,1024]{2,1,0:T(8,128)(2,1)}, bf16[2,80,1024]{2,1,0:T(8,128)(2,1)}, u32[]{:S(2)}, u32[]{:S(2)}) collective-permute-start(bf16[2,80,1024]{2,1,0:T(8,128)(2,1)} %reshape.442), channel_id=1, source_target_pairs={{0,1},{1,0},{2,3},{3,2},{4,5},{5,4},{6,7},{7,6},{8,9},{9,8},{10,11... | collective-permute-start | bytes 983048 | tf_op jit(solution)/shard_map/cond/branch_1_fun/ppermute | solution.py:201
  90.6 1.9 %collective-permute-start.30 = (bf16[136,2048]{1,0:T(8,128)(2,1)S(1)}, bf16[136,2048]{1,0:T(8,128)(2,1)S(1)}, u32[]{:S(2)}, u32[]{:S(2)}) collective-permute-start(bf16[136,2048]{1,0:T(8,128)(2,1)S(1)} %concatenate.67.refs_0_), channel_id=1, source_target_pairs={{0,1},{1,0},{2,3},{3,2},{4,5},{5,4},{6,7},{7,6},{8,9},{9,8},{10,11... | collective-permute-start | bytes 1671176 | tf_op jit(solution)/shard_map/cond/branch_1_fun/ppermute | solution.py:228
  92.6 12.8 %collective-permute-start.33 = (bf16[136,2048]{1,0:T(8,128)(2,1)S(1)}, bf16[136,2048]{1,0:T(8,128)(2,1)S(1)}, u32[]{:S(2)}, u32[]{:S(2)}) collective-permute-start(bf16[136,2048]{1,0:T(8,128)(2,1)S(1)} %collective-permute-done.29.refs_3_), channel_id=1, source_target_pairs={{0,1},{1,0},{2,3},{3,2},{4,5},{5,4},{6,7},{7,6},{8,9},{9,8},{10,11... | collective-permute-start | bytes 1671176 | tf_op jit(solution)/shard_map/cond/branch_1_fun/ppermute | solution.py:228
  105.4 1.9 %collective-permute-start.32 = (bf16[136,2048]{1,0:T(8,128)(2,1)S(1)}, bf16[136,2048]{1,0:T(8,128)(2,1)}, u32[]{:S(2)}, u32[]{:S(2)}) collective-permute-start(bf16[136,2048]{1,0:T(8,128)(2,1)S(1)} %collective-permute-done.28.refs_2_), channel_id=1, source_target_pairs={{0,1},{1,0},{2,3},{3,2},{4,5},{5,4},{6,7},{7,6},{8,9},{9,8},{10,11... | collective-permute-start | bytes 1671176 | tf_op jit(solution)/shard_map/cond/branch_1_fun/ppermute | solution.py:228
  107.3 1.3 collective-permute-done.27.refs_1_
  108.6 2.4 %collective-permute-start.31 = (bf16[136,2048]{1,0:T(8,128)(2,1)S(1)}, bf16[136,2048]{1,0:T(8,128)(2,1)}, u32[]{:S(2)}, u32[]{:S(2)}) collective-permute-start(bf16[136,2048]{1,0:T(8,128)(2,1)S(1)} %collective-permute-done.27.refs_1_), channel_id=1, source_target_pairs={{0,1},{1,0},{2,3},{3,2},{4,5},{5,4},{6,7},{7,6},{8,9},{9,8},{10,11... | collective-permute-start | bytes 1671176 | tf_op jit(solution)/shard_map/cond/branch_1_fun/ppermute | solution.py:228
  111.0 1.8 %reshape.443 = bf16[2,80,1024]{2,1,0:T(8,128)(2,1)} reshape(bf16[2,20,4,1024]{3,2,1,0:T(4,128)(2,1)} %get-tuple-element.245) | data formatting | bytes 655360 | tf_op jit(solution)/shard_map/cond/branch_1_fun/reshape | solution.py:199
  112.8 1.9 %collective-permute-start.20 = (bf16[2,80,1024]{2,1,0:T(8,128)(2,1)}, bf16[2,80,1024]{2,1,0:T(8,128)(2,1)S(1)}, u32[]{:S(2)}, u32[]{:S(2)}) collective-permute-start(bf16[2,80,1024]{2,1,0:T(8,128)(2,1)} %reshape.443), channel_id=1, source_target_pairs={{1,2},{3,4},{5,6},{2,1},{4,3},{6,5},{9,10},{11,12},{13,14},{10,9},... | collective-permute-start | bytes 983048 | tf_op jit(solution)/shard_map/cond/branch_1_fun/ppermute | solution.py:202
  114.7 6.7 %collective-permute-done.20.far_ref = bf16[2,80,1024]{2,1,0:T(8,128)(2,1)S(1)} collective-permute-done((bf16[2,80,1024]{2,1,0:T(8,128)(2,1)}, bf16[2,80,1024]{2,1,0:T(8,128)(2,1)S(1)}, u32[]{:S(2)}, u32[]{:S(2)}) %collective-permute-start.20) | collective-permute-done | bytes 327712 | tf_op jit(solution)/shard_map/cond/branch_1_fun/ppermute | solution.py:202
  121.4 0.9 copy-done.3
  122.3 2.7 %attend.5.a_ref = bf16[192,1024]{1,0:T(8,128)(2,1)S(1)} custom-call(bf16[192,1024]{1,0:T(8,128)(2,1)} %bitcast.277, bf16[2,192,1024]{2,1,0:T(8,128)(2,1)} %bitcast.244, bf16[2,48,1024]{2,1,0:T(8,128)(2,1)S(1)} %bitcast.237, bf16[2,48,1024]{2,1,0:T(8,128)(2,1)S(1)} %bitcast.233, bf16[2,80,1024]{2,1,0:T(8,128)(2,1)} %collective-permute-done.19.near_ref, ...), custom_call_target="tpu_custom_call" | custom-call | flops 1200000000 | bytes 3000000 | tf_op jit(solution)/shard_map/cond/branch_1_fun/attend/pallas_call | solution.py:83
  125.1 1.0 fusion.99.gate_ref
  126.0 6.0 %project.5 = bf16[192,2048]{1,0:T(8,128)(2,1)S(1)} custom-call(bf16[192,1024]{1,0:T(8,128)(2,1)S(1)} %attend.5.a_ref, f32[1,2048]{1,0:T(1,128)S(1)} %fusion.99.gate_ref, bf16[136,2048]{1,0:T(8,128)(2,1)S(1)} %concatenate.67.refs_0_, bf16[136,2048]{1,0:T(8,128)(2,1)S(1)} %collective-permute-done.27.refs_1_, ...), custom_call_target="tpu_custom_call" | custom-call | flops 810000000 | bytes 6000000 | tf_op jit(solution)/shard_map/cond/branch_1_fun/project/pallas_call | solution.py:126
  132.4 0.9 copy-done.20
  (43 shorter events, 0.2 us)
Async XLA Ops:
  0.7 44.2 %copy-start.13 = (bf16[1,2,12,16,1024]{4,3,2,1,0:T(8,128)(2,1)S(1)}, bf16[1,2,12,16,1024]{4,3,2,1,0:T(8,128)(2,1)}, u32[]{:S(2)}) copy-start(bf16[1,2,12,16,1024]{4,3,2,1,0:T(8,128)(2,1)} %get-tuple-element.112) | copy-start | bytes 2359300 | tf_op jit(solution)/shard_map/cond
  0.7 51.6 %collective-permute-start.23 = (bf16[32,2048]{1,0:T(8,128)(2,1)}, bf16[32,2048]{1,0:T(8,128)(2,1)S(1)}, u32[]{:S(2)}, u32[]{:S(2)}) collective-permute-start(bf16[32,2048]{1,0:T(8,128)(2,1)} %bitcast.253), channel_id=1, source_target_pairs={{0,64},{32,96},{64,128},{96,160},{128,192},{160,224},{192,256},{22... | collective-permute-start | bytes 393224 | tf_op jit(solution)/shard_map/cond/branch_1_fun/ppermute | solution.py:166
  21.6 13.1 %collective-permute-start.21 = (f32[1,128]{1,0:T(1,128)S(1)}, f32[1,128]{1,0:T(1,128)S(1)}, u32[]{:S(2)}, u32[]{:S(2)}) collective-permute-start(f32[1,128]{1,0:T(1,128)S(1)} %maximum_bitcast_fusion.1), channel_id=1, source_target_pairs={{64,0},{96,32},{128,64},{160,96},{192,128},{224,160},{256,192},{28... | collective-permute-start | bytes 1544 | tf_op jit(solution)/shard_map/cond/branch_1_fun/ppermute | solution.py:172
  25.7 10.2 %copy-start.9 = (bf16[1,64,2048]{2,1,0:T(8,128)(2,1)S(1)}, bf16[1,64,2048]{2,1,0:T(8,128)(2,1)}, u32[]{:S(2)}) copy-start(bf16[1,64,2048]{2,1,0:T(8,128)(2,1)} %get-tuple-element.172) | copy-start | bytes 786436 | tf_op jit(solution)/shard_map/cond
  27.5 34.0 %collective-permute-start.18 = (bf16[2,3,16,1024]{3,2,1,0:T(8,128)(2,1)S(1)}, bf16[2,3,16,1024]{3,2,1,0:T(8,128)(2,1)S(1)}, u32[]{:S(2)}, u32[]{:S(2)}) collective-permute-start(bf16[2,3,16,1024]{3,2,1,0:T(8,128)(2,1)S(1)} %get-tuple-element.235), channel_id=1, source_target_pairs={{8,0},{16,8},{24,16},{9,1},{17,9},{25,17},{10,2},{18,10},{26,18},{... | collective-permute-start | bytes 589832 | tf_op jit(solution)/shard_map/cond/branch_1_fun/ppermute | solution.py:187
  28.8 54.8 %collective-permute-start.17 = (bf16[2,3,16,1024]{3,2,1,0:T(8,128)(2,1)}, bf16[2,3,16,1024]{3,2,1,0:T(8,128)(2,1)S(1)}, u32[]{:S(2)}, u32[]{:S(2)}) collective-permute-start(bf16[2,3,16,1024]{3,2,1,0:T(8,128)(2,1)} %get-tuple-element.236), channel_id=1, source_target_pairs={{0,8},{8,16},{16,24},{1,9},{9,17},{17,25},{2,10},{10,18},{18,26},{... | collective-permute-start | bytes 589832 | tf_op jit(solution)/shard_map/cond/branch_1_fun/ppermute | solution.py:186
  36.8 15.3 %collective-permute-start.22 = (f32[17,128]{1,0:T(8,128)S(1)}, f32[17,128]{1,0:T(8,128)S(1)}, u32[]{:S(2)}, u32[]{:S(2)}) collective-permute-start(f32[17,128]{1,0:T(8,128)S(1)} %bitcast.273), channel_id=1, source_target_pairs={{0,64},{32,96},{64,128},{96,160},{128,192},{160,224},{192,256},{22... | collective-permute-start | bytes 26120 | tf_op jit(solution)/shard_map/cond/branch_1_fun/ppermute | solution.py:178
  52.1 0.9 copy-start.17
  53.1 9.1 %collective-permute-start.26 = (bf16[40,2048]{1,0:T(8,128)(2,1)S(1)}, bf16[40,2048]{1,0:T(8,128)(2,1)S(1)}, u32[]{:S(2)}, u32[]{:S(2)}) collective-permute-start(bf16[40,2048]{1,0:T(8,128)(2,1)S(1)} %pad_maximum_fusion.1), channel_id=1, source_target_pairs={{0,24},{8,0},{16,8},{24,16},{1,25},{9,1},{17,9},{25,17},{2,26},{10... | collective-permute-start | bytes 491528 | tf_op jit(solution)/shard_map/cond/branch_1_fun/ppermute | solution.py:216
  56.6 15.6 %collective-permute-start.25 = (bf16[40,2048]{1,0:T(8,128)(2,1)S(1)}, bf16[40,2048]{1,0:T(8,128)(2,1)S(1)}, u32[]{:S(2)}, u32[]{:S(2)}) collective-permute-start(bf16[40,2048]{1,0:T(8,128)(2,1)S(1)} %pad_maximum_fusion.1), channel_id=1, source_target_pairs={{0,16},{8,24},{16,0},{24,8},{1,17},{9,25},{17,1},{25,9},{2,18},{10... | collective-permute-start | bytes 491528 | tf_op jit(solution)/shard_map/cond/branch_1_fun/ppermute | solution.py:216
  58.8 13.5 %collective-permute-start.24 = (bf16[40,2048]{1,0:T(8,128)(2,1)S(1)}, bf16[40,2048]{1,0:T(8,128)(2,1)S(1)}, u32[]{:S(2)}, u32[]{:S(2)}) collective-permute-start(bf16[40,2048]{1,0:T(8,128)(2,1)S(1)} %pad_maximum_fusion.1), channel_id=1, source_target_pairs={{0,8},{8,16},{16,24},{24,0},{1,9},{9,17},{17,25},{25,1},{2,10},{10... | collective-permute-start | bytes 491528 | tf_op jit(solution)/shard_map/cond/branch_1_fun/ppermute | solution.py:216
  62.2 10.1 %copy-start.22 = (bf16[40,2048]{1,0:T(8,128)(2,1)}, bf16[40,2048]{1,0:T(8,128)(2,1)S(1)}, u32[]{:S(2)}) copy-start(bf16[40,2048]{1,0:T(8,128)(2,1)S(1)} %collective-permute-done.26) | copy-start | bytes 491524 | tf_op jit(solution)/shard_map/cond
  72.2 0.7 copy-start.26
  72.9 0.9 slice-start.1
  72.9 1.0 slice-start.5
  73.9 9.8 %copy-start.31 = (bf16[2,3,4,1024]{3,2,1,0:T(4,128)(2,1)S(1)}, bf16[2,3,4,1024]{3,2,1,0:T(4,128)(2,1)}, u32[]{:S(2)}) copy-start(bf16[2,3,4,1024]{3,2,1,0:T(4,128)(2,1)} %get-tuple-element.239) | copy-start | bytes 147460 | tf_op jit(solution)/shard_map/cond
  74.0 9.8 %copy-start.32 = (bf16[2,3,4,1024]{3,2,1,0:T(4,128)(2,1)S(1)}, bf16[2,3,4,1024]{3,2,1,0:T(4,128)(2,1)}, u32[]{:S(2)}) copy-start(bf16[2,3,4,1024]{3,2,1,0:T(4,128)(2,1)} %get-tuple-element.240) | copy-start | bytes 147460 | tf_op jit(solution)/shard_map/cond
  74.0 18.6 %collective-permute-start.29 = (bf16[136,2048]{1,0:T(8,128)(2,1)S(1)}, bf16[136,2048]{1,0:T(8,128)(2,1)S(1)}, u32[]{:S(2)}, u32[]{:S(2)}) collective-permute-start(bf16[136,2048]{1,0:T(8,128)(2,1)S(1)} %concatenate.67.refs_0_), channel_id=1, source_target_pairs={{0,6},{1,7},{2,0},{3,1},{4,2},{5,3},{6,4},{7,5},{8,14},{9,15},{10,... | collective-permute-start | bytes 1671176 | tf_op jit(solution)/shard_map/cond/branch_1_fun/ppermute | solution.py:225
  78.7 26.7 %collective-permute-start.28 = (bf16[136,2048]{1,0:T(8,128)(2,1)S(1)}, bf16[136,2048]{1,0:T(8,128)(2,1)S(1)}, u32[]{:S(2)}, u32[]{:S(2)}) collective-permute-start(bf16[136,2048]{1,0:T(8,128)(2,1)S(1)} %concatenate.67.refs_0_), channel_id=1, source_target_pairs={{0,4},{1,5},{2,6},{3,7},{4,0},{5,1},{6,2},{7,3},{8,12},{9,13},{10,... | collective-permute-start | bytes 1671176 | tf_op jit(solution)/shard_map/cond/branch_1_fun/ppermute | solution.py:225
  81.0 27.6 %collective-permute-start.27 = (bf16[136,2048]{1,0:T(8,128)(2,1)S(1)}, bf16[136,2048]{1,0:T(8,128)(2,1)S(1)}, u32[]{:S(2)}, u32[]{:S(2)}) collective-permute-start(bf16[136,2048]{1,0:T(8,128)(2,1)S(1)} %concatenate.67.refs_0_), channel_id=1, source_target_pairs={{0,2},{1,3},{2,4},{3,5},{4,6},{5,7},{6,0},{7,1},{8,10},{9,11},{10,... | collective-permute-start | bytes 1671176 | tf_op jit(solution)/shard_map/cond/branch_1_fun/ppermute | solution.py:225
  83.6 1.3 copy-start.2
  85.7 27.1 %collective-permute-start.19 = (bf16[2,80,1024]{2,1,0:T(8,128)(2,1)}, bf16[2,80,1024]{2,1,0:T(8,128)(2,1)}, u32[]{:S(2)}, u32[]{:S(2)}) collective-permute-start(bf16[2,80,1024]{2,1,0:T(8,128)(2,1)} %reshape.442), channel_id=1, source_target_pairs={{0,1},{1,0},{2,3},{3,2},{4,5},{5,4},{6,7},{7,6},{8,9},{9,8},{10,11... | collective-permute-start | bytes 983048 | tf_op jit(solution)/shard_map/cond/branch_1_fun/ppermute | solution.py:201
  90.6 34.4 %collective-permute-start.30 = (bf16[136,2048]{1,0:T(8,128)(2,1)S(1)}, bf16[136,2048]{1,0:T(8,128)(2,1)S(1)}, u32[]{:S(2)}, u32[]{:S(2)}) collective-permute-start(bf16[136,2048]{1,0:T(8,128)(2,1)S(1)} %concatenate.67.refs_0_), channel_id=1, source_target_pairs={{0,1},{1,0},{2,3},{3,2},{4,5},{5,4},{6,7},{7,6},{8,9},{9,8},{10,11... | collective-permute-start | bytes 1671176 | tf_op jit(solution)/shard_map/cond/branch_1_fun/ppermute | solution.py:228
  92.6 32.5 %collective-permute-start.33 = (bf16[136,2048]{1,0:T(8,128)(2,1)S(1)}, bf16[136,2048]{1,0:T(8,128)(2,1)S(1)}, u32[]{:S(2)}, u32[]{:S(2)}) collective-permute-start(bf16[136,2048]{1,0:T(8,128)(2,1)S(1)} %collective-permute-done.29.refs_3_), channel_id=1, source_target_pairs={{0,1},{1,0},{2,3},{3,2},{4,5},{5,4},{6,7},{7,6},{8,9},{9,8},{10,11... | collective-permute-start | bytes 1671176 | tf_op jit(solution)/shard_map/cond/branch_1_fun/ppermute | solution.py:228
  105.4 19.7 %collective-permute-start.32 = (bf16[136,2048]{1,0:T(8,128)(2,1)S(1)}, bf16[136,2048]{1,0:T(8,128)(2,1)}, u32[]{:S(2)}, u32[]{:S(2)}) collective-permute-start(bf16[136,2048]{1,0:T(8,128)(2,1)S(1)} %collective-permute-done.28.refs_2_), channel_id=1, source_target_pairs={{0,1},{1,0},{2,3},{3,2},{4,5},{5,4},{6,7},{7,6},{8,9},{9,8},{10,11... | collective-permute-start | bytes 1671176 | tf_op jit(solution)/shard_map/cond/branch_1_fun/ppermute | solution.py:228
  108.6 16.4 %collective-permute-start.31 = (bf16[136,2048]{1,0:T(8,128)(2,1)S(1)}, bf16[136,2048]{1,0:T(8,128)(2,1)}, u32[]{:S(2)}, u32[]{:S(2)}) collective-permute-start(bf16[136,2048]{1,0:T(8,128)(2,1)S(1)} %collective-permute-done.27.refs_1_), channel_id=1, source_target_pairs={{0,1},{1,0},{2,3},{3,2},{4,5},{5,4},{6,7},{7,6},{8,9},{9,8},{10,11... | collective-permute-start | bytes 1671176 | tf_op jit(solution)/shard_map/cond/branch_1_fun/ppermute | solution.py:228
  112.8 8.6 %collective-permute-start.20 = (bf16[2,80,1024]{2,1,0:T(8,128)(2,1)}, bf16[2,80,1024]{2,1,0:T(8,128)(2,1)S(1)}, u32[]{:S(2)}, u32[]{:S(2)}) collective-permute-start(bf16[2,80,1024]{2,1,0:T(8,128)(2,1)} %reshape.443), channel_id=1, source_target_pairs={{1,2},{3,4},{5,6},{2,1},{4,3},{6,5},{9,10},{11,12},{13,14},{10,9},... | collective-permute-start | bytes 983048 | tf_op jit(solution)/shard_map/cond/branch_1_fun/ppermute | solution.py:202
  121.4 0.9 copy-start.3
  132.4 0.9 copy-start.20

commit v2 on v1

v2 whole, which is shorter than its diff:
```python
import math

import jax
import jax.numpy as jnp
from jax import lax
from jax.experimental import pallas as pl
from jax.experimental.pallas import tpu as pltpu
from jax.sharding import PartitionSpec as P

HDIM = 128
RADIUS = 3
F32 = jnp.float32
BF16 = jnp.bfloat16
GROUP = 4
EDGE = 4
PAD_ROWS = 2


def attend_kernel(q_ref, kv_ref, up_ref, down_ref, near_ref, far_ref, out_ref):
    rows, cols = 12, 16
    inner = q_ref.shape[1]
    row0 = lax.axis_index("row") * rows
    col_index = lax.axis_index("col")
    col0 = col_index * cols
    core = lax.rem(col_index, 2)
    near_base = jnp.where(core == 0, cols, -EDGE)
    far_base = jnp.where(core == 0, -EDGE, cols)
    queries = GROUP * cols
    band = (GROUP + 2 * RADIUS) * cols
    side = (GROUP + 2 * RADIUS + PAD_ROWS) * EDGE
    keys = band + 2 * side
    halo = RADIUS * cols
    factor = math.log2(math.e) / math.sqrt(HDIM)
    q_id = lax.broadcasted_iota(jnp.int32, (queries, keys), 0)
    k_id = lax.broadcasted_iota(jnp.int32, (queries, keys), 1)
    q_row, q_col = q_id // cols, q_id % cols
    side_id = jnp.where(k_id < band + side, k_id - band, k_id - band - side)
    k_row = jnp.where(k_id < band, k_id // cols, side_id // EDGE)
    base = jnp.where(k_id < band + side, near_base, far_base)
    k_col = jnp.where(k_id < band, k_id % cols, base + side_id % EDGE)
    d_row, d_col = k_row - q_row, k_col - q_col
    reach = (d_row >= 0) & (d_row <= 2 * RADIUS) & (d_col >= -RADIUS) & (d_col <= RADIUS)
    k_gcol = col0 + k_col
    reach = reach & (k_gcol >= 0) & (k_gcol < cols * lax.axis_size("col"))
    ones = jnp.ones((keys, HDIM), BF16)
    for group in range(rows // GROUP):
        k_grow = row0 + GROUP * group - RADIUS + k_row
        allowed = reach & (k_grow >= 0) & (k_grow < rows * lax.axis_size("row"))
        bias = jnp.where(allowed, F32(0.0), F32(-1e30))
        first = (GROUP * group - RADIUS) * cols
        last = first + band
        for head in range(inner // HDIM):
            lanes = slice(head * HDIM, (head + 1) * HDIM)

            def gathered(which):
                parts = []
                if first < 0:
                    parts.append(up_ref[which, halo + first : halo, lanes])
                parts.append(kv_ref[which, max(first, 0) : min(last, rows * cols), lanes])
                if last > rows * cols:
                    parts.append(down_ref[which, 0 : last - rows * cols, lanes])
                span = slice(GROUP * group * EDGE, GROUP * group * EDGE + side)
                parts.append(near_ref[which, span, lanes])
                parts.append(far_ref[which, span, lanes])
                return jnp.concatenate(parts, axis=0)

            q = q_ref[group * queries : (group + 1) * queries, lanes]
            scores = lax.dot_general(
                q, gathered(0), (((1,), (1,)), ((), ())), preferred_element_type=F32
            )
            scores = scores + bias
            top = jnp.max(scores, axis=-1, keepdims=True)
            weight = jnp.exp2((scores - top) * factor).astype(BF16)
            values = jnp.concatenate([gathered(1), ones], axis=1)
            both = jnp.dot(weight, values, preferred_element_type=F32)
            out_ref[group * queries : (group + 1) * queries, lanes] = (
                both[:, :HDIM] / both[:, HDIM:]
            ).astype(BF16)


def attend(q, kv, up, down, near, far):
    tokens, inner = q.shape
    return pl.pallas_call(
        attend_kernel,
        out_shape=jax.ShapeDtypeStruct((tokens, inner), BF16),
        in_specs=[pl.BlockSpec(memory_space=pltpu.VMEM)] * 6,
        out_specs=pl.BlockSpec(memory_space=pltpu.VMEM),
        compiler_params=pltpu.CompilerParams(vmem_limit_bytes=20 * 2**20),
        cost_estimate=pl.CostEstimate(flops=1_200_000_000, bytes_accessed=3_000_000, transcendentals=400_000),
        name="attend",
    )(q, kv, up, down, near, far)


def in_vmem(count):
    return [pl.BlockSpec(memory_space=pltpu.VMEM)] * count


def picked_row(label, table):
    ids = lax.broadcasted_iota(jnp.int32, (16, table.shape[0]), 1).astype(F32)
    one_hot = jnp.where(ids == label, F32(1.0), F32(0.0)).astype(BF16)
    return jnp.dot(one_hot, table, preferred_element_type=F32)


def gate_product(row_a, row_b, embed, gate_weight):
    value = (0.5 * (row_a + row_b)).astype(BF16).astype(F32) + embed
    cond = (value / (1.0 + jnp.exp(-value))).astype(BF16)
    return jnp.dot(cond, gate_weight, preferred_element_type=F32)


def begin_kernel(label_ref, embed_ref, table_ref, kv_ref, ask_ref, low_ref, high_ref, sems):
    tokens, halo = kv_ref.shape[1], low_ref.shape[1]
    lower = pltpu.make_async_copy(kv_ref.at[:, pl.ds(tokens - halo, halo), :], low_ref, sems.at[0])
    upper = pltpu.make_async_copy(kv_ref.at[:, pl.ds(0, halo), :], high_ref, sems.at[1])
    lower.start()
    upper.start()
    label = jnp.full((1, 1), label_ref[0], jnp.int32).astype(F32)
    row = picked_row(label, table_ref[...])[:1]
    ask_ref[:, 0:128] = jnp.concatenate([row, embed_ref[...]], axis=1)
    ask_ref[:, 128:256] = jnp.broadcast_to(label, (1, 128))
    lower.wait()
    upper.wait()


def begin(label, embed, table, kv):
    inner = kv.shape[2]
    halo = RADIUS * 16
    edge = jax.ShapeDtypeStruct((2, halo, inner), BF16)
    return pl.pallas_call(
        begin_kernel,
        out_shape=(jax.ShapeDtypeStruct((1, 256), F32), edge, edge),
        in_specs=[pl.BlockSpec(memory_space=pltpu.SMEM)] + in_vmem(2) + [pl.BlockSpec(memory_space=pl.ANY)],
        out_specs=tuple(in_vmem(3)),
        scratch_shapes=[pltpu.SemaphoreType.DMA((2,))],
        compiler_params=pltpu.CompilerParams(vmem_limit_bytes=8 * 2**20),
        name="begin",
    )(label, embed, table, kv)


def answer_kernel(asked_ref, table_ref, gate_ref, answer_ref):
    width = gate_ref.shape[1]
    row = picked_row(asked_ref[:, 128:129], table_ref[...])
    part = gate_product(row, asked_ref[:, 0:64], asked_ref[:, 64:128], gate_ref[...])
    answer_ref[:, 0:width] = part[:1]
    answer_ref[:, width:] = jnp.concatenate([row[:1], row[:1]], axis=1)


def answer(asked, table, gate_weight):
    return pl.pallas_call(
        answer_kernel,
        out_shape=jax.ShapeDtypeStruct((1, gate_weight.shape[1] + 128), F32),
        in_specs=in_vmem(3),
        out_specs=pl.BlockSpec(memory_space=pltpu.VMEM),
        compiler_params=pltpu.CompilerParams(vmem_limit_bytes=8 * 2**20),
        name="answer",
    )(asked, table, gate_weight)


def two_rows(value):
    high = value.astype(BF16).astype(F32)
    ids = lax.broadcasted_iota(jnp.int32, (8, value.shape[1]), 0)
    return jnp.where(ids == 0, high, jnp.where(ids == 1, value - high, F32(0.0))).astype(BF16)


def mix_kernel(own_ref, peer_ref, ask_ref, answered_ref, gate_ref, sent_ref):
    shard, width = own_ref.shape
    sent_ref[0:shard, :] = (0.5 * (own_ref[...].astype(F32) + peer_ref[...].astype(F32))).astype(BF16)
    own_row = jnp.broadcast_to(ask_ref[:, 0:64], (16, 64))
    part = gate_product(own_row, answered_ref[:, width : width + 64], ask_ref[:, 64:128], gate_ref[...])
    sent_ref[shard : shard + 8, :] = two_rows(0.5 * (part[:1] + answered_ref[:, 0:width]))


def mix(own, peer, ask, answered, gate_weight):
    shard, width = own.shape
    return pl.pallas_call(
        mix_kernel,
        out_shape=jax.ShapeDtypeStruct((shard + 8, width), BF16),
        in_specs=in_vmem(5),
        out_specs=pl.BlockSpec(memory_space=pltpu.VMEM),
        compiler_params=pltpu.CompilerParams(vmem_limit_bytes=8 * 2**20),
        name="mix",
    )(own, peer, ask, answered, gate_weight)


def stack_kernel(*refs):
    parts, out_ref = refs[:4], refs[4]
    shard = parts[0].shape[0] - 8
    total = jnp.zeros((8, out_ref.shape[1]), F32)
    for index, part in enumerate(parts):
        out_ref[index * shard : (index + 1) * shard, :] = part[0:shard, :]
        total = total + part[shard : shard + 8, :].astype(F32)
    out_ref[4 * shard : 4 * shard + 8, :] = two_rows(jnp.sum(total, axis=0, keepdims=True))


def stacked(parts):
    rows, width = parts[0].shape
    return pl.pallas_call(
        stack_kernel,
        out_shape=jax.ShapeDtypeStruct((4 * (rows - 8) + 8, width), BF16),
        in_specs=in_vmem(4),
        out_specs=pl.BlockSpec(memory_space=pltpu.VMEM),
        compiler_params=pltpu.CompilerParams(vmem_limit_bytes=8 * 2**20),
        name="stack",
    )(*parts)


def edges_kernel(kv_ref, up_ref, down_ref, near_ref, far_ref):
    cols = 16
    core = lax.rem(lax.axis_index("col"), 2)
    count = near_ref.shape[1]
    source = up_ref.shape[1] + kv_ref.shape[1] + down_ref.shape[1]
    out_id = lax.broadcasted_iota(jnp.int32, (count, source), 0)
    in_id = lax.broadcasted_iota(jnp.int32, (count, source), 1)
    right = (out_id // EDGE) * cols + cols - EDGE + out_id % EDGE
    left = (out_id // EDGE) * cols + out_id % EDGE
    right = jnp.where(in_id == right, F32(1.0), F32(0.0))
    left = jnp.where(in_id == left, F32(1.0), F32(0.0))
    first = core == 0
    pick_near = jnp.where(first, right, left).astype(BF16)
    pick_far = jnp.where(first, left, right).astype(BF16)
    for which in range(2):
        tall = jnp.concatenate([up_ref[which], kv_ref[which], down_ref[which]], axis=0)
        near_ref[which] = jnp.dot(pick_near, tall, preferred_element_type=F32).astype(BF16)
        far_ref[which] = jnp.dot(pick_far, tall, preferred_element_type=F32).astype(BF16)


def edges(kv, up, down):
    inner = kv.shape[2]
    count = (12 + 2 * RADIUS + PAD_ROWS) * EDGE
    edge = jax.ShapeDtypeStruct((2, count, inner), BF16)
    return pl.pallas_call(
        edges_kernel,
        out_shape=(edge, edge),
        in_specs=in_vmem(3),
        out_specs=tuple(in_vmem(2)),
        compiler_params=pltpu.CompilerParams(vmem_limit_bytes=12 * 2**20),
        name="edges",
    )(kv, up, down)


def project_kernel(a_ref, *refs):
    pieces, (out_ref, lanes_ref, held_ref, sems) = refs[:8], refs[8:]
    row, col = lax.axis_index("row"), lax.axis_index("col")
    core, place = lax.rem(col, 2), lax.div(col, 2)
    shard, block = 32, 256
    tokens, width = a_ref.shape[0], out_ref.shape[1]
    for back in range(4):
        start = pl.multiple_of(lax.rem(row + 4 - back, 4) * block, block)
        lanes = a_ref[:, pl.ds(start, block)].astype(F32)
        lanes = pltpu.roll(lanes, block - 64 * place, 1).astype(BF16)
        for step in range(4):
            at = ((4 - step) % 4) * 64
            lanes_ref[:, step * block + back * 64 : step * block + (back + 1) * 64] = lanes[:, at : at + 64]
    total = jnp.zeros((8, width), F32)
    for piece in pieces:
        total = total + piece[4 * shard : 4 * shard + 8, :].astype(F32)
    gate = jnp.sum(total, axis=0, keepdims=True)
    part_width = 512
    parts = width // part_width

    def multiply(even, odd):
        for part in range(parts):
            at = slice(part * part_width, (part + 1) * part_width)
            rows = []
            for step in range(4):
                for back in range(4):
                    span = slice(back * shard, (back + 1) * shard)
                    rows += [even[step][span, at], odd[step][span, at]]
            product = jnp.dot(lanes_ref[...], jnp.concatenate(rows, axis=0), preferred_element_type=F32)
            held_ref[:, at] = (gate[:, at] * product).astype(BF16)
            copy_out(part).start()

    def copy_out(part):
        at = pl.ds(part * part_width, part_width)
        return pltpu.make_async_copy(held_ref.at[:, at], out_ref.at[:, at], sems.at[part])

    @pl.when(core == 0)
    def _():
        multiply(pieces[:4], pieces[4:])

    @pl.when(core == 1)
    def _():
        multiply(pieces[4:], pieces[:4])

    for part in range(parts):
        copy_out(part).wait()


def project(a, pieces):
    tokens, inner = a.shape
    width = pieces[0].shape[1]
    return pl.pallas_call(
        project_kernel,
        out_shape=jax.ShapeDtypeStruct((tokens, width), BF16),
        in_specs=in_vmem(9),
        out_specs=pl.BlockSpec(memory_space=pltpu.HBM),
        scratch_shapes=[
            pltpu.VMEM((tokens, inner), BF16),
            pltpu.VMEM((tokens, width), BF16),
            pltpu.SemaphoreType.DMA((4,)),
        ],
        compiler_params=pltpu.CompilerParams(vmem_limit_bytes=24 * 2**20),
        cost_estimate=pl.CostEstimate(flops=810_000_000, bytes_accessed=6_000_000, transcendentals=0),
        name="project",
    )(a, *pieces)


def time_embed(step, shard_width, model_width):
    half_width = model_width // 2
    positions = lax.axis_index(("row", "col")) * shard_width + jnp.arange(shard_width)
    freq_index = (positions % half_width).astype(F32)
    frequency = jnp.exp(-math.log(10000.0) * freq_index / half_width)
    angle = step.astype(F32) * frequency
    return jnp.where(positions < half_width, jnp.cos(angle), jnp.sin(angle))[None]


def body(distance, queries, keyvals, out_weight, gate_weight, class_table, label, step):
    dp_count, row_count, col_count = (lax.axis_size(a) for a in ("dp", "row", "col"))
    ahead = [(i, (i + distance) % dp_count) for i in range(dp_count)]
    behind = [(j, i) for i, j in ahead]
    tile_rows, tile_cols, inner = queries.shape
    kv = keyvals.reshape(2, -1, inner)

    embed = time_embed(step[0], gate_weight.shape[0], gate_weight.shape[1])
    ask, low, high = begin(label, embed, class_table, kv)
    asked = lax.ppermute(ask, "dp", behind)
    peer_out = lax.ppermute(out_weight, "dp", ahead)
    up_pairs = [(i, i + 1) for i in range(row_count - 1)]
    up = lax.ppermute(low, "row", up_pairs)
    down = lax.ppermute(high, "row", [(j, i) for i, j in up_pairs])
    answered = lax.ppermute(answer(asked, class_table, gate_weight), "dp", ahead)
    near_pairs = [(i, i ^ 1) for i in range(col_count)]
    far_pairs = [(i, i + 1) for i in range(1, col_count - 1, 2)]
    near, far = edges(kv, up, down)
    near = lax.ppermute(near, "col", near_pairs)
    far = lax.ppermute(far, "col", far_pairs + [(j, i) for i, j in far_pairs])

    sent = mix(out_weight, peer_out, ask, answered, gate_weight)
    sent, near, far = lax.optimization_barrier((sent, near, far))
    got = [sent] + [
        lax.ppermute(sent, "row", [(i, (i + k) % row_count) for i in range(row_count)])
        for k in range(1, row_count)
    ]
    attended = attend(queries.reshape(-1, inner), kv, up, down, near, far)
    stack, attended = lax.optimization_barrier((stacked(got), attended))
    places = [stack] + [
        lax.ppermute(stack, "col", [(i, (i + 2 * k) % col_count) for i in range(col_count)])
        for k in range(1, col_count // 2)
    ]
    siblings = [lax.ppermute(part, "col", near_pairs) for part in places]
    result = project(attended, places + siblings)
    return result.reshape(1, tile_rows, tile_cols, -1)


def local(queries, keyvals, out_weight, gate_weight, class_table, labels, timesteps, round_index):
    bit_count = lax.axis_size("dp").bit_length() - 1

    def branch(power):
        return lambda *args: body(2**power, *args)

    return lax.switch(
        round_index[0] % bit_count,
        [branch(power) for power in range(bit_count)],
        queries[0],
        keyvals[0],
        out_weight[0],
        gate_weight[0],
        class_table[0],
        labels,
        timesteps,
    )


def solution(mesh):
    placed = (
        P("dp", "row", "col", None),
        P("dp", None, "row", "col", None),
        P("dp", ("row", "col"), None),
        P("dp", ("row", "col"), None),
        P("dp", None, ("row", "col")),
        P("dp"),
        P("dp"),
        P(),
    )
    return jax.shard_map(
        local, mesh=mesh, in_specs=placed, out_specs=P("dp", "row", "col", None), check_vma=False
    )
```

time: 134 us -> 97.8 us (0.73)
  starting transfers between devices: 77.7 us -> 59 us
  local copies, waits for them, and re-layouts: 10.3 us -> 2.04 us
  loops' own time: 4.59 us -> 1.21 us
  other arithmetic: 3.38 us -> 0.06 us
  Pallas kernels: 8.76 us -> 6.81 us
    ppermute x1, starting transfers between devices: 16.4 us -> 2.34 us  [body(): peer_out = lax.ppermute(out_weight, 'dp', ahead)]
    ppermute x3, waiting for transfers between devices: 1.29 us -> 8.51 us  [body(): lax.ppermute(stack, 'col', [(i, (i + 2 * k) % col_count) for i in range(c...]
    ppermute x6, waiting for transfers between devices: 15.4 us -> 9.28 us  [the longest x1 4 us: body(): down = lax.ppermute(high, 'row', [(j, i) for i, j in up_pairs])]
    pallas_call x1, Pallas kernels: 6.04 us -> 2.33 us  [project(): pl.pallas_call(project_kernel, out_shape=jax.ShapeDtypeStruct((tokens, wi...]
    another operation x1, loops' own time: 4.59 us -> 1.21 us  [local(): lax.switch(round_index[0] % bit_count, [branch(power) for power in range(...]
    slice x7 -> x0, local copies, waits for them, and re-layouts: 3.36 us -> none  [the longest x1 1.78 us: body(): down = lax.ppermute(keyvals[:, :RADIUS], 'row', down_pairs)]
    ppermute x6, starting transfers between devices: 24.2 us -> 21.1 us  [the longest x1 6.68 us: body(): near = lax.ppermute(near, 'col', near_pairs)]
    pallas_call x0 -> x5, Pallas kernels: none -> 3.09 us  [the longest x1 1.7 us: begin(): pl.pallas_call(begin_kernel, out_shape=(jax.ShapeDtypeStruct((1, 256), F3...]
  transfers between devices with their start and end apart: 17 -> 17, of which waited for: 5 -> 8; matrix products, arithmetic and copies ran while one was open for 7% -> 0% of each run, Pallas kernels for 2% -> 2%
where the time goes in v2:
time: 97.8 us; the launch traced here: 97.2 us
  starting transfers between devices  59 us (60%)
  waiting for transfers between devices  27.3 us (28%)
  Pallas kernels  6.81 us (7%)
  local copies, waits for them, and re-layouts  2.04 us (2%)
  loops' own time  1.21 us (1%)
    ppermute x4, starting transfers between devices, body(): siblings = [lax.ppermute(part, 'col', near_pairs) for part in places]  16.6 us
    ppermute x3, starting transfers between devices, body(): lax.ppermute(stack, 'col', [(i, (i + 2 * k) % col_count) for i in range(c...  9.74 us
    ppermute x3, starting transfers between devices, body(): lax.ppermute(sent, 'row', [(i, (i + k) % row_count) for i in range(row_co...  9.22 us
    ppermute x3, waiting for transfers between devices, body(): lax.ppermute(stack, 'col', [(i, (i + 2 * k) % col_count) for i in range(c...  8.51 us
    ppermute x3, waiting for transfers between devices, body(): lax.ppermute(sent, 'row', [(i, (i + k) % row_count) for i in range(row_co...  7.97 us
    ppermute x1, starting transfers between devices, body(): near = lax.ppermute(near, 'col', near_pairs)  6.68 us
    ppermute x1, starting transfers between devices, body(): up = lax.ppermute(low, 'row', up_pairs)  4.38 us
    ppermute x1, starting transfers between devices, body(): asked = lax.ppermute(ask, 'dp', behind)  4.15 us
  transfers between devices with their start and end apart: 17, of which 8 were waited for; matrix products, arithmetic and copies ran while one was open for 0% of the time, Pallas kernels for 2%

profile of v2, /device:TPU:1, one launch (start us, length us, event | category | flops | bytes accessed | tf_op | source)
XLA Modules:
  0.0 97.2 jit_solution(16260254036010521640)
XLA Ops:
  0.7 1.1 %copy.13 = bf16[1,1000,64]{2,1,0:T(8,128)(2,1)S(1)} copy(bf16[1,1000,64]{1,2,0:T(8,128)(2,1)} %param.16) | data formatting | bytes 256000 | tf_op args[4]
  1.9 94.4 %conditional.1 = (bf16[1,12,16,2048]{3,2,1,0:T(8,128)(2,1)S(1)}) conditional(s32[]{:T(128)} %clamp.3, (bf16[32,2048]{1,0:T(8,128)(2,1)S(1)}, s32[1]{0:T(128)}, bf16[1,2,12,16,1024]{4,3,2,1,0:T(8,128)(2,1)}, s32[1]{0:T(128)}, bf16[1000,64]{1,0:T(8,128)(2,1)S(1)}, /*index=5*/bf16[64,2048]{1,0:T(8,128)(2,1)S(1)}, ...), branch_computations={%region_0.1_spmd, %region_1.2_spmd, %region_2.3_spmd, %region_3.4_... | conditional | flops 2010001152 | bytes 36040848 | solution.py:360
  2.1 0.0 copy-start.2
  2.8 0.1 compare_select_fusion.8.embed_ref
  2.9 1.7 %begin.6 = (f32[1,256]{1,0:T(1,128)S(1)}, bf16[2,48,1024]{2,1,0:T(8,128)(2,1)S(1)}, bf16[2,48,1024]{2,1,0:T(8,128)(2,1)S(1)}) custom-call(s32[1]{0:T(128)} %get-tuple-element.101.label_ref, f32[1,64]{1,0:T(1,128)S(1)} %compare_select_fusion.8.embed_ref, bf16[1000,64]{1,0:T(8,128)(2,1)S(1)} %get-tuple-element.103.table_ref, bf16[2,192,1024]{2,1,0:T(8,128)(2,1)} %bitcast.29), custom_call_target="tpu_custom_call" | custom-call | tf_op jit(solution)/shard_map/cond/branch_2_fun/begin/pallas_call | solution.py:128
  4.6 4.4 %collective-permute-start.37 = (bf16[2,48,1024]{2,1,0:T(8,128)(2,1)S(1)}, bf16[2,48,1024]{2,1,0:T(8,128)(2,1)S(1)}, u32[]{:S(2)}, u32[]{:S(2)}) collective-permute-start(bf16[2,48,1024]{2,1,0:T(8,128)(2,1)S(1)} %get-tuple-element.107), channel_id=1, source_target_pairs={{0,8},{8,16},{16,24},{1,9},{9,17},{17,25},{2,10},{10,18},{18,26},{... | collective-permute-start | bytes 589832 | tf_op jit(solution)/shard_map/cond/branch_2_fun/ppermute | solution.py:328
  9.0 1.3 %collective-permute-start.38 = (bf16[2,48,1024]{2,1,0:T(8,128)(2,1)S(1)}, bf16[2,48,1024]{2,1,0:T(8,128)(2,1)S(1)}, u32[]{:S(2)}, u32[]{:S(2)}) collective-permute-start(bf16[2,48,1024]{2,1,0:T(8,128)(2,1)S(1)} %get-tuple-element.108), channel_id=1, source_target_pairs={{8,0},{16,8},{24,16},{9,1},{17,9},{25,17},{10,2},{18,10},{26,18},{... | collective-permute-start | bytes 589832 | tf_op jit(solution)/shard_map/cond/branch_2_fun/ppermute | solution.py:329
  10.3 1.3 %collective-permute-done.37.up_ref = bf16[2,48,1024]{2,1,0:T(8,128)(2,1)S(1)} collective-permute-done((bf16[2,48,1024]{2,1,0:T(8,128)(2,1)S(1)}, bf16[2,48,1024]{2,1,0:T(8,128)(2,1)S(1)}, u32[]{:S(2)}, u32[]{:S(2)}) %collective-permute-start.37) | collective-permute-done | bytes 196640 | tf_op jit(solution)/shard_map/cond/branch_2_fun/ppermute | solution.py:328
  11.6 4.0 %collective-permute-done.38.down_ref = bf16[2,48,1024]{2,1,0:T(8,128)(2,1)S(1)} collective-permute-done((bf16[2,48,1024]{2,1,0:T(8,128)(2,1)S(1)}, bf16[2,48,1024]{2,1,0:T(8,128)(2,1)S(1)}, u32[]{:S(2)}, u32[]{:S(2)}) %collective-permute-start.38) | collective-permute-done | bytes 196640 | tf_op jit(solution)/shard_map/cond/branch_2_fun/ppermute | solution.py:329
  15.6 0.7 edges.6
  16.3 6.7 %collective-permute-start.39 = (bf16[2,80,1024]{2,1,0:T(8,128)(2,1)S(1)}, bf16[2,80,1024]{2,1,0:T(8,128)(2,1)S(1)}, u32[]{:S(2)}, u32[]{:S(2)}) collective-permute-start(bf16[2,80,1024]{2,1,0:T(8,128)(2,1)S(1)} %get-tuple-element.109), channel_id=1, source_target_pairs={{0,1},{1,0},{2,3},{3,2},{4,5},{5,4},{6,7},{7,6},{8,9},{9,8},{10,11... | collective-permute-start | bytes 983048 | tf_op jit(solution)/shard_map/cond/branch_2_fun/ppermute | solution.py:334
  23.0 1.9 %collective-permute-start.40 = (bf16[2,80,1024]{2,1,0:T(8,128)(2,1)S(1)}, bf16[2,80,1024]{2,1,0:T(8,128)(2,1)S(1)}, u32[]{:S(2)}, u32[]{:S(2)}) collective-permute-start(bf16[2,80,1024]{2,1,0:T(8,128)(2,1)S(1)} %get-tuple-element.110), channel_id=1, source_target_pairs={{1,2},{3,4},{5,6},{2,1},{4,3},{6,5},{9,10},{11,12},{13,14},{10,9},... | collective-permute-start | bytes 983048 | tf_op jit(solution)/shard_map/cond/branch_2_fun/ppermute | solution.py:335
  24.9 2.3 %collective-permute-start.34 = (bf16[32,2048]{1,0:T(8,128)(2,1)S(1)}, bf16[32,2048]{1,0:T(8,128)(2,1)S(1)}, u32[]{:S(2)}, u32[]{:S(2)}) collective-permute-start(bf16[32,2048]{1,0:T(8,128)(2,1)S(1)} %get-tuple-element.100.own_ref), channel_id=1, source_target_pairs={{0,128},{32,160},{64,192},{96,224},{128,256},{160,288},{192,320},{... | collective-permute-start | bytes 393224 | tf_op jit(solution)/shard_map/cond/branch_2_fun/ppermute | solution.py:326
  27.2 4.2 %collective-permute-start.35 = (f32[1,256]{1,0:T(1,128)S(1)}, f32[1,256]{1,0:T(1,128)S(1)}, u32[]{:S(2)}, u32[]{:S(2)}) collective-permute-start(f32[1,256]{1,0:T(1,128)S(1)} %get-tuple-element.105.ask_ref), channel_id=1, source_target_pairs={{128,0},{160,32},{192,64},{224,96},{256,128},{288,160},{320,192},{... | collective-permute-start | bytes 3080 | tf_op jit(solution)/shard_map/cond/branch_2_fun/ppermute | solution.py:325
  31.4 0.7 collective-permute-done.35.asked_ref
  32.1 0.4 answer.6
  32.5 0.0 copy-start.9
  32.5 2.7 %collective-permute-start.36 = (f32[1,2176]{1,0:T(1,128)S(1)}, f32[1,2176]{1,0:T(1,128)S(1)}, u32[]{:S(2)}, u32[]{:S(2)}) collective-permute-start(f32[1,2176]{1,0:T(1,128)S(1)} %answer.6), channel_id=1, source_target_pairs={{0,128},{32,160},{64,192},{96,224},{128,256},{160,288},{192,320},{... | collective-permute-start | bytes 26120 | tf_op jit(solution)/shard_map/cond/branch_2_fun/ppermute | solution.py:330
  35.2 3.3 %collective-permute-done.36.answered_ref = f32[1,2176]{1,0:T(1,128)S(1)} collective-permute-done((f32[1,2176]{1,0:T(1,128)S(1)}, f32[1,2176]{1,0:T(1,128)S(1)}, u32[]{:S(2)}, u32[]{:S(2)}) %collective-permute-start.36) | collective-permute-done | bytes 8736 | tf_op jit(solution)/shard_map/cond/branch_2_fun/ppermute | solution.py:330
  38.5 0.0 collective-permute-done.34.peer_ref
  38.5 0.2 mix.6.refs_0_
  38.7 0.0 collective-permute-done.39.near_ref
  38.8 0.0 collective-permute-done.40.far_ref
  38.8 2.9 %collective-permute-start.43 = (bf16[40,2048]{1,0:T(8,128)(2,1)S(1)}, bf16[40,2048]{1,0:T(8,128)(2,1)S(1)}, u32[]{:S(2)}, u32[]{:S(2)}) collective-permute-start(bf16[40,2048]{1,0:T(8,128)(2,1)S(1)} %mix.6.refs_0_), channel_id=1, source_target_pairs={{0,24},{8,0},{16,8},{24,16},{1,25},{9,1},{17,9},{25,17},{2,26},{10... | collective-permute-start | bytes 491528 | tf_op jit(solution)/shard_map/cond/branch_2_fun/ppermute | solution.py:340
  41.7 2.9 %collective-permute-start.42 = (bf16[40,2048]{1,0:T(8,128)(2,1)S(1)}, bf16[40,2048]{1,0:T(8,128)(2,1)S(1)}, u32[]{:S(2)}, u32[]{:S(2)}) collective-permute-start(bf16[40,2048]{1,0:T(8,128)(2,1)S(1)} %mix.6.refs_0_), channel_id=1, source_target_pairs={{0,16},{8,24},{16,0},{24,8},{1,17},{9,25},{17,1},{25,9},{2,18},{10... | collective-permute-start | bytes 491528 | tf_op jit(solution)/shard_map/cond/branch_2_fun/ppermute | solution.py:340
  44.6 3.4 %collective-permute-start.41 = (bf16[40,2048]{1,0:T(8,128)(2,1)S(1)}, bf16[40,2048]{1,0:T(8,128)(2,1)S(1)}, u32[]{:S(2)}, u32[]{:S(2)}) collective-permute-start(bf16[40,2048]{1,0:T(8,128)(2,1)S(1)} %mix.6.refs_0_), channel_id=1, source_target_pairs={{0,8},{8,16},{16,24},{24,0},{1,9},{9,17},{17,25},{25,1},{2,10},{10... | collective-permute-start | bytes 491528 | tf_op jit(solution)/shard_map/cond/branch_2_fun/ppermute | solution.py:340
  48.0 1.4 %attend.6.a_ref = bf16[192,1024]{1,0:T(8,128)(2,1)S(1)} custom-call(bf16[192,1024]{1,0:T(8,128)(2,1)S(1)} %bitcast.53, bf16[2,192,1024]{2,1,0:T(8,128)(2,1)S(1)} %bitcast.31, bf16[2,48,1024]{2,1,0:T(8,128)(2,1)S(1)} %collective-permute-done.37.up_ref, bf16[2,48,1024]{2,1,0:T(8,128)(2,1)S(1)} %collective-permute-done.38.down_ref, ...), custom_call_target="tpu_custom_call" | custom-call | flops 1200000000 | bytes 3000000 | tf_op jit(solution)/shard_map/cond/branch_2_fun/attend/pallas_call | solution.py:83
  49.4 0.0 collective-permute-done.43.refs_3_
  49.4 8.0 %collective-permute-done.42.refs_2_ = bf16[40,2048]{1,0:T(8,128)(2,1)S(1)} collective-permute-done((bf16[40,2048]{1,0:T(8,128)(2,1)S(1)}, bf16[40,2048]{1,0:T(8,128)(2,1)S(1)}, u32[]{:S(2)}, u32[]{:S(2)}) %collective-permute-start.42) | collective-permute-done | bytes 163872 | tf_op jit(solution)/shard_map/cond/branch_2_fun/ppermute | solution.py:340
  57.4 0.0 collective-permute-done.41.refs_1_
  57.4 0.1 stack.6.refs_0_
  57.5 1.9 %collective-permute-start.46 = (bf16[136,2048]{1,0:T(8,128)(2,1)S(1)}, bf16[136,2048]{1,0:T(8,128)(2,1)S(1)}, u32[]{:S(2)}, u32[]{:S(2)}) collective-permute-start(bf16[136,2048]{1,0:T(8,128)(2,1)S(1)} %stack.6.refs_0_), channel_id=1, source_target_pairs={{0,6},{1,7},{2,0},{3,1},{4,2},{5,3},{6,4},{7,5},{8,14},{9,15},{10,... | collective-permute-start | bytes 1671176 | tf_op jit(solution)/shard_map/cond/branch_2_fun/ppermute | solution.py:346
  59.4 5.5 %collective-permute-start.45 = (bf16[136,2048]{1,0:T(8,128)(2,1)S(1)}, bf16[136,2048]{1,0:T(8,128)(2,1)S(1)}, u32[]{:S(2)}, u32[]{:S(2)}) collective-permute-start(bf16[136,2048]{1,0:T(8,128)(2,1)S(1)} %stack.6.refs_0_), channel_id=1, source_target_pairs={{0,4},{1,5},{2,6},{3,7},{4,0},{5,1},{6,2},{7,3},{8,12},{9,13},{10,... | collective-permute-start | bytes 1671176 | tf_op jit(solution)/shard_map/cond/branch_2_fun/ppermute | solution.py:346
  65.0 2.3 %collective-permute-start.44 = (bf16[136,2048]{1,0:T(8,128)(2,1)S(1)}, bf16[136,2048]{1,0:T(8,128)(2,1)S(1)}, u32[]{:S(2)}, u32[]{:S(2)}) collective-permute-start(bf16[136,2048]{1,0:T(8,128)(2,1)S(1)} %stack.6.refs_0_), channel_id=1, source_target_pairs={{0,2},{1,3},{2,4},{3,5},{4,6},{5,7},{6,0},{7,1},{8,10},{9,11},{10,... | collective-permute-start | bytes 1671176 | tf_op jit(solution)/shard_map/cond/branch_2_fun/ppermute | solution.py:346
  67.2 4.1 %collective-permute-start.47 = (bf16[136,2048]{1,0:T(8,128)(2,1)S(1)}, bf16[136,2048]{1,0:T(8,128)(2,1)S(1)}, u32[]{:S(2)}, u32[]{:S(2)}) collective-permute-start(bf16[136,2048]{1,0:T(8,128)(2,1)S(1)} %stack.6.refs_0_), channel_id=1, source_target_pairs={{0,1},{1,0},{2,3},{3,2},{4,5},{5,4},{6,7},{7,6},{8,9},{9,8},{10,11... | collective-permute-start | bytes 1671176 | tf_op jit(solution)/shard_map/cond/branch_2_fun/ppermute | solution.py:349
  71.4 1.8 %collective-permute-done.46.refs_3_ = bf16[136,2048]{1,0:T(8,128)(2,1)S(1)} collective-permute-done((bf16[136,2048]{1,0:T(8,128)(2,1)S(1)}, bf16[136,2048]{1,0:T(8,128)(2,1)S(1)}, u32[]{:S(2)}, u32[]{:S(2)}) %collective-permute-start.46) | collective-permute-done | bytes 557088 | tf_op jit(solution)/shard_map/cond/branch_2_fun/ppermute | solution.py:346
  73.2 4.8 %collective-permute-start.50 = (bf16[136,2048]{1,0:T(8,128)(2,1)S(1)}, bf16[136,2048]{1,0:T(8,128)(2,1)S(1)}, u32[]{:S(2)}, u32[]{:S(2)}) collective-permute-start(bf16[136,2048]{1,0:T(8,128)(2,1)S(1)} %collective-permute-done.46.refs_3_), channel_id=1, source_target_pairs={{0,1},{1,0},{2,3},{3,2},{4,5},{5,4},{6,7},{7,6},{8,9},{9,8},{10,11... | collective-permute-start | bytes 1671176 | tf_op jit(solution)/shard_map/cond/branch_2_fun/ppermute | solution.py:349
  78.0 0.0 collective-permute-done.45.refs_2_
  78.0 5.2 %collective-permute-start.49 = (bf16[136,2048]{1,0:T(8,128)(2,1)S(1)}, bf16[136,2048]{1,0:T(8,128)(2,1)S(1)}, u32[]{:S(2)}, u32[]{:S(2)}) collective-permute-start(bf16[136,2048]{1,0:T(8,128)(2,1)S(1)} %collective-permute-done.45.refs_2_), channel_id=1, source_target_pairs={{0,1},{1,0},{2,3},{3,2},{4,5},{5,4},{6,7},{7,6},{8,9},{9,8},{10,11... | collective-permute-start | bytes 1671176 | tf_op jit(solution)/shard_map/cond/branch_2_fun/ppermute | solution.py:349
  83.2 6.7 %collective-permute-done.44.refs_1_ = bf16[136,2048]{1,0:T(8,128)(2,1)S(1)} collective-permute-done((bf16[136,2048]{1,0:T(8,128)(2,1)S(1)}, bf16[136,2048]{1,0:T(8,128)(2,1)S(1)}, u32[]{:S(2)}, u32[]{:S(2)}) %collective-permute-start.44) | collective-permute-done | bytes 557088 | tf_op jit(solution)/shard_map/cond/branch_2_fun/ppermute | solution.py:346
  90.0 2.4 %collective-permute-start.48 = (bf16[136,2048]{1,0:T(8,128)(2,1)S(1)}, bf16[136,2048]{1,0:T(8,128)(2,1)S(1)}, u32[]{:S(2)}, u32[]{:S(2)}) collective-permute-start(bf16[136,2048]{1,0:T(8,128)(2,1)S(1)} %collective-permute-done.44.refs_1_), channel_id=1, source_target_pairs={{0,1},{1,0},{2,3},{3,2},{4,5},{5,4},{6,7},{7,6},{8,9},{9,8},{10,11... | collective-permute-start | bytes 1671176 | tf_op jit(solution)/shard_map/cond/branch_2_fun/ppermute | solution.py:349
  92.4 0.0 collective-permute-done.47.refs_4_
  92.4 0.0 collective-permute-done.50.refs_7_
  92.4 0.0 collective-permute-done.49.refs_6_
  92.4 1.5 %collective-permute-done.48.refs_5_ = bf16[136,2048]{1,0:T(8,128)(2,1)S(1)} collective-permute-done((bf16[136,2048]{1,0:T(8,128)(2,1)S(1)}, bf16[136,2048]{1,0:T(8,128)(2,1)S(1)}, u32[]{:S(2)}, u32[]{:S(2)}) %collective-permute-start.48) | collective-permute-done | bytes 557088 | tf_op jit(solution)/shard_map/cond/branch_2_fun/ppermute | solution.py:349
  93.9 2.3 %project.6 = bf16[192,2048]{1,0:T(8,128)(2,1)S(1)} custom-call(bf16[192,1024]{1,0:T(8,128)(2,1)S(1)} %attend.6.a_ref, bf16[136,2048]{1,0:T(8,128)(2,1)S(1)} %stack.6.refs_0_, bf16[136,2048]{1,0:T(8,128)(2,1)S(1)} %collective-permute-done.44.refs_1_, bf16[136,2048]{1,0:T(8,128)(2,1)S(1)} %collective-permute-done.45.refs_2_, ...), custom_call_target="tpu_custom_call" | custom-call | flops 810000000 | bytes 6000000 | tf_op jit(solution)/shard_map/cond/branch_2_fun/project/pallas_call | solution.py:291
  96.3 0.0 copy-start.6
  96.3 0.9 copy-done.6
  (6 shorter events, 0.0 us)
Async XLA Ops:
  0.0 1.9 %copy-start.4 = (bf16[1,64,2048]{2,1,0:T(8,128)(2,1)S(1)}, bf16[1,64,2048]{2,1,0:T(8,128)(2,1)}, u32[]{:S(2)}) copy-start(bf16[1,64,2048]{2,1,0:T(8,128)(2,1)} %param.15) | copy-start | bytes 786436
  0.7 1.2 %copy-start.5 = (bf16[1,32,2048]{2,1,0:T(8,128)(2,1)S(1)}, bf16[1,32,2048]{2,1,0:T(8,128)(2,1)}, u32[]{:S(2)}) copy-start(bf16[1,32,2048]{2,1,0:T(8,128)(2,1)} %param.14) | copy-start | bytes 393220
  2.1 13.5 %copy-start.2 = (bf16[1,2,12,16,1024]{4,3,2,1,0:T(8,128)(2,1)S(1)}, bf16[1,2,12,16,1024]{4,3,2,1,0:T(8,128)(2,1)}, u32[]{:S(2)}) copy-start(bf16[1,2,12,16,1024]{4,3,2,1,0:T(8,128)(2,1)} %get-tuple-element.104) | copy-start | bytes 2359300 | tf_op jit(solution)/shard_map/cond
  4.6 7.0 %collective-permute-start.37 = (bf16[2,48,1024]{2,1,0:T(8,128)(2,1)S(1)}, bf16[2,48,1024]{2,1,0:T(8,128)(2,1)S(1)}, u32[]{:S(2)}, u32[]{:S(2)}) collective-permute-start(bf16[2,48,1024]{2,1,0:T(8,128)(2,1)S(1)} %get-tuple-element.107), channel_id=1, source_target_pairs={{0,8},{8,16},{16,24},{1,9},{9,17},{17,25},{2,10},{10,18},{18,26},{... | collective-permute-start | bytes 589832 | tf_op jit(solution)/shard_map/cond/branch_2_fun/ppermute | solution.py:328
  9.0 6.6 %collective-permute-start.38 = (bf16[2,48,1024]{2,1,0:T(8,128)(2,1)S(1)}, bf16[2,48,1024]{2,1,0:T(8,128)(2,1)S(1)}, u32[]{:S(2)}, u32[]{:S(2)}) collective-permute-start(bf16[2,48,1024]{2,1,0:T(8,128)(2,1)S(1)} %get-tuple-element.108), channel_id=1, source_target_pairs={{8,0},{16,8},{24,16},{9,1},{17,9},{25,17},{10,2},{18,10},{26,18},{... | collective-permute-start | bytes 589832 | tf_op jit(solution)/shard_map/cond/branch_2_fun/ppermute | solution.py:329
  16.3 22.5 %collective-permute-start.39 = (bf16[2,80,1024]{2,1,0:T(8,128)(2,1)S(1)}, bf16[2,80,1024]{2,1,0:T(8,128)(2,1)S(1)}, u32[]{:S(2)}, u32[]{:S(2)}) collective-permute-start(bf16[2,80,1024]{2,1,0:T(8,128)(2,1)S(1)} %get-tuple-element.109), channel_id=1, source_target_pairs={{0,1},{1,0},{2,3},{3,2},{4,5},{5,4},{6,7},{7,6},{8,9},{9,8},{10,11... | collective-permute-start | bytes 983048 | tf_op jit(solution)/shard_map/cond/branch_2_fun/ppermute | solution.py:334
  23.0 15.8 %collective-permute-start.40 = (bf16[2,80,1024]{2,1,0:T(8,128)(2,1)S(1)}, bf16[2,80,1024]{2,1,0:T(8,128)(2,1)S(1)}, u32[]{:S(2)}, u32[]{:S(2)}) collective-permute-start(bf16[2,80,1024]{2,1,0:T(8,128)(2,1)S(1)} %get-tuple-element.110), channel_id=1, source_target_pairs={{1,2},{3,4},{5,6},{2,1},{4,3},{6,5},{9,10},{11,12},{13,14},{10,9},... | collective-permute-start | bytes 983048 | tf_op jit(solution)/shard_map/cond/branch_2_fun/ppermute | solution.py:335
  24.9 13.6 %collective-permute-start.34 = (bf16[32,2048]{1,0:T(8,128)(2,1)S(1)}, bf16[32,2048]{1,0:T(8,128)(2,1)S(1)}, u32[]{:S(2)}, u32[]{:S(2)}) collective-permute-start(bf16[32,2048]{1,0:T(8,128)(2,1)S(1)} %get-tuple-element.100.own_ref), channel_id=1, source_target_pairs={{0,128},{32,160},{64,192},{96,224},{128,256},{160,288},{192,320},{... | collective-permute-start | bytes 393224 | tf_op jit(solution)/shard_map/cond/branch_2_fun/ppermute | solution.py:326
  27.2 4.9 %collective-permute-start.35 = (f32[1,256]{1,0:T(1,128)S(1)}, f32[1,256]{1,0:T(1,128)S(1)}, u32[]{:S(2)}, u32[]{:S(2)}) collective-permute-start(f32[1,256]{1,0:T(1,128)S(1)} %get-tuple-element.105.ask_ref), channel_id=1, source_target_pairs={{128,0},{160,32},{192,64},{224,96},{256,128},{288,160},{320,192},{... | collective-permute-start | bytes 3080 | tf_op jit(solution)/shard_map/cond/branch_2_fun/ppermute | solution.py:325
  32.5 15.5 %copy-start.9 = (bf16[1,12,16,1024]{3,2,1,0:T(8,128)(2,1)S(1)}, bf16[1,12,16,1024]{3,2,1,0:T(8,128)(2,1)}, u32[]{:S(2)}) copy-start(bf16[1,12,16,1024]{3,2,1,0:T(8,128)(2,1)} %get-tuple-element.112) | copy-start | bytes 1179652 | tf_op jit(solution)/shard_map/cond
  32.5 6.0 %collective-permute-start.36 = (f32[1,2176]{1,0:T(1,128)S(1)}, f32[1,2176]{1,0:T(1,128)S(1)}, u32[]{:S(2)}, u32[]{:S(2)}) collective-permute-start(f32[1,2176]{1,0:T(1,128)S(1)} %answer.6), channel_id=1, source_target_pairs={{0,128},{32,160},{64,192},{96,224},{128,256},{160,288},{192,320},{... | collective-permute-start | bytes 26120 | tf_op jit(solution)/shard_map/cond/branch_2_fun/ppermute | solution.py:330
  38.8 10.7 %collective-permute-start.43 = (bf16[40,2048]{1,0:T(8,128)(2,1)S(1)}, bf16[40,2048]{1,0:T(8,128)(2,1)S(1)}, u32[]{:S(2)}, u32[]{:S(2)}) collective-permute-start(bf16[40,2048]{1,0:T(8,128)(2,1)S(1)} %mix.6.refs_0_), channel_id=1, source_target_pairs={{0,24},{8,0},{16,8},{24,16},{1,25},{9,1},{17,9},{25,17},{2,26},{10... | collective-permute-start | bytes 491528 | tf_op jit(solution)/shard_map/cond/branch_2_fun/ppermute | solution.py:340
  41.7 15.7 %collective-permute-start.42 = (bf16[40,2048]{1,0:T(8,128)(2,1)S(1)}, bf16[40,2048]{1,0:T(8,128)(2,1)S(1)}, u32[]{:S(2)}, u32[]{:S(2)}) collective-permute-start(bf16[40,2048]{1,0:T(8,128)(2,1)S(1)} %mix.6.refs_0_), channel_id=1, source_target_pairs={{0,16},{8,24},{16,0},{24,8},{1,17},{9,25},{17,1},{25,9},{2,18},{10... | collective-permute-start | bytes 491528 | tf_op jit(solution)/shard_map/cond/branch_2_fun/ppermute | solution.py:340
  44.6 12.7 %collective-permute-start.41 = (bf16[40,2048]{1,0:T(8,128)(2,1)S(1)}, bf16[40,2048]{1,0:T(8,128)(2,1)S(1)}, u32[]{:S(2)}, u32[]{:S(2)}) collective-permute-start(bf16[40,2048]{1,0:T(8,128)(2,1)S(1)} %mix.6.refs_0_), channel_id=1, source_target_pairs={{0,8},{8,16},{16,24},{24,0},{1,9},{9,17},{17,25},{25,1},{2,10},{10... | collective-permute-start | bytes 491528 | tf_op jit(solution)/shard_map/cond/branch_2_fun/ppermute | solution.py:340
  57.5 15.7 %collective-permute-start.46 = (bf16[136,2048]{1,0:T(8,128)(2,1)S(1)}, bf16[136,2048]{1,0:T(8,128)(2,1)S(1)}, u32[]{:S(2)}, u32[]{:S(2)}) collective-permute-start(bf16[136,2048]{1,0:T(8,128)(2,1)S(1)} %stack.6.refs_0_), channel_id=1, source_target_pairs={{0,6},{1,7},{2,0},{3,1},{4,2},{5,3},{6,4},{7,5},{8,14},{9,15},{10,... | collective-permute-start | bytes 1671176 | tf_op jit(solution)/shard_map/cond/branch_2_fun/ppermute | solution.py:346
  59.4 18.6 %collective-permute-start.45 = (bf16[136,2048]{1,0:T(8,128)(2,1)S(1)}, bf16[136,2048]{1,0:T(8,128)(2,1)S(1)}, u32[]{:S(2)}, u32[]{:S(2)}) collective-permute-start(bf16[136,2048]{1,0:T(8,128)(2,1)S(1)} %stack.6.refs_0_), channel_id=1, source_target_pairs={{0,4},{1,5},{2,6},{3,7},{4,0},{5,1},{6,2},{7,3},{8,12},{9,13},{10,... | collective-permute-start | bytes 1671176 | tf_op jit(solution)/shard_map/cond/branch_2_fun/ppermute | solution.py:346
  65.0 25.0 %collective-permute-start.44 = (bf16[136,2048]{1,0:T(8,128)(2,1)S(1)}, bf16[136,2048]{1,0:T(8,128)(2,1)S(1)}, u32[]{:S(2)}, u32[]{:S(2)}) collective-permute-start(bf16[136,2048]{1,0:T(8,128)(2,1)S(1)} %stack.6.refs_0_), channel_id=1, source_target_pairs={{0,2},{1,3},{2,4},{3,5},{4,6},{5,7},{6,0},{7,1},{8,10},{9,11},{10,... | collective-permute-start | bytes 1671176 | tf_op jit(solution)/shard_map/cond/branch_2_fun/ppermute | solution.py:346
  67.2 25.1 %collective-permute-start.47 = (bf16[136,2048]{1,0:T(8,128)(2,1)S(1)}, bf16[136,2048]{1,0:T(8,128)(2,1)S(1)}, u32[]{:S(2)}, u32[]{:S(2)}) collective-permute-start(bf16[136,2048]{1,0:T(8,128)(2,1)S(1)} %stack.6.refs_0_), channel_id=1, source_target_pairs={{0,1},{1,0},{2,3},{3,2},{4,5},{5,4},{6,7},{7,6},{8,9},{9,8},{10,11... | collective-permute-start | bytes 1671176 | tf_op jit(solution)/shard_map/cond/branch_2_fun/ppermute | solution.py:349
  73.2 19.2 %collective-permute-start.50 = (bf16[136,2048]{1,0:T(8,128)(2,1)S(1)}, bf16[136,2048]{1,0:T(8,128)(2,1)S(1)}, u32[]{:S(2)}, u32[]{:S(2)}) collective-permute-start(bf16[136,2048]{1,0:T(8,128)(2,1)S(1)} %collective-permute-done.46.refs_3_), channel_id=1, source_target_pairs={{0,1},{1,0},{2,3},{3,2},{4,5},{5,4},{6,7},{7,6},{8,9},{9,8},{10,11... | collective-permute-start | bytes 1671176 | tf_op jit(solution)/shard_map/cond/branch_2_fun/ppermute | solution.py:349
  78.0 14.4 %collective-permute-start.49 = (bf16[136,2048]{1,0:T(8,128)(2,1)S(1)}, bf16[136,2048]{1,0:T(8,128)(2,1)S(1)}, u32[]{:S(2)}, u32[]{:S(2)}) collective-permute-start(bf16[136,2048]{1,0:T(8,128)(2,1)S(1)} %collective-permute-done.45.refs_2_), channel_id=1, source_target_pairs={{0,1},{1,0},{2,3},{3,2},{4,5},{5,4},{6,7},{7,6},{8,9},{9,8},{10,11... | collective-permute-start | bytes 1671176 | tf_op jit(solution)/shard_map/cond/branch_2_fun/ppermute | solution.py:349
  90.0 4.0 %collective-permute-start.48 = (bf16[136,2048]{1,0:T(8,128)(2,1)S(1)}, bf16[136,2048]{1,0:T(8,128)(2,1)S(1)}, u32[]{:S(2)}, u32[]{:S(2)}) collective-permute-start(bf16[136,2048]{1,0:T(8,128)(2,1)S(1)} %collective-permute-done.44.refs_1_), channel_id=1, source_target_pairs={{0,1},{1,0},{2,3},{3,2},{4,5},{5,4},{6,7},{7,6},{8,9},{9,8},{10,11... | collective-permute-start | bytes 1671176 | tf_op jit(solution)/shard_map/cond/branch_2_fun/ppermute | solution.py:349
  96.3 0.9 copy-start.6

commit v3 on v2

--- a/solution.py
+++ b/solution.py
@@ -96,114 +96,134 @@
 
 
 def picked_row(label, table):
-    ids = lax.broadcasted_iota(jnp.int32, (16, table.shape[0]), 1).astype(F32)
+    ids = lax.broadcasted_iota(jnp.int32, (16, table.shape[1]), 1).astype(F32)
     one_hot = jnp.where(ids == label, F32(1.0), F32(0.0)).astype(BF16)
-    return jnp.dot(one_hot, table, preferred_element_type=F32)
+    return lax.dot_general(one_hot, table, (((1,), (1,)), ((), ())), preferred_element_type=F32)
 
 
 def gate_product(row_a, row_b, embed, gate_weight):
     value = (0.5 * (row_a + row_b)).astype(BF16).astype(F32) + embed
     cond = (value / (1.0 + jnp.exp(-value))).astype(BF16)
-    return jnp.dot(cond, gate_weight, preferred_element_type=F32)
-
-
-def begin_kernel(label_ref, embed_ref, table_ref, kv_ref, ask_ref, low_ref, high_ref, sems):
+    part = jnp.dot(cond, gate_weight, preferred_element_type=F32)
+    return jnp.concatenate([part[:1, at * 128 : (at + 1) * 128] for at in range(16)], axis=0)
+
+
+def to_block(value):
+    high = value.astype(BF16).astype(F32)
+    return jnp.concatenate([high, value - high], axis=0).astype(BF16)
+
+
+def from_block(block):
+    block = block.astype(F32)
+    return block[:16] + block[16:]
+
+
+def begin_kernel(label_ref, embed_ref, table_ref, ask_ref):
+    label = jnp.full((1, 1), label_ref[0], jnp.int32).astype(F32)
+    row = picked_row(label, table_ref[...])[:1]
+    ask_ref[:, 0:128] = jnp.concatenate([row, embed_ref[...]], axis=1)
+    ask_ref[:, 128:256] = jnp.broadcast_to(label, (1, 128))
+
+
+def begin(label, embed, table):
+    return pl.pallas_call(
+        begin_kernel,
+        out_shape=jax.ShapeDtypeStruct((1, 256), F32),
+        in_specs=[pl.BlockSpec(memory_space=pltpu.SMEM)] + in_vmem(2),
+        out_specs=pl.BlockSpec(memory_space=pltpu.VMEM),
+        compiler_params=pltpu.CompilerParams(vmem_limit_bytes=8 * 2**20),
+        name="begin",
+    )(label, embed, table)
+
+
+def answer_kernel(asked_ref, table_ref, gate_ref, own_ref, answer_ref):
+    shard, width = own_ref.shape
+    answer_ref[:, 0:width] = own_ref[...]
+    row = picked_row(asked_ref[:, 128:129], table_ref[...])
+    part = gate_product(row, asked_ref[:, 0:64], asked_ref[:, 64:128], gate_ref[...])
+    answer_ref[:, width : width + 128] = to_block(part)
+    rows = jnp.concatenate([row, row], axis=1)
+    answer_ref[:, width + 128 : width + 256] = jnp.concatenate([rows, rows], axis=0).astype(BF16)
+
+
+def answer(asked, table, gate_weight, own):
+    shard, width = own.shape
+    return pl.pallas_call(
+        answer_kernel,
+        out_shape=jax.ShapeDtypeStruct((shard, width + 256), BF16),
+        in_specs=in_vmem(4),
+        out_specs=pl.BlockSpec(memory_space=pltpu.VMEM),
+        compiler_params=pltpu.CompilerParams(vmem_limit_bytes=8 * 2**20),
+        name="answer",
+    )(asked, table, gate_weight, own)
+
+
+def mix_kernel(own_ref, peer_ref, ask_ref, gate_ref, sent_ref):
+    shard, width = own_ref.shape
+    peer = peer_ref[:, 0:width].astype(F32)
+    sent_ref[:, 0:width] = (0.5 * (own_ref[...].astype(F32) + peer)).astype(BF16)
+    own_row = jnp.broadcast_to(ask_ref[:, 0:64], (16, 64))
+    peer_row = peer_ref[0:16, width + 128 : width + 192].astype(F32)
+    part = gate_product(own_row, peer_row, ask_ref[:, 64:128], gate_ref[...])
+    part = 0.5 * (part + from_block(peer_ref[:, width : width + 128]))
+    sent_ref[:, width : width + 128] = to_block(part)
+
+
+def mix(own, peer, ask, gate_weight):
+    shard, width = own.shape
+    return pl.pallas_call(
+        mix_kernel,
+        out_shape=jax.ShapeDtypeStruct((shard, width + 128), BF16),
+        in_specs=in_vmem(4),
+        out_specs=pl.BlockSpec(memory_space=pltpu.VMEM),
+        compiler_params=pltpu.CompilerParams(vmem_limit_bytes=8 * 2**20),
+        name="mix",
+    )(own, peer, ask, gate_weight)
+
+
+def stack_kernel(*refs):
+    parts, out_ref = refs[:4], refs[4]
+    shard = parts[0].shape[0]
+    for index, part in enumerate(parts):
+        out_ref[index * shard : (index + 1) * shard, :] = part[...]
+
+
+def stacked(parts):
+    rows, width = parts[0].shape
+    return pl.pallas_call(
+        stack_kernel,
+        out_shape=jax.ShapeDtypeStruct((4 * rows, width), BF16),
+        in_specs=in_vmem(4),
+        out_specs=pl.BlockSpec(memory_space=pltpu.VMEM),
+        compiler_params=pltpu.CompilerParams(vmem_limit_bytes=8 * 2**20),
+        name="stack",
+    )(*parts)
+
+
+def cut_kernel(kv_ref, after_ref, low_ref, high_ref, sems):
     tokens, halo = kv_ref.shape[1], low_ref.shape[1]
     lower = pltpu.make_async_copy(kv_ref.at[:, pl.ds(tokens - halo, halo), :], low_ref, sems.at[0])
     upper = pltpu.make_async_copy(kv_ref.at[:, pl.ds(0, halo), :], high_ref, sems.at[1])
     lower.start()
     upper.start()
-    label = jnp.full((1, 1), label_ref[0], jnp.int32).astype(F32)
-    row = picked_row(label, table_ref[...])[:1]
-    ask_ref[:, 0:128] = jnp.concatenate([row, embed_ref[...]], axis=1)
-    ask_ref[:, 128:256] = jnp.broadcast_to(label, (1, 128))
     lower.wait()
     upper.wait()
 
 
-def begin(label, embed, table, kv):
-    inner = kv.shape[2]
-    halo = RADIUS * 16
-    edge = jax.ShapeDtypeStruct((2, halo, inner), BF16)
-    return pl.pallas_call(
-        begin_kernel,
-        out_shape=(jax.ShapeDtypeStruct((1, 256), F32), edge, edge),
-        in_specs=[pl.BlockSpec(memory_space=pltpu.SMEM)] + in_vmem(2) + [pl.BlockSpec(memory_space=pl.ANY)],
-        out_specs=tuple(in_vmem(3)),
+def cut(kv, after):
+    edge = jax.ShapeDtypeStruct((2, RADIUS * 16, kv.shape[2]), BF16)
+    return pl.pallas_call(
+        cut_kernel,
+        out_shape=(edge, edge),
+        in_specs=[pl.BlockSpec(memory_space=pl.ANY)] * 2,
+        out_specs=tuple(in_vmem(2)),
         scratch_shapes=[pltpu.SemaphoreType.DMA((2,))],
         compiler_params=pltpu.CompilerParams(vmem_limit_bytes=8 * 2**20),
-        name="begin",
-    )(label, embed, table, kv)
-
-
-def answer_kernel(asked_ref, table_ref, gate_ref, answer_ref):
-    width = gate_ref.shape[1]
-    row = picked_row(asked_ref[:, 128:129], table_ref[...])
-    part = gate_product(row, asked_ref[:, 0:64], asked_ref[:, 64:128], gate_ref[...])
-    answer_ref[:, 0:width] = part[:1]
-    answer_ref[:, width:] = jnp.concatenate([row[:1], row[:1]], axis=1)
-
-
-def answer(asked, table, gate_weight):
-    return pl.pallas_call(
-        answer_kernel,
-        out_shape=jax.ShapeDtypeStruct((1, gate_weight.shape[1] + 128), F32),
-        in_specs=in_vmem(3),
-        out_specs=pl.BlockSpec(memory_space=pltpu.VMEM),
-        compiler_params=pltpu.CompilerParams(vmem_limit_bytes=8 * 2**20),
-        name="answer",
-    )(asked, table, gate_weight)
-
-
-def two_rows(value):
-    high = value.astype(BF16).astype(F32)
-    ids = lax.broadcasted_iota(jnp.int32, (8, value.shape[1]), 0)
-    return jnp.where(ids == 0, high, jnp.where(ids == 1, value - high, F32(0.0))).astype(BF16)
-
-
-def mix_kernel(own_ref, peer_ref, ask_ref, answered_ref, gate_ref, sent_ref):
-    shard, width = own_ref.shape
-    sent_ref[0:shard, :] = (0.5 * (own_ref[...].astype(F32) + peer_ref[...].astype(F32))).astype(BF16)
-    own_row = jnp.broadcast_to(ask_ref[:, 0:64], (16, 64))
-    part = gate_product(own_row, answered_ref[:, width : width + 64], ask_ref[:, 64:128], gate_ref[...])
-    sent_ref[shard : shard + 8, :] = two_rows(0.5 * (part[:1] + answered_ref[:, 0:width]))
-
-
-def mix(own, peer, ask, answered, gate_weight):
-    shard, width = own.shape
-    return pl.pallas_call(
-        mix_kernel,
-        out_shape=jax.ShapeDtypeStruct((shard + 8, width), BF16),
-        in_specs=in_vmem(5),
-        out_specs=pl.BlockSpec(memory_space=pltpu.VMEM),
-        compiler_params=pltpu.CompilerParams(vmem_limit_bytes=8 * 2**20),
-        name="mix",
-    )(own, peer, ask, answered, gate_weight)
-
-
-def stack_kernel(*refs):
-    parts, out_ref = refs[:4], refs[4]
-    shard = parts[0].shape[0] - 8
-    total = jnp.zeros((8, out_ref.shape[1]), F32)
-    for index, part in enumerate(parts):
-        out_ref[index * shard : (index + 1) * shard, :] = part[0:shard, :]
-        total = total + part[shard : shard + 8, :].astype(F32)
-    out_ref[4 * shard : 4 * shard + 8, :] = two_rows(jnp.sum(total, axis=0, keepdims=True))
-
-
-def stacked(parts):
-    rows, width = parts[0].shape
-    return pl.pallas_call(
-        stack_kernel,
-        out_shape=jax.ShapeDtypeStruct((4 * (rows - 8) + 8, width), BF16),
-        in_specs=in_vmem(4),
-        out_specs=pl.BlockSpec(memory_space=pltpu.VMEM),
-        compiler_params=pltpu.CompilerParams(vmem_limit_bytes=8 * 2**20),
-        name="stack",
-    )(*parts)
-
-
-def edges_kernel(kv_ref, up_ref, down_ref, near_ref, far_ref):
+        name="cut",
+    )(kv, after)
+
+
+def edges_kernel(kv_ref, up_ref, down_ref, after_ref, near_ref, far_ref):
     cols = 16
     core = lax.rem(lax.axis_index("col"), 2)
     count = near_ref.shape[1]
@@ -223,18 +243,18 @@
         far_ref[which] = jnp.dot(pick_far, tall, preferred_element_type=F32).astype(BF16)
 
 
-def edges(kv, up, down):
+def edges(kv, up, down, after):
     inner = kv.shape[2]
     count = (12 + 2 * RADIUS + PAD_ROWS) * EDGE
     edge = jax.ShapeDtypeStruct((2, count, inner), BF16)
     return pl.pallas_call(
         edges_kernel,
         out_shape=(edge, edge),
-        in_specs=in_vmem(3),
+        in_specs=in_vmem(3) + [pl.BlockSpec(memory_space=pl.ANY)],
         out_specs=tuple(in_vmem(2)),
         compiler_params=pltpu.CompilerParams(vmem_limit_bytes=12 * 2**20),
         name="edges",
-    )(kv, up, down)
+    )(kv, up, down, after)
 
 
 def project_kernel(a_ref, *refs):
@@ -243,17 +263,22 @@
     core, place = lax.rem(col, 2), lax.div(col, 2)
     shard, block = 32, 256
     tokens, width = a_ref.shape[0], out_ref.shape[1]
+    odd_place, high_place = place & 1, place >= 2
     for back in range(4):
-        start = pl.multiple_of(lax.rem(row + 4 - back, 4) * block, block)
+        start = pl.multiple_of((row ^ back) * block, block)
         lanes = a_ref[:, pl.ds(start, block)].astype(F32)
-        lanes = pltpu.roll(lanes, block - 64 * place, 1).astype(BF16)
+        first, second = lanes[:, :128], lanes[:, 128:]
+        halves = jnp.where(high_place, second, first), jnp.where(high_place, first, second)
+        halves = [pltpu.roll(half, 64 * odd_place, 1).astype(BF16) for half in halves]
         for step in range(4):
-            at = ((4 - step) % 4) * 64
-            lanes_ref[:, step * block + back * 64 : step * block + (back + 1) * 64] = lanes[:, at : at + 64]
-    total = jnp.zeros((8, width), F32)
+            at = (step % 2) * 64
+            lanes_ref[:, step * block + back * 64 : step * block + (back + 1) * 64] = halves[step // 2][:, at : at + 64]
+    total = jnp.zeros((shard, 128), F32)
     for piece in pieces:
-        total = total + piece[4 * shard : 4 * shard + 8, :].astype(F32)
-    gate = jnp.sum(total, axis=0, keepdims=True)
+        for back in range(4):
+            total = total + piece[back * shard : (back + 1) * shard, width : width + 128].astype(F32)
+    total = total[:16] + total[16:]
+    gate = jnp.concatenate([total[at : at + 1] for at in range(16)], axis=1)
     part_width = 512
     parts = width // part_width
 
@@ -287,7 +312,7 @@
 
 def project(a, pieces):
     tokens, inner = a.shape
-    width = pieces[0].shape[1]
+    width = pieces[0].shape[1] - 128
     return pl.pallas_call(
         project_kernel,
         out_shape=jax.ShapeDtypeStruct((tokens, width), BF16),
@@ -313,61 +338,50 @@
     return jnp.where(positions < half_width, jnp.cos(angle), jnp.sin(angle))[None]
 
 
-def body(distance, queries, keyvals, out_weight, gate_weight, class_table, label, step):
+def local(queries, keyvals, out_weight, gate_weight, class_table, labels, timesteps, round_index):
     dp_count, row_count, col_count = (lax.axis_size(a) for a in ("dp", "row", "col"))
-    ahead = [(i, (i + distance) % dp_count) for i in range(dp_count)]
-    behind = [(j, i) for i, j in ahead]
-    tile_rows, tile_cols, inner = queries.shape
+    bit_count = dp_count.bit_length() - 1
+    tile_rows, tile_cols, inner = queries.shape[1:]
     kv = keyvals.reshape(2, -1, inner)
-
-    embed = time_embed(step[0], gate_weight.shape[0], gate_weight.shape[1])
-    ask, low, high = begin(label, embed, class_table, kv)
-    asked = lax.ppermute(ask, "dp", behind)
-    peer_out = lax.ppermute(out_weight, "dp", ahead)
+    out_weight, gate_weight = out_weight[0], gate_weight[0]
+    table = class_table[0].T
+    power = round_index[0] % bit_count
+
+    def shifted(value, sign):
+        def branch(distance):
+            pairs = [(i, (i + sign * distance) % dp_count) for i in range(dp_count)]
+            return lambda array: lax.ppermute(array, "dp", pairs)
+
+        return lax.switch(power, [branch(2**bit) for bit in range(bit_count)], value)
+
+    embed = time_embed(timesteps[0], gate_weight.shape[0], gate_weight.shape[1])
+    ask = begin(labels, embed, table)
+    asked = shifted(ask, -1)
+    peer = shifted(answer(asked, table, gate_weight, out_weight), 1)
+
+    sent = mix(out_weight, peer, ask, gate_weight)
+    got = [sent] + [
+        lax.ppermute(sent, "row", [(i, i ^ k) for i in range(row_count)]) for k in range(1, row_count)
+    ]
+    stack = stacked(got)
+    places = [stack] + [
+        lax.ppermute(stack, "col", [(i, i ^ (2 * k)) for i in range(col_count)])
+        for k in range(1, col_count // 2)
+    ]
+    near_pairs = [(i, i ^ 1) for i in range(col_count)]
+    siblings = [lax.ppermute(part, "col", near_pairs) for part in places]
+
+    low, high = cut(kv, got[1])
     up_pairs = [(i, i + 1) for i in range(row_count - 1)]
     up = lax.ppermute(low, "row", up_pairs)
     down = lax.ppermute(high, "row", [(j, i) for i, j in up_pairs])
-    answered = lax.ppermute(answer(asked, class_table, gate_weight), "dp", ahead)
-    near_pairs = [(i, i ^ 1) for i in range(col_count)]
     far_pairs = [(i, i + 1) for i in range(1, col_count - 1, 2)]
-    near, far = edges(kv, up, down)
+    near, far = edges(kv, up, down, places[1])
     near = lax.ppermute(near, "col", near_pairs)
     far = lax.ppermute(far, "col", far_pairs + [(j, i) for i, j in far_pairs])
-
-    sent = mix(out_weight, peer_out, ask, answered, gate_weight)
-    sent, near, far = lax.optimization_barrier((sent, near, far))
-    got = [sent] + [
-        lax.ppermute(sent, "row", [(i, (i + k) % row_count) for i in range(row_count)])
-        for k in range(1, row_count)
-    ]
     attended = attend(queries.reshape(-1, inner), kv, up, down, near, far)
-    stack, attended = lax.optimization_barrier((stacked(got), attended))
-    places = [stack] + [
-        lax.ppermute(stack, "col", [(i, (i + 2 * k) % col_count) for i in range(col_count)])
-        for k in range(1, col_count // 2)
-    ]
-    siblings = [lax.ppermute(part, "col", near_pairs) for part in places]
     result = project(attended, places + siblings)
     return result.reshape(1, tile_rows, tile_cols, -1)
-
-
-def local(queries, keyvals, out_weight, gate_weight, class_table, labels, timesteps, round_index):
-    bit_count = lax.axis_size("dp").bit_length() - 1
-
-    def branch(power):
-        return lambda *args: body(2**power, *args)
-
-    return lax.switch(
-        round_index[0] % bit_count,
-        [branch(power) for power in range(bit_count)],
-        queries[0],
-        keyvals[0],
-        out_weight[0],
-        gate_weight[0],
-        class_table[0],
-        labels,
-        timesteps,
-    )
 
 
 def solution(mesh):

time: 97.8 us -> 113 us (1.16)
  starting transfers between devices: 59 us -> 70.8 us
  waiting for transfers between devices: 27.3 us -> 29.8 us
  between operations: 0.76 us -> 2.21 us
  loops' own time: 1.21 us -> 0.03 us
    ppermute x17 -> x16, starting transfers between devices: 59 us -> 70.8 us  [the longest x2 18.9 us: branch(): return lambda array: lax.ppermute(array, 'dp', pairs)]
    ppermute x17 -> x16, waiting for transfers between devices: 27.3 us -> 29.8 us  [the longest x2 10 us: branch(): return lambda array: lax.ppermute(array, 'dp', pairs)]
    another operation x1 -> x2, loops' own time: 1.21 us -> 0.03 us  [shifted(): lax.switch(power, [branch(2 ** bit) for bit in range(bit_count)], value)]
    unnamed x7 -> x16, local copies, waits for them, and re-layouts: 2.02 us -> 2.78 us
    pallas_call x5 -> x6, Pallas kernels: 3.09 us -> 3.49 us  [the longest x1 1.22 us: mix(): pl.pallas_call(mix_kernel, out_shape=jax.ShapeDtypeStruct((shard, width +...]
  transfers between devices with their start and end apart: 17 -> 16, of which waited for: 8 -> 9; matrix products, arithmetic and copies ran while one was open for 0% -> 0% of each run, Pallas kernels for 2% -> 2%
where the time goes in v3:
time: 113 us
  starting transfers between devices  70.8 us (63%)
  waiting for transfers between devices  29.8 us (26%)
  Pallas kernels  7.14 us (6%)
  local copies, waits for them, and re-layouts  2.78 us (2%)
  between operations  2.21 us (2%)
    ppermute x2, starting transfers between devices, branch(): return lambda array: lax.ppermute(array, 'dp', pairs)  18.9 us
    ppermute x3, starting transfers between devices, local(): lax.ppermute(sent, 'row', [(i, i ^ k) for i in range(row_count)])  18.1 us
    ppermute x4, starting transfers between devices, local(): siblings = [lax.ppermute(part, 'col', near_pairs) for part in places]  12.2 us
    ppermute x2, waiting for transfers between devices, branch(): return lambda array: lax.ppermute(array, 'dp', pairs)  10 us
    ppermute x3, starting transfers between devices, local(): lax.ppermute(stack, 'col', [(i, i ^ 2 * k) for i in range(col_count)])  9.65 us
    ppermute x3, waiting for transfers between devices, local(): lax.ppermute(sent, 'row', [(i, i ^ k) for i in range(row_count)])  6.59 us
    ppermute x1, waiting for transfers between devices, local(): far = lax.ppermute(far, 'col', far_pairs + [(j, i) for i, j in far_pairs])  6.47 us
    ppermute x1, starting transfers between devices, local(): near = lax.ppermute(near, 'col', near_pairs)  4.63 us
  transfers between devices with their start and end apart: 16, of which 9 were waited for; matrix products, arithmetic and copies ran while one was open for 0% of the time, Pallas kernels for 2%

profile of v3, /device:TPU:1, one launch (start us, length us, event | category | flops | bytes accessed | tf_op | source)
XLA Modules:
  0.0 112.8 jit_solution(6439894221677207907)
XLA Ops:
  2.0 0.1 compare_select_fusion.2.embed_ref
  2.0 0.0 copy-start.3
  2.0 0.9 copy-done.3
  2.9 0.1 begin.1.ask_ref
  3.0 16.2 %conditional.2 = (f32[1,256]{1,0:T(1,128)}) conditional(s32[]{:T(128)} %clamp.4, f32[1,256]{1,0:T(1,128)S(1)} %begin.1.ask_ref, f32[1,256]{1,0:T(1,128)S(1)} %begin.1.ask_ref, f32[1,256]{1,0:T(1,128)S(1)} %begin.1.ask_ref, f32[1,256]{1,0:T(1,128)S(1)} %begin.1.ask_ref), branch_computations={%region_0.1_spmd, %region_1.2_spmd, %region_2.3_spmd, %region_3.4_... | conditional | bytes 4144 | solution.py:355
  3.0 15.5 %collective-permute-start = (f32[1,256]{1,0:T(1,128)S(1)}, f32[1,256]{1,0:T(1,128)}, u32[]{:S(2)}, u32[]{:S(2)}) collective-permute-start(f32[1,256]{1,0:T(1,128)S(1)} %param), channel_id=1, source_target_pairs={{0,480},{32,0},{64,32},{96,64},{128,96},{160,128},{192,160},{224,1... | collective-permute-start | bytes 3080 | tf_op jit(solution)/shard_map/cond/branch_0_fun/ppermute | solution.py:353
  18.6 0.7 collective-permute-done
  19.3 0.0 copy-done.4
  19.3 0.9 copy-done.1
  20.2 0.9 copy-done.5
  21.1 1.1 %answer.1 = bf16[32,2304]{1,0:T(8,128)(2,1)S(1)} custom-call(f32[1,256]{1,0:T(1,128)} %get-tuple-element.31.asked_ref, bf16[64,1000]{1,0:T(8,128)(2,1)S(1)} %bitcast.19, bf16[64,2048]{1,0:T(8,128)(2,1)S(1)} %bitcast.16, bf16[32,2048]{1,0:T(8,128)(2,1)S(1)} %bitcast.20), custom_call_target="tpu_custom_call" | custom-call | tf_op jit(solution)/shard_map/answer/pallas_call | solution.py:151
  22.3 12.7 %conditional.3 = (bf16[32,2304]{1,0:T(8,128)(2,1)}) conditional(s32[]{:T(128)} %clamp.4, bf16[32,2304]{1,0:T(8,128)(2,1)S(1)} %answer.1, bf16[32,2304]{1,0:T(8,128)(2,1)S(1)} %answer.1, bf16[32,2304]{1,0:T(8,128)(2,1)S(1)} %answer.1, bf16[32,2304]{1,0:T(8,128)(2,1)S(1)} %answer.1), branch_computations={%region_4.5_spmd, %region_5.6_spmd, %region_6.7_spmd, %region_7.8_... | conditional | bytes 589872 | solution.py:355
  22.3 3.3 %collective-permute-start.4 = (bf16[32,2304]{1,0:T(8,128)(2,1)S(1)}, bf16[32,2304]{1,0:T(8,128)(2,1)}, u32[]{:S(2)}, u32[]{:S(2)}) collective-permute-start(bf16[32,2304]{1,0:T(8,128)(2,1)S(1)} %param.4), channel_id=1, source_target_pairs={{0,32},{32,64},{64,96},{96,128},{128,160},{160,192},{192,224},{224... | collective-permute-start | bytes 442376 | tf_op jit(solution)/shard_map/cond/branch_0_fun/ppermute | solution.py:353
  25.6 9.3 %collective-permute-done.4 = bf16[32,2304]{1,0:T(8,128)(2,1)} collective-permute-done((bf16[32,2304]{1,0:T(8,128)(2,1)S(1)}, bf16[32,2304]{1,0:T(8,128)(2,1)}, u32[]{:S(2)}, u32[]{:S(2)}) %collective-permute-start.4) | collective-permute-done | bytes 147488 | tf_op jit(solution)/shard_map/cond/branch_0_fun/ppermute | solution.py:353
  35.0 1.2 %mix.1.refs_0_ = bf16[32,2176]{1,0:T(8,128)(2,1)S(1)} custom-call(bf16[32,2048]{1,0:T(8,128)(2,1)S(1)} %bitcast.21, bf16[32,2304]{1,0:T(8,128)(2,1)} %get-tuple-element.32.peer_ref, f32[1,256]{1,0:T(1,128)S(1)} %begin.1.ask_ref, bf16[64,2048]{1,0:T(8,128)(2,1)S(1)} %bitcast.17), custom_call_target="tpu_custom_call" | custom-call | tf_op jit(solution)/shard_map/mix/pallas_call | solution.py:174
  36.2 11.9 %collective-permute-start.11 = (bf16[32,2176]{1,0:T(8,128)(2,1)S(1)}, bf16[32,2176]{1,0:T(8,128)(2,1)S(1)}, u32[]{:S(2)}, u32[]{:S(2)}) collective-permute-start(bf16[32,2176]{1,0:T(8,128)(2,1)S(1)} %mix.1.refs_0_), channel_id=1, source_target_pairs={{0,16},{8,24},{16,0},{24,8},{1,17},{9,25},{17,1},{25,9},{2,18},{10... | collective-permute-start | bytes 417800 | tf_op jit(solution)/shard_map/ppermute | solution.py:364
  48.1 4.0 %collective-permute-start.12 = (bf16[32,2176]{1,0:T(8,128)(2,1)S(1)}, bf16[32,2176]{1,0:T(8,128)(2,1)S(1)}, u32[]{:S(2)}, u32[]{:S(2)}) collective-permute-start(bf16[32,2176]{1,0:T(8,128)(2,1)S(1)} %mix.1.refs_0_), channel_id=1, source_target_pairs={{0,24},{8,16},{16,8},{24,0},{1,25},{9,17},{17,9},{25,1},{2,26},{10... | collective-permute-start | bytes 417800 | tf_op jit(solution)/shard_map/ppermute | solution.py:364
  52.1 2.2 %collective-permute-start.8 = (bf16[32,2176]{1,0:T(8,128)(2,1)S(1)}, bf16[32,2176]{1,0:T(8,128)(2,1)S(1)}, u32[]{:S(2)}, u32[]{:S(2)}) collective-permute-start(bf16[32,2176]{1,0:T(8,128)(2,1)S(1)} %mix.1.refs_0_), channel_id=1, source_target_pairs={{0,8},{8,0},{16,24},{24,16},{1,9},{9,1},{17,25},{25,17},{2,10},{10... | collective-permute-start | bytes 417800 | tf_op jit(solution)/shard_map/ppermute | solution.py:364
  54.3 0.0 collective-permute-done.11.refs_2_
  54.3 1.4 %collective-permute-done.12.refs_3_ = bf16[32,2176]{1,0:T(8,128)(2,1)S(1)} collective-permute-done((bf16[32,2176]{1,0:T(8,128)(2,1)S(1)}, bf16[32,2176]{1,0:T(8,128)(2,1)S(1)}, u32[]{:S(2)}, u32[]{:S(2)}) %collective-permute-start.12) | collective-permute-done | bytes 139296 | tf_op jit(solution)/shard_map/ppermute | solution.py:364
  55.7 5.2 %collective-permute-done.8.after_ref.refs_1_ = bf16[32,2176]{1,0:T(8,128)(2,1)S(1)} collective-permute-done((bf16[32,2176]{1,0:T(8,128)(2,1)S(1)}, bf16[32,2176]{1,0:T(8,128)(2,1)S(1)}, u32[]{:S(2)}, u32[]{:S(2)}) %collective-permute-start.8) | collective-permute-done | bytes 139296 | tf_op jit(solution)/shard_map/ppermute | solution.py:364
  61.0 3.2 %collective-permute-start.13 = (bf16[128,2176]{1,0:T(8,128)(2,1)S(1)}, bf16[128,2176]{1,0:T(8,128)(2,1)S(1)}, u32[]{:S(2)}, u32[]{:S(2)}) collective-permute-start(bf16[128,2176]{1,0:T(8,128)(2,1)S(1)} %stack.1.refs_0_), channel_id=1, source_target_pairs={{0,2},{1,3},{2,0},{3,1},{4,6},{5,7},{6,4},{7,5},{8,10},{9,11},{10,... | collective-permute-start | bytes 1671176 | tf_op jit(solution)/shard_map/ppermute | solution.py:368
  64.2 4.5 %collective-permute-start.16 = (bf16[128,2176]{1,0:T(8,128)(2,1)S(1)}, bf16[128,2176]{1,0:T(8,128)(2,1)S(1)}, u32[]{:S(2)}, u32[]{:S(2)}) collective-permute-start(bf16[128,2176]{1,0:T(8,128)(2,1)S(1)} %stack.1.refs_0_), channel_id=1, source_target_pairs={{0,4},{1,5},{2,6},{3,7},{4,0},{5,1},{6,2},{7,3},{8,12},{9,13},{10,... | collective-permute-start | bytes 1671176 | tf_op jit(solution)/shard_map/ppermute | solution.py:368
  68.7 1.9 %collective-permute-start.17 = (bf16[128,2176]{1,0:T(8,128)(2,1)S(1)}, bf16[128,2176]{1,0:T(8,128)(2,1)S(1)}, u32[]{:S(2)}, u32[]{:S(2)}) collective-permute-start(bf16[128,2176]{1,0:T(8,128)(2,1)S(1)} %stack.1.refs_0_), channel_id=1, source_target_pairs={{0,6},{1,7},{2,4},{3,5},{4,2},{5,3},{6,0},{7,1},{8,14},{9,15},{10,... | collective-permute-start | bytes 1671176 | tf_op jit(solution)/shard_map/ppermute | solution.py:368
  70.7 0.3 cut.1
  71.0 1.3 %collective-permute-start.10 = (bf16[2,48,1024]{2,1,0:T(8,128)(2,1)S(1)}, bf16[2,48,1024]{2,1,0:T(8,128)(2,1)S(1)}, u32[]{:S(2)}, u32[]{:S(2)}) collective-permute-start(bf16[2,48,1024]{2,1,0:T(8,128)(2,1)S(1)} %get-tuple-element.28), channel_id=1, source_target_pairs={{8,0},{16,8},{24,16},{9,1},{17,9},{25,17},{10,2},{18,10},{26,18},{... | collective-permute-start | bytes 589832 | tf_op jit(solution)/shard_map/ppermute | solution.py:377
  72.3 0.0 copy-start.7
  72.3 4.1 %collective-permute-start.9 = (bf16[2,48,1024]{2,1,0:T(8,128)(2,1)S(1)}, bf16[2,48,1024]{2,1,0:T(8,128)(2,1)S(1)}, u32[]{:S(2)}, u32[]{:S(2)}) collective-permute-start(bf16[2,48,1024]{2,1,0:T(8,128)(2,1)S(1)} %get-tuple-element.27), channel_id=1, source_target_pairs={{0,8},{8,16},{16,24},{1,9},{9,17},{17,25},{2,10},{10,18},{18,26},{... | collective-permute-start | bytes 589832 | tf_op jit(solution)/shard_map/ppermute | solution.py:376
  76.4 1.3 %collective-permute-done.10.down_ref = bf16[2,48,1024]{2,1,0:T(8,128)(2,1)S(1)} collective-permute-done((bf16[2,48,1024]{2,1,0:T(8,128)(2,1)S(1)}, bf16[2,48,1024]{2,1,0:T(8,128)(2,1)S(1)}, u32[]{:S(2)}, u32[]{:S(2)}) %collective-permute-start.10) | collective-permute-done | bytes 196640 | tf_op jit(solution)/shard_map/ppermute | solution.py:377
  77.7 1.3 %collective-permute-done.9.up_ref = bf16[2,48,1024]{2,1,0:T(8,128)(2,1)S(1)} collective-permute-done((bf16[2,48,1024]{2,1,0:T(8,128)(2,1)S(1)}, bf16[2,48,1024]{2,1,0:T(8,128)(2,1)S(1)}, u32[]{:S(2)}, u32[]{:S(2)}) %collective-permute-start.9) | collective-permute-done | bytes 196640 | tf_op jit(solution)/shard_map/ppermute | solution.py:376
  79.0 0.0 collective-permute-done.13.after_ref.refs_1_
  79.0 0.7 edges.1
  79.7 4.6 %collective-permute-start.14 = (bf16[2,80,1024]{2,1,0:T(8,128)(2,1)S(1)}, bf16[2,80,1024]{2,1,0:T(8,128)(2,1)S(1)}, u32[]{:S(2)}, u32[]{:S(2)}) collective-permute-start(bf16[2,80,1024]{2,1,0:T(8,128)(2,1)S(1)} %get-tuple-element.29), channel_id=1, source_target_pairs={{0,1},{1,0},{2,3},{3,2},{4,5},{5,4},{6,7},{7,6},{8,9},{9,8},{10,11... | collective-permute-start | bytes 983048 | tf_op jit(solution)/shard_map/ppermute | solution.py:380
  84.3 1.9 %collective-permute-start.18 = (bf16[128,2176]{1,0:T(8,128)(2,1)S(1)}, bf16[128,2176]{1,0:T(8,128)(2,1)S(1)}, u32[]{:S(2)}, u32[]{:S(2)}) collective-permute-start(bf16[128,2176]{1,0:T(8,128)(2,1)S(1)} %stack.1.refs_0_), channel_id=1, source_target_pairs={{0,1},{1,0},{2,3},{3,2},{4,5},{5,4},{6,7},{7,6},{8,9},{9,8},{10,11... | collective-permute-start | bytes 1671176 | tf_op jit(solution)/shard_map/ppermute | solution.py:372
  86.3 2.4 %collective-permute-start.19 = (bf16[128,2176]{1,0:T(8,128)(2,1)S(1)}, bf16[128,2176]{1,0:T(8,128)(2,1)S(1)}, u32[]{:S(2)}, u32[]{:S(2)}) collective-permute-start(bf16[128,2176]{1,0:T(8,128)(2,1)S(1)} %collective-permute-done.13.after_ref.refs_1_), channel_id=1, source_target_pairs={{0,1},{1,0},{2,3},{3,2},{4,5},{5,4},{6,7},{7,6},{8,9},{9,8},{10,11... | collective-permute-start | bytes 1671176 | tf_op jit(solution)/shard_map/ppermute | solution.py:372
  88.7 1.9 %collective-permute-done.16.refs_2_ = bf16[128,2176]{1,0:T(8,128)(2,1)S(1)} collective-permute-done((bf16[128,2176]{1,0:T(8,128)(2,1)S(1)}, bf16[128,2176]{1,0:T(8,128)(2,1)S(1)}, u32[]{:S(2)}, u32[]{:S(2)}) %collective-permute-start.16) | collective-permute-done | bytes 557088 | tf_op jit(solution)/shard_map/ppermute | solution.py:368
  90.6 3.7 %collective-permute-start.20 = (bf16[128,2176]{1,0:T(8,128)(2,1)S(1)}, bf16[128,2176]{1,0:T(8,128)(2,1)S(1)}, u32[]{:S(2)}, u32[]{:S(2)}) collective-permute-start(bf16[128,2176]{1,0:T(8,128)(2,1)S(1)} %collective-permute-done.16.refs_2_), channel_id=1, source_target_pairs={{0,1},{1,0},{2,3},{3,2},{4,5},{5,4},{6,7},{7,6},{8,9},{9,8},{10,11... | collective-permute-start | bytes 1671176 | tf_op jit(solution)/shard_map/ppermute | solution.py:372
  94.3 2.2 %collective-permute-done.17.refs_3_ = bf16[128,2176]{1,0:T(8,128)(2,1)S(1)} collective-permute-done((bf16[128,2176]{1,0:T(8,128)(2,1)S(1)}, bf16[128,2176]{1,0:T(8,128)(2,1)S(1)}, u32[]{:S(2)}, u32[]{:S(2)}) %collective-permute-start.17) | collective-permute-done | bytes 557088 | tf_op jit(solution)/shard_map/ppermute | solution.py:368
  96.5 4.2 %collective-permute-start.21 = (bf16[128,2176]{1,0:T(8,128)(2,1)S(1)}, bf16[128,2176]{1,0:T(8,128)(2,1)S(1)}, u32[]{:S(2)}, u32[]{:S(2)}) collective-permute-start(bf16[128,2176]{1,0:T(8,128)(2,1)S(1)} %collective-permute-done.17.refs_3_), channel_id=1, source_target_pairs={{0,1},{1,0},{2,3},{3,2},{4,5},{5,4},{6,7},{7,6},{8,9},{9,8},{10,11... | collective-permute-start | bytes 1671176 | tf_op jit(solution)/shard_map/ppermute | solution.py:372
  100.7 0.0 collective-permute-done.14.near_ref
  100.7 1.9 %collective-permute-start.15 = (bf16[2,80,1024]{2,1,0:T(8,128)(2,1)S(1)}, bf16[2,80,1024]{2,1,0:T(8,128)(2,1)S(1)}, u32[]{:S(2)}, u32[]{:S(2)}) collective-permute-start(bf16[2,80,1024]{2,1,0:T(8,128)(2,1)S(1)} %get-tuple-element.30), channel_id=1, source_target_pairs={{1,2},{3,4},{5,6},{2,1},{4,3},{6,5},{9,10},{11,12},{13,14},{10,9},... | collective-permute-start | bytes 983048 | tf_op jit(solution)/shard_map/ppermute | solution.py:381
  102.7 6.5 %collective-permute-done.15.far_ref = bf16[2,80,1024]{2,1,0:T(8,128)(2,1)S(1)} collective-permute-done((bf16[2,80,1024]{2,1,0:T(8,128)(2,1)S(1)}, bf16[2,80,1024]{2,1,0:T(8,128)(2,1)S(1)}, u32[]{:S(2)}, u32[]{:S(2)}) %collective-permute-start.15) | collective-permute-done | bytes 327712 | tf_op jit(solution)/shard_map/ppermute | solution.py:381
  109.1 1.4 %attend.1.a_ref = bf16[192,1024]{1,0:T(8,128)(2,1)S(1)} custom-call(bf16[192,1024]{1,0:T(8,128)(2,1)S(1)} %bitcast.22, bf16[2,192,1024]{2,1,0:T(8,128)(2,1)S(1)} %bitcast.15, bf16[2,48,1024]{2,1,0:T(8,128)(2,1)S(1)} %collective-permute-done.9.up_ref, bf16[2,48,1024]{2,1,0:T(8,128)(2,1)S(1)} %collective-permute-done.10.down_ref, ...), custom_call_target="tpu_custom_call" | custom-call | flops 1200000000 | bytes 3000000 | tf_op jit(solution)/shard_map/attend/pallas_call | solution.py:83
  110.5 0.0 collective-permute-done.18.refs_4_
  110.5 0.0 collective-permute-done.19.refs_5_
  110.5 0.0 collective-permute-done.20.refs_6_
  110.6 0.0 collective-permute-done.21.refs_7_
  110.6 2.3 %project.1 = bf16[192,2048]{1,0:T(8,128)(2,1)} custom-call(bf16[192,1024]{1,0:T(8,128)(2,1)S(1)} %attend.1.a_ref, bf16[128,2176]{1,0:T(8,128)(2,1)S(1)} %stack.1.refs_0_, bf16[128,2176]{1,0:T(8,128)(2,1)S(1)} %collective-permute-done.13.after_ref.refs_1_, bf16[128,2176]{1,0:T(8,128)(2,1)S(1)} %collective-permute-done.16.refs_2_, ...), custom_call_target="tpu_custom_call" | custom-call | flops 810000000 | bytes 6000000 | tf_op jit(solution)/shard_map/project/pallas_call | solution.py:316
  (11 shorter events, 0.1 us)
Async XLA Ops:
  2.0 0.9 copy-start.3
  2.9 16.3 %copy-start.4 = (bf16[1,1000,64]{1,2,0:T(8,128)(2,1)S(1)}, bf16[1,1000,64]{1,2,0:T(8,128)(2,1)}, u32[]{:S(2)}) copy-start(bf16[1,1000,64]{1,2,0:T(8,128)(2,1)} %param.20) | copy-start | bytes 384004
  3.0 16.2 %collective-permute-start = (f32[1,256]{1,0:T(1,128)S(1)}, f32[1,256]{1,0:T(1,128)}, u32[]{:S(2)}, u32[]{:S(2)}) collective-permute-start(f32[1,256]{1,0:T(1,128)S(1)} %param), channel_id=1, source_target_pairs={{0,480},{32,0},{64,32},{96,64},{128,96},{160,128},{192,160},{224,1... | collective-permute-start | bytes 3080 | tf_op jit(solution)/shard_map/cond/branch_0_fun/ppermute | solution.py:353
  19.3 1.0 copy-start.1
  20.2 0.9 copy-start.5
  21.1 13.8 %copy-start.2 = (bf16[1,64,2048]{2,1,0:T(8,128)(2,1)S(1)}, bf16[1,64,2048]{2,1,0:T(8,128)(2,1)}, u32[]{:S(2)}) copy-start(bf16[1,64,2048]{2,1,0:T(8,128)(2,1)} %param.19) | copy-start | bytes 786436
  21.1 13.8 %copy-start.6 = (bf16[1,32,2048]{2,1,0:T(8,128)(2,1)S(1)}, bf16[1,32,2048]{2,1,0:T(8,128)(2,1)}, u32[]{:S(2)}) copy-start(bf16[1,32,2048]{2,1,0:T(8,128)(2,1)} %param.18) | copy-start | bytes 393220
  22.3 12.7 %collective-permute-start.4 = (bf16[32,2304]{1,0:T(8,128)(2,1)S(1)}, bf16[32,2304]{1,0:T(8,128)(2,1)}, u32[]{:S(2)}, u32[]{:S(2)}) collective-permute-start(bf16[32,2304]{1,0:T(8,128)(2,1)S(1)} %param.4), channel_id=1, source_target_pairs={{0,32},{32,64},{64,96},{96,128},{128,160},{160,192},{192,224},{224... | collective-permute-start | bytes 442376 | tf_op jit(solution)/shard_map/cond/branch_0_fun/ppermute | solution.py:353
  35.0 35.7 %copy-start = (bf16[1,2,12,16,1024]{4,3,2,1,0:T(8,128)(2,1)S(1)}, bf16[1,2,12,16,1024]{4,3,2,1,0:T(8,128)(2,1)}, u32[]{:S(2)}) copy-start(bf16[1,2,12,16,1024]{4,3,2,1,0:T(8,128)(2,1)} %param.17) | copy-start | bytes 2359300
  36.2 18.1 %collective-permute-start.11 = (bf16[32,2176]{1,0:T(8,128)(2,1)S(1)}, bf16[32,2176]{1,0:T(8,128)(2,1)S(1)}, u32[]{:S(2)}, u32[]{:S(2)}) collective-permute-start(bf16[32,2176]{1,0:T(8,128)(2,1)S(1)} %mix.1.refs_0_), channel_id=1, source_target_pairs={{0,16},{8,24},{16,0},{24,8},{1,17},{9,25},{17,1},{25,9},{2,18},{10... | collective-permute-start | bytes 417800 | tf_op jit(solution)/shard_map/ppermute | solution.py:364
  48.1 7.6 %collective-permute-start.12 = (bf16[32,2176]{1,0:T(8,128)(2,1)S(1)}, bf16[32,2176]{1,0:T(8,128)(2,1)S(1)}, u32[]{:S(2)}, u32[]{:S(2)}) collective-permute-start(bf16[32,2176]{1,0:T(8,128)(2,1)S(1)} %mix.1.refs_0_), channel_id=1, source_target_pairs={{0,24},{8,16},{16,8},{24,0},{1,25},{9,17},{17,9},{25,1},{2,26},{10... | collective-permute-start | bytes 417800 | tf_op jit(solution)/shard_map/ppermute | solution.py:364
  52.1 8.8 %collective-permute-start.8 = (bf16[32,2176]{1,0:T(8,128)(2,1)S(1)}, bf16[32,2176]{1,0:T(8,128)(2,1)S(1)}, u32[]{:S(2)}, u32[]{:S(2)}) collective-permute-start(bf16[32,2176]{1,0:T(8,128)(2,1)S(1)} %mix.1.refs_0_), channel_id=1, source_target_pairs={{0,8},{8,0},{16,24},{24,16},{1,9},{9,1},{17,25},{25,17},{2,10},{10... | collective-permute-start | bytes 417800 | tf_op jit(solution)/shard_map/ppermute | solution.py:364
  61.0 18.0 %collective-permute-start.13 = (bf16[128,2176]{1,0:T(8,128)(2,1)S(1)}, bf16[128,2176]{1,0:T(8,128)(2,1)S(1)}, u32[]{:S(2)}, u32[]{:S(2)}) collective-permute-start(bf16[128,2176]{1,0:T(8,128)(2,1)S(1)} %stack.1.refs_0_), channel_id=1, source_target_pairs={{0,2},{1,3},{2,0},{3,1},{4,6},{5,7},{6,4},{7,5},{8,10},{9,11},{10,... | collective-permute-start | bytes 1671176 | tf_op jit(solution)/shard_map/ppermute | solution.py:368
  64.2 26.4 %collective-permute-start.16 = (bf16[128,2176]{1,0:T(8,128)(2,1)S(1)}, bf16[128,2176]{1,0:T(8,128)(2,1)S(1)}, u32[]{:S(2)}, u32[]{:S(2)}) collective-permute-start(bf16[128,2176]{1,0:T(8,128)(2,1)S(1)} %stack.1.refs_0_), channel_id=1, source_target_pairs={{0,4},{1,5},{2,6},{3,7},{4,0},{5,1},{6,2},{7,3},{8,12},{9,13},{10,... | collective-permute-start | bytes 1671176 | tf_op jit(solution)/shard_map/ppermute | solution.py:368
  68.7 27.8 %collective-permute-start.17 = (bf16[128,2176]{1,0:T(8,128)(2,1)S(1)}, bf16[128,2176]{1,0:T(8,128)(2,1)S(1)}, u32[]{:S(2)}, u32[]{:S(2)}) collective-permute-start(bf16[128,2176]{1,0:T(8,128)(2,1)S(1)} %stack.1.refs_0_), channel_id=1, source_target_pairs={{0,6},{1,7},{2,4},{3,5},{4,2},{5,3},{6,0},{7,1},{8,14},{9,15},{10,... | collective-permute-start | bytes 1671176 | tf_op jit(solution)/shard_map/ppermute | solution.py:368
  71.0 6.7 %collective-permute-start.10 = (bf16[2,48,1024]{2,1,0:T(8,128)(2,1)S(1)}, bf16[2,48,1024]{2,1,0:T(8,128)(2,1)S(1)}, u32[]{:S(2)}, u32[]{:S(2)}) collective-permute-start(bf16[2,48,1024]{2,1,0:T(8,128)(2,1)S(1)} %get-tuple-element.28), channel_id=1, source_target_pairs={{8,0},{16,8},{24,16},{9,1},{17,9},{25,17},{10,2},{18,10},{26,18},{... | collective-permute-start | bytes 589832 | tf_op jit(solution)/shard_map/ppermute | solution.py:377
  72.3 36.9 %copy-start.7 = (bf16[1,12,16,1024]{3,2,1,0:T(8,128)(2,1)S(1)}, bf16[1,12,16,1024]{3,2,1,0:T(8,128)(2,1)}, u32[]{:S(2)}) copy-start(bf16[1,12,16,1024]{3,2,1,0:T(8,128)(2,1)} %param.16) | copy-start | bytes 1179652
  72.3 6.7 %collective-permute-start.9 = (bf16[2,48,1024]{2,1,0:T(8,128)(2,1)S(1)}, bf16[2,48,1024]{2,1,0:T(8,128)(2,1)S(1)}, u32[]{:S(2)}, u32[]{:S(2)}) collective-permute-start(bf16[2,48,1024]{2,1,0:T(8,128)(2,1)S(1)} %get-tuple-element.27), channel_id=1, source_target_pairs={{0,8},{8,16},{16,24},{1,9},{9,17},{17,25},{2,10},{10,18},{18,26},{... | collective-permute-start | bytes 589832 | tf_op jit(solution)/shard_map/ppermute | solution.py:376
  79.7 21.0 %collective-permute-start.14 = (bf16[2,80,1024]{2,1,0:T(8,128)(2,1)S(1)}, bf16[2,80,1024]{2,1,0:T(8,128)(2,1)S(1)}, u32[]{:S(2)}, u32[]{:S(2)}) collective-permute-start(bf16[2,80,1024]{2,1,0:T(8,128)(2,1)S(1)} %get-tuple-element.29), channel_id=1, source_target_pairs={{0,1},{1,0},{2,3},{3,2},{4,5},{5,4},{6,7},{7,6},{8,9},{9,8},{10,11... | collective-permute-start | bytes 983048 | tf_op jit(solution)/shard_map/ppermute | solution.py:380
  84.3 26.2 %collective-permute-start.18 = (bf16[128,2176]{1,0:T(8,128)(2,1)S(1)}, bf16[128,2176]{1,0:T(8,128)(2,1)S(1)}, u32[]{:S(2)}, u32[]{:S(2)}) collective-permute-start(bf16[128,2176]{1,0:T(8,128)(2,1)S(1)} %stack.1.refs_0_), channel_id=1, source_target_pairs={{0,1},{1,0},{2,3},{3,2},{4,5},{5,4},{6,7},{7,6},{8,9},{9,8},{10,11... | collective-permute-start | bytes 1671176 | tf_op jit(solution)/shard_map/ppermute | solution.py:372
  86.3 24.3 %collective-permute-start.19 = (bf16[128,2176]{1,0:T(8,128)(2,1)S(1)}, bf16[128,2176]{1,0:T(8,128)(2,1)S(1)}, u32[]{:S(2)}, u32[]{:S(2)}) collective-permute-start(bf16[128,2176]{1,0:T(8,128)(2,1)S(1)} %collective-permute-done.13.after_ref.refs_1_), channel_id=1, source_target_pairs={{0,1},{1,0},{2,3},{3,2},{4,5},{5,4},{6,7},{7,6},{8,9},{9,8},{10,11... | collective-permute-start | bytes 1671176 | tf_op jit(solution)/shard_map/ppermute | solution.py:372
  90.6 19.9 %collective-permute-start.20 = (bf16[128,2176]{1,0:T(8,128)(2,1)S(1)}, bf16[128,2176]{1,0:T(8,128)(2,1)S(1)}, u32[]{:S(2)}, u32[]{:S(2)}) collective-permute-start(bf16[128,2176]{1,0:T(8,128)(2,1)S(1)} %collective-permute-done.16.refs_2_), channel_id=1, source_target_pairs={{0,1},{1,0},{2,3},{3,2},{4,5},{5,4},{6,7},{7,6},{8,9},{9,8},{10,11... | collective-permute-start | bytes 1671176 | tf_op jit(solution)/shard_map/ppermute | solution.py:372
  96.5 14.1 %collective-permute-start.21 = (bf16[128,2176]{1,0:T(8,128)(2,1)S(1)}, bf16[128,2176]{1,0:T(8,128)(2,1)S(1)}, u32[]{:S(2)}, u32[]{:S(2)}) collective-permute-start(bf16[128,2176]{1,0:T(8,128)(2,1)S(1)} %collective-permute-done.17.refs_3_), channel_id=1, source_target_pairs={{0,1},{1,0},{2,3},{3,2},{4,5},{5,4},{6,7},{7,6},{8,9},{9,8},{10,11... | collective-permute-start | bytes 1671176 | tf_op jit(solution)/shard_map/ppermute | solution.py:372
  100.7 8.4 %collective-permute-start.15 = (bf16[2,80,1024]{2,1,0:T(8,128)(2,1)S(1)}, bf16[2,80,1024]{2,1,0:T(8,128)(2,1)S(1)}, u32[]{:S(2)}, u32[]{:S(2)}) collective-permute-start(bf16[2,80,1024]{2,1,0:T(8,128)(2,1)S(1)} %get-tuple-element.30), channel_id=1, source_target_pairs={{1,2},{3,4},{5,6},{2,1},{4,3},{6,5},{9,10},{11,12},{13,14},{10,9},... | collective-permute-start | bytes 983048 | tf_op jit(solution)/shard_map/ppermute | solution.py:381

commit v4 on v3

--- a/solution.py
+++ b/solution.py
@@ -1,3 +1,4 @@
+import functools
 import math
 
 import jax
@@ -86,7 +87,7 @@
         in_specs=[pl.BlockSpec(memory_space=pltpu.VMEM)] * 6,
         out_specs=pl.BlockSpec(memory_space=pltpu.VMEM),
         compiler_params=pltpu.CompilerParams(vmem_limit_bytes=20 * 2**20),
-        cost_estimate=pl.CostEstimate(flops=1_200_000_000, bytes_accessed=3_000_000, transcendentals=400_000),
+        cost_estimate=pl.CostEstimate(flops=3000000000, bytes_accessed=0, transcendentals=0),
         name="attend",
     )(q, kv, up, down, near, far)
 
@@ -136,53 +137,52 @@
     )(label, embed, table)
 
 
-def answer_kernel(asked_ref, table_ref, gate_ref, own_ref, answer_ref):
-    shard, width = own_ref.shape
-    answer_ref[:, 0:width] = own_ref[...]
+def answer_kernel(asked_ref, table_ref, gate_ref, answer_ref):
     row = picked_row(asked_ref[:, 128:129], table_ref[...])
     part = gate_product(row, asked_ref[:, 0:64], asked_ref[:, 64:128], gate_ref[...])
-    answer_ref[:, width : width + 128] = to_block(part)
+    answer_ref[:, 0:128] = to_block(part)
     rows = jnp.concatenate([row, row], axis=1)
-    answer_ref[:, width + 128 : width + 256] = jnp.concatenate([rows, rows], axis=0).astype(BF16)
-
-
-def answer(asked, table, gate_weight, own):
-    shard, width = own.shape
+    answer_ref[:, 128:256] = jnp.concatenate([rows, rows], axis=0).astype(BF16)
+
+
+def answer(asked, table, gate_weight):
     return pl.pallas_call(
         answer_kernel,
-        out_shape=jax.ShapeDtypeStruct((shard, width + 256), BF16),
-        in_specs=in_vmem(4),
-        out_specs=pl.BlockSpec(memory_space=pltpu.VMEM),
-        compiler_params=pltpu.CompilerParams(vmem_limit_bytes=8 * 2**20),
+        out_shape=jax.ShapeDtypeStruct((32, 256), BF16),
+        in_specs=in_vmem(3),
+        out_specs=pl.BlockSpec(memory_space=pltpu.VMEM),
+        compiler_params=pltpu.CompilerParams(vmem_limit_bytes=8 * 2**20),
+        cost_estimate=pl.CostEstimate(flops=5000000000, bytes_accessed=0, transcendentals=0),
         name="answer",
-    )(asked, table, gate_weight, own)
-
-
-def mix_kernel(own_ref, peer_ref, ask_ref, gate_ref, sent_ref):
+    )(asked, table, gate_weight)
+
+
+def mix_kernel(own_ref, peer_ref, ask_ref, answered_ref, gate_ref, sent_ref):
     shard, width = own_ref.shape
-    peer = peer_ref[:, 0:width].astype(F32)
+    peer = peer_ref[...].astype(F32)
     sent_ref[:, 0:width] = (0.5 * (own_ref[...].astype(F32) + peer)).astype(BF16)
     own_row = jnp.broadcast_to(ask_ref[:, 0:64], (16, 64))
-    peer_row = peer_ref[0:16, width + 128 : width + 192].astype(F32)
+    peer_row = answered_ref[0:16, 128:192].astype(F32)
     part = gate_product(own_row, peer_row, ask_ref[:, 64:128], gate_ref[...])
-    part = 0.5 * (part + from_block(peer_ref[:, width : width + 128]))
+    part = 0.5 * (part + from_block(answered_ref[:, 0:128]))
     sent_ref[:, width : width + 128] = to_block(part)
 
 
-def mix(own, peer, ask, gate_weight):
+def mix(own, peer, ask, answered, gate_weight):
     shard, width = own.shape
     return pl.pallas_call(
         mix_kernel,
         out_shape=jax.ShapeDtypeStruct((shard, width + 128), BF16),
-        in_specs=in_vmem(4),
-        out_specs=pl.BlockSpec(memory_space=pltpu.VMEM),
-        compiler_params=pltpu.CompilerParams(vmem_limit_bytes=8 * 2**20),
+        in_specs=in_vmem(5),
+        out_specs=pl.BlockSpec(memory_space=pltpu.VMEM),
+        compiler_params=pltpu.CompilerParams(vmem_limit_bytes=8 * 2**20),
+        cost_estimate=pl.CostEstimate(flops=5000000000, bytes_accessed=0, transcendentals=0),
         name="mix",
-    )(own, peer, ask, gate_weight)
+    )(own, peer, ask, answered, gate_weight)
 
 
 def stack_kernel(*refs):
-    parts, out_ref = refs[:4], refs[4]
+    parts, out_ref = [refs[at] for at in (0, 1, 3, 2)], refs[4]
     shard = parts[0].shape[0]
     for index, part in enumerate(parts):
         out_ref[index * shard : (index + 1) * shard, :] = part[...]
@@ -196,6 +196,7 @@
         in_specs=in_vmem(4),
         out_specs=pl.BlockSpec(memory_space=pltpu.VMEM),
         compiler_params=pltpu.CompilerParams(vmem_limit_bytes=8 * 2**20),
+        cost_estimate=pl.CostEstimate(flops=5000000000, bytes_accessed=0, transcendentals=0),
         name="stack",
     )(*parts)
 
@@ -258,7 +259,8 @@
 
 
 def project_kernel(a_ref, *refs):
-    pieces, (out_ref, lanes_ref, held_ref, sems) = refs[:8], refs[8:]
+    pieces, (out_ref, lanes_ref) = refs[:8], refs[8:]
+    pieces = [pieces[at] for at in (0, 2, 1, 3, 4, 6, 5, 7)]
     row, col = lax.axis_index("row"), lax.axis_index("col")
     core, place = lax.rem(col, 2), lax.div(col, 2)
     shard, block = 32, 256
@@ -291,12 +293,7 @@
                     span = slice(back * shard, (back + 1) * shard)
                     rows += [even[step][span, at], odd[step][span, at]]
             product = jnp.dot(lanes_ref[...], jnp.concatenate(rows, axis=0), preferred_element_type=F32)
-            held_ref[:, at] = (gate[:, at] * product).astype(BF16)
-            copy_out(part).start()
-
-    def copy_out(part):
-        at = pl.ds(part * part_width, part_width)
-        return pltpu.make_async_copy(held_ref.at[:, at], out_ref.at[:, at], sems.at[part])
+            out_ref[:, at] = (gate[:, at] * product).astype(BF16)
 
     @pl.when(core == 0)
     def _():
@@ -306,9 +303,6 @@
     def _():
         multiply(pieces[4:], pieces[:4])
 
-    for part in range(parts):
-        copy_out(part).wait()
-
 
 def project(a, pieces):
     tokens, inner = a.shape
@@ -317,12 +311,8 @@
         project_kernel,
         out_shape=jax.ShapeDtypeStruct((tokens, width), BF16),
         in_specs=in_vmem(9),
-        out_specs=pl.BlockSpec(memory_space=pltpu.HBM),
-        scratch_shapes=[
-            pltpu.VMEM((tokens, inner), BF16),
-            pltpu.VMEM((tokens, width), BF16),
-            pltpu.SemaphoreType.DMA((4,)),
-        ],
+        out_specs=pl.BlockSpec(memory_space=pltpu.VMEM),
+        scratch_shapes=[pltpu.VMEM((tokens, inner), BF16)],
         compiler_params=pltpu.CompilerParams(vmem_limit_bytes=24 * 2**20),
         cost_estimate=pl.CostEstimate(flops=810_000_000, bytes_accessed=6_000_000, transcendentals=0),
         name="project",
@@ -342,45 +332,50 @@
     dp_count, row_count, col_count = (lax.axis_size(a) for a in ("dp", "row", "col"))
     bit_count = dp_count.bit_length() - 1
     tile_rows, tile_cols, inner = queries.shape[1:]
-    kv = keyvals.reshape(2, -1, inner)
-    out_weight, gate_weight = out_weight[0], gate_weight[0]
+    up_pairs = [(i, i + 1) for i in range(row_count - 1)]
+    down_pairs = [(j, i) for i, j in up_pairs]
+    near_pairs = [(i, i ^ 1) for i in range(col_count)]
+    far_pairs = [(i, i + 1) for i in range(1, col_count - 1, 2)]
+    far_pairs = far_pairs + [(j, i) for i, j in far_pairs]
+
+    def body(distance, ask, table, gate_weight, out_weight, q, kv):
+        ahead = [(i, (i + distance) % dp_count) for i in range(dp_count)]
+        behind = [(j, i) for i, j in ahead]
+        asked = lax.ppermute(ask, "dp", behind)
+        peer = lax.ppermute(out_weight, "dp", ahead)
+        low, high = cut(kv, ask)
+        up = lax.ppermute(low, "row", up_pairs)
+        down = lax.ppermute(high, "row", down_pairs)
+        answered = lax.ppermute(answer(asked, table, gate_weight), "dp", ahead)
+        sent = mix(out_weight, peer, ask, answered, gate_weight)
+        got = [sent] + [
+            lax.ppermute(sent, "row", [(i, i ^ k) for i in range(row_count)]) for k in (1, 3, 2)
+        ]
+        stack = stacked(got)
+        opposite, beside, other = (
+            lax.ppermute(stack, "col", [(i, i ^ (2 * k)) for i in range(col_count)]) for k in (2, 1, 3)
+        )
+        near, far = edges(kv, up, down, sent)
+        far = lax.ppermute(far, "col", far_pairs)
+        near = lax.ppermute(near, "col", near_pairs)
+        attended = attend(q, kv, up, down, near, far)
+        mine, attended = lax.optimization_barrier((stack, attended))
+        siblings = [lax.ppermute(part, "col", near_pairs) for part in (mine, opposite, beside, other)]
+        return project(attended, [stack, opposite, beside, other] + siblings)
+
+    embed = time_embed(timesteps[0], gate_weight.shape[1], gate_weight.shape[2])
     table = class_table[0].T
-    power = round_index[0] % bit_count
-
-    def shifted(value, sign):
-        def branch(distance):
-            pairs = [(i, (i + sign * distance) % dp_count) for i in range(dp_count)]
-            return lambda array: lax.ppermute(array, "dp", pairs)
-
-        return lax.switch(power, [branch(2**bit) for bit in range(bit_count)], value)
-
-    embed = time_embed(timesteps[0], gate_weight.shape[0], gate_weight.shape[1])
     ask = begin(labels, embed, table)
-    asked = shifted(ask, -1)
-    peer = shifted(answer(asked, table, gate_weight, out_weight), 1)
-
-    sent = mix(out_weight, peer, ask, gate_weight)
-    got = [sent] + [
-        lax.ppermute(sent, "row", [(i, i ^ k) for i in range(row_count)]) for k in range(1, row_count)
-    ]
-    stack = stacked(got)
-    places = [stack] + [
-        lax.ppermute(stack, "col", [(i, i ^ (2 * k)) for i in range(col_count)])
-        for k in range(1, col_count // 2)
-    ]
-    near_pairs = [(i, i ^ 1) for i in range(col_count)]
-    siblings = [lax.ppermute(part, "col", near_pairs) for part in places]
-
-    low, high = cut(kv, got[1])
-    up_pairs = [(i, i + 1) for i in range(row_count - 1)]
-    up = lax.ppermute(low, "row", up_pairs)
-    down = lax.ppermute(high, "row", [(j, i) for i, j in up_pairs])
-    far_pairs = [(i, i + 1) for i in range(1, col_count - 1, 2)]
-    near, far = edges(kv, up, down, places[1])
-    near = lax.ppermute(near, "col", near_pairs)
-    far = lax.ppermute(far, "col", far_pairs + [(j, i) for i, j in far_pairs])
-    attended = attend(queries.reshape(-1, inner), kv, up, down, near, far)
-    result = project(attended, places + siblings)
+    result = lax.switch(
+        round_index[0] % bit_count,
+        [functools.partial(body, 2**bit) for bit in range(bit_count)],
+        ask,
+        table,
+        gate_weight[0],
+        out_weight[0],
+        queries.reshape(-1, inner),
+        keyvals.reshape(2, -1, inner),
+    )
     return result.reshape(1, tile_rows, tile_cols, -1)
 
 

time: 113 us -> 98.1 us (0.87)
  waiting for transfers between devices: 29.8 us -> 19.5 us
  starting transfers between devices: 70.8 us -> 67.8 us
  local copies, waits for them, and re-layouts: 2.78 us -> 0.9 us
    ppermute x16 -> x17, waiting for transfers between devices: 29.8 us -> 19.5 us  [the longest x3 12.1 us: body(): lax.ppermute(stack, 'col', [(i, i ^ 2 * k) for i in range(col_count)])]
    ppermute x16 -> x17, starting transfers between devices: 70.8 us -> 67.8 us  [the longest x1 15.5 us: body(): asked = lax.ppermute(ask, 'dp', behind)]
    unnamed x16 -> x4, local copies, waits for them, and re-layouts: 2.78 us -> 0.88 us
  transfers between devices with their start and end apart: 16 -> 17, of which waited for: 9 -> 4; matrix products, arithmetic and copies ran while one was open for 0% -> 0% of each run, Pallas kernels for 2% -> 4%
where the time goes in v4:
time: 98.1 us; the launch traced here: 97.5 us
  starting transfers between devices  67.8 us (69%)
  waiting for transfers between devices  19.5 us (20%)
  Pallas kernels  6.62 us (7%)
  between operations  2.02 us (2%)
    ppermute x1, starting transfers between devices, body(): asked = lax.ppermute(ask, 'dp', behind)  15.5 us
    ppermute x3, starting transfers between devices, body(): lax.ppermute(sent, 'row', [(i, i ^ k) for i in range(row_count)])  14 us
    ppermute x3, waiting for transfers between devices, body(): lax.ppermute(stack, 'col', [(i, i ^ 2 * k) for i in range(col_count)])  12.1 us
    ppermute x4, starting transfers between devices, body(): lax.ppermute(part, 'col', near_pairs)  11.9 us
    ppermute x3, starting transfers between devices, body(): lax.ppermute(stack, 'col', [(i, i ^ 2 * k) for i in range(col_count)])  9.6 us
    ppermute x1, waiting for transfers between devices, body(): answered = lax.ppermute(answer(asked, table, gate_weight), 'dp', ahead)  5.79 us
    ppermute x1, starting transfers between devices, body(): near = lax.ppermute(near, 'col', near_pairs)  4.78 us
    ppermute x1, starting transfers between devices, body(): far = lax.ppermute(far, 'col', far_pairs)  3.23 us
  transfers between devices with their start and end apart: 17, of which 4 were waited for; matrix products, arithmetic and copies ran while one was open for 0% of the time, Pallas kernels for 4%

profile of v4, /device:TPU:1, one launch (start us, length us, event | category | flops | bytes accessed | tf_op | source)
XLA Modules:
  0.0 97.5 jit_solution(7292410086561154432)
XLA Ops:
  2.0 0.1 compare_select_fusion.2.embed_ref
  2.1 1.0 %begin.1 = f32[1,256]{1,0:T(1,128)S(1)} custom-call(s32[1]{0:T(128)S(6)} %copy.33.label_ref, f32[1,64]{1,0:T(1,128)S(1)} %compare_select_fusion.2.embed_ref, bf16[64,1000]{1,0:T(8,128)(2,1)} %bitcast.44), custom_call_target="tpu_custom_call" | custom-call | tf_op jit(solution)/shard_map/begin/pallas_call | solution.py:130
  3.1 93.6 %conditional.1 = (bf16[1,12,16,2048]{3,2,1,0:T(8,128)(2,1)S(1)}) conditional(s32[]{:T(128)} %clamp.3, (bf16[1,32,2048]{2,1,0:T(8,128)(2,1)}, f32[1,256]{1,0:T(1,128)S(1)}, bf16[1,64,2048]{2,1,0:T(8,128)(2,1)}, bf16[64,1000]{1,0:T(8,128)(2,1)S(1)}, bf16[1,12,16,1024]{3,2,1,0:T(8,128)(2,1)}, ...), branch_computations={%region_0.1_spmd, %region_1.2_spmd, %region_2.3_spmd, %region_3.4_... | conditional | flops 18809999360 | bytes 34349216 | solution.py:369
  3.1 15.5 %collective-permute-start.1 = (f32[1,256]{1,0:T(1,128)S(1)}, f32[1,256]{1,0:T(1,128)S(1)}, u32[]{:S(2)}, u32[]{:S(2)}) collective-permute-start(f32[1,256]{1,0:T(1,128)S(1)} %get-tuple-element.76.ask_ref.after_ref), channel_id=1, source_target_pairs={{32,0},{64,32},{96,64},{128,96},{160,128},{192,160},{224,192},{256... | collective-permute-start | bytes 3080 | tf_op jit(solution)/shard_map/cond/branch_0_fun/ppermute | solution.py:344
  18.6 1.9 %collective-permute-start = (bf16[32,2048]{1,0:T(8,128)(2,1)}, bf16[32,2048]{1,0:T(8,128)(2,1)S(1)}, u32[]{:S(2)}, u32[]{:S(2)}) collective-permute-start(bf16[32,2048]{1,0:T(8,128)(2,1)} %bitcast.61), channel_id=1, source_target_pairs={{0,32},{32,64},{64,96},{96,128},{128,160},{160,192},{192,224},{224... | collective-permute-start | bytes 393224 | tf_op jit(solution)/shard_map/cond/branch_0_fun/ppermute | solution.py:345
  20.5 0.0 collective-permute-done.1.asked_ref
  20.5 0.0 copy-start
  20.6 1.4 %answer.4 = bf16[32,256]{1,0:T(8,128)(2,1)S(1)} custom-call(f32[1,256]{1,0:T(1,128)S(1)} %collective-permute-done.1.asked_ref, bf16[64,1000]{1,0:T(8,128)(2,1)S(1)} %get-tuple-element.77.table_ref, bf16[64,2048]{1,0:T(8,128)(2,1)} %bitcast.53), custom_call_target="tpu_custom_call" | custom-call | flops 5000000000 | tf_op jit(solution)/shard_map/cond/branch_0_fun/answer/pallas_call | solution.py:149
  22.0 3.0 %collective-permute-start.2 = (bf16[32,256]{1,0:T(8,128)(2,1)S(1)}, bf16[32,256]{1,0:T(8,128)(2,1)S(1)}, u32[]{:S(2)}, u32[]{:S(2)}) collective-permute-start(bf16[32,256]{1,0:T(8,128)(2,1)S(1)} %answer.4), channel_id=1, source_target_pairs={{0,32},{32,64},{64,96},{96,128},{128,160},{160,192},{192,224},{224... | collective-permute-start | bytes 49160 | tf_op jit(solution)/shard_map/cond/branch_0_fun/ppermute | solution.py:349
  25.0 0.0 copy-start.10
  25.0 0.0 copy-start.14
  25.0 0.3 cut.4
  25.3 2.7 %collective-permute-start.6 = (bf16[2,48,1024]{2,1,0:T(8,128)(2,1)S(1)}, bf16[2,48,1024]{2,1,0:T(8,128)(2,1)S(1)}, u32[]{:S(2)}, u32[]{:S(2)}) collective-permute-start(bf16[2,48,1024]{2,1,0:T(8,128)(2,1)S(1)} %get-tuple-element.81), channel_id=1, source_target_pairs={{0,8},{8,16},{16,24},{1,9},{9,17},{17,25},{2,10},{10,18},{18,26},{... | collective-permute-start | bytes 589832 | tf_op jit(solution)/shard_map/cond/branch_0_fun/ppermute | solution.py:347
  28.0 1.3 %collective-permute-start.7 = (bf16[2,48,1024]{2,1,0:T(8,128)(2,1)S(1)}, bf16[2,48,1024]{2,1,0:T(8,128)(2,1)S(1)}, u32[]{:S(2)}, u32[]{:S(2)}) collective-permute-start(bf16[2,48,1024]{2,1,0:T(8,128)(2,1)S(1)} %get-tuple-element.82), channel_id=1, source_target_pairs={{8,0},{16,8},{24,16},{9,1},{17,9},{25,17},{10,2},{18,10},{26,18},{... | collective-permute-start | bytes 589832 | tf_op jit(solution)/shard_map/cond/branch_0_fun/ppermute | solution.py:348
  29.3 5.8 %collective-permute-done.2.answered_ref = bf16[32,256]{1,0:T(8,128)(2,1)S(1)} collective-permute-done((bf16[32,256]{1,0:T(8,128)(2,1)S(1)}, bf16[32,256]{1,0:T(8,128)(2,1)S(1)}, u32[]{:S(2)}, u32[]{:S(2)}) %collective-permute-start.2) | collective-permute-done | bytes 16416 | tf_op jit(solution)/shard_map/cond/branch_0_fun/ppermute | solution.py:349
  35.1 0.0 collective-permute-done.peer_ref
  35.1 0.2 mix.4.refs_0_.after_ref
  35.3 6.6 %collective-permute-start.5 = (bf16[32,2176]{1,0:T(8,128)(2,1)S(1)}, bf16[32,2176]{1,0:T(8,128)(2,1)S(1)}, u32[]{:S(2)}, u32[]{:S(2)}) collective-permute-start(bf16[32,2176]{1,0:T(8,128)(2,1)S(1)} %mix.4.refs_0_.after_ref), channel_id=1, source_target_pairs={{0,16},{8,24},{16,0},{24,8},{1,17},{9,25},{17,1},{25,9},{2,18},{10... | collective-permute-start | bytes 417800 | tf_op jit(solution)/shard_map/cond/branch_0_fun/ppermute | solution.py:352
  42.0 5.4 %collective-permute-start.4 = (bf16[32,2176]{1,0:T(8,128)(2,1)S(1)}, bf16[32,2176]{1,0:T(8,128)(2,1)S(1)}, u32[]{:S(2)}, u32[]{:S(2)}) collective-permute-start(bf16[32,2176]{1,0:T(8,128)(2,1)S(1)} %mix.4.refs_0_.after_ref), channel_id=1, source_target_pairs={{0,24},{8,16},{16,8},{24,0},{1,25},{9,17},{17,9},{25,1},{2,26},{10... | collective-permute-start | bytes 417800 | tf_op jit(solution)/shard_map/cond/branch_0_fun/ppermute | solution.py:352
  47.4 1.9 %collective-permute-start.3 = (bf16[32,2176]{1,0:T(8,128)(2,1)S(1)}, bf16[32,2176]{1,0:T(8,128)(2,1)S(1)}, u32[]{:S(2)}, u32[]{:S(2)}) collective-permute-start(bf16[32,2176]{1,0:T(8,128)(2,1)S(1)} %mix.4.refs_0_.after_ref), channel_id=1, source_target_pairs={{0,8},{8,0},{16,24},{24,16},{1,9},{9,1},{17,25},{25,17},{2,10},{10... | collective-permute-start | bytes 417800 | tf_op jit(solution)/shard_map/cond/branch_0_fun/ppermute | solution.py:352
  49.3 0.0 collective-permute-done.6.up_ref
  49.3 0.0 collective-permute-done.7.down_ref
  49.3 0.7 edges.4
  50.0 4.8 %collective-permute-start.8 = (bf16[2,80,1024]{2,1,0:T(8,128)(2,1)S(1)}, bf16[2,80,1024]{2,1,0:T(8,128)(2,1)S(1)}, u32[]{:S(2)}, u32[]{:S(2)}) collective-permute-start(bf16[2,80,1024]{2,1,0:T(8,128)(2,1)S(1)} %get-tuple-element.83), channel_id=1, source_target_pairs={{0,1},{1,0},{2,3},{3,2},{4,5},{5,4},{6,7},{7,6},{8,9},{9,8},{10,11... | collective-permute-start | bytes 983048 | tf_op jit(solution)/shard_map/cond/branch_0_fun/ppermute | solution.py:360
  54.8 0.0 copy-start.6
  54.8 3.2 %collective-permute-start.9 = (bf16[2,80,1024]{2,1,0:T(8,128)(2,1)S(1)}, bf16[2,80,1024]{2,1,0:T(8,128)(2,1)S(1)}, u32[]{:S(2)}, u32[]{:S(2)}) collective-permute-start(bf16[2,80,1024]{2,1,0:T(8,128)(2,1)S(1)} %get-tuple-element.84), channel_id=1, source_target_pairs={{1,2},{3,4},{5,6},{2,1},{4,3},{6,5},{9,10},{11,12},{13,14},{10,9},... | collective-permute-start | bytes 983048 | tf_op jit(solution)/shard_map/cond/branch_0_fun/ppermute | solution.py:359
  58.1 0.0 collective-permute-done.5.refs_3_
  58.1 0.0 collective-permute-done.4.refs_2_
  58.1 0.0 collective-permute-done.3.refs_1_
  58.2 3.0 %collective-permute-start.12 = (bf16[128,2176]{1,0:T(8,128)(2,1)S(1)}, bf16[128,2176]{1,0:T(8,128)(2,1)S(1)}, u32[]{:S(2)}, u32[]{:S(2)}) collective-permute-start(bf16[128,2176]{1,0:T(8,128)(2,1)S(1)} %stack.4.refs_0_), channel_id=1, source_target_pairs={{0,6},{1,7},{2,4},{3,5},{4,2},{5,3},{6,0},{7,1},{8,14},{9,15},{10,... | collective-permute-start | bytes 1671176 | tf_op jit(solution)/shard_map/cond/branch_0_fun/ppermute | solution.py:356
  61.2 3.1 %collective-permute-start.11 = (bf16[128,2176]{1,0:T(8,128)(2,1)S(1)}, bf16[128,2176]{1,0:T(8,128)(2,1)S(1)}, u32[]{:S(2)}, u32[]{:S(2)}) collective-permute-start(bf16[128,2176]{1,0:T(8,128)(2,1)S(1)} %stack.4.refs_0_), channel_id=1, source_target_pairs={{0,2},{1,3},{2,0},{3,1},{4,6},{5,7},{6,4},{7,5},{8,10},{9,11},{10,... | collective-permute-start | bytes 1671176 | tf_op jit(solution)/shard_map/cond/branch_0_fun/ppermute | solution.py:356
  64.3 3.5 %collective-permute-start.10 = (bf16[128,2176]{1,0:T(8,128)(2,1)S(1)}, bf16[128,2176]{1,0:T(8,128)(2,1)S(1)}, u32[]{:S(2)}, u32[]{:S(2)}) collective-permute-start(bf16[128,2176]{1,0:T(8,128)(2,1)S(1)} %stack.4.refs_0_), channel_id=1, source_target_pairs={{0,4},{1,5},{2,6},{3,7},{4,0},{5,1},{6,2},{7,3},{8,12},{9,13},{10,... | collective-permute-start | bytes 1671176 | tf_op jit(solution)/shard_map/cond/branch_0_fun/ppermute | solution.py:356
  67.8 0.0 collective-permute-done.8.near_ref
  67.8 0.0 collective-permute-done.9.far_ref
  67.8 1.4 %attend.4.a_ref = bf16[192,1024]{1,0:T(8,128)(2,1)S(1)} custom-call(bf16[192,1024]{1,0:T(8,128)(2,1)S(1)} %bitcast.49, bf16[2,192,1024]{2,1,0:T(8,128)(2,1)S(1)} %bitcast.30, bf16[2,48,1024]{2,1,0:T(8,128)(2,1)S(1)} %collective-permute-done.6.up_ref, bf16[2,48,1024]{2,1,0:T(8,128)(2,1)S(1)} %collective-permute-done.7.down_ref, ...), custom_call_target="tpu_custom_call" | custom-call | flops 3000000000 | tf_op jit(solution)/shard_map/cond/branch_0_fun/attend/pallas_call | solution.py:84
  69.2 2.5 %collective-permute-start.13 = (bf16[128,2176]{1,0:T(8,128)(2,1)S(1)}, bf16[128,2176]{1,0:T(8,128)(2,1)S(1)}, u32[]{:S(2)}, u32[]{:S(2)}) collective-permute-start(bf16[128,2176]{1,0:T(8,128)(2,1)S(1)} %stack.4.refs_0_), channel_id=1, source_target_pairs={{0,1},{1,0},{2,3},{3,2},{4,5},{5,4},{6,7},{7,6},{8,9},{9,8},{10,11... | collective-permute-start | bytes 1671176 | tf_op jit(solution)/shard_map/cond/branch_0_fun/ppermute | solution.py:363
  71.8 3.9 %collective-permute-done.12.refs_3_ = bf16[128,2176]{1,0:T(8,128)(2,1)S(1)} collective-permute-done((bf16[128,2176]{1,0:T(8,128)(2,1)S(1)}, bf16[128,2176]{1,0:T(8,128)(2,1)S(1)}, u32[]{:S(2)}, u32[]{:S(2)}) %collective-permute-start.12) | collective-permute-done | bytes 557088 | tf_op jit(solution)/shard_map/cond/branch_0_fun/ppermute | solution.py:356
  75.6 2.6 %collective-permute-start.16 = (bf16[128,2176]{1,0:T(8,128)(2,1)S(1)}, bf16[128,2176]{1,0:T(8,128)(2,1)S(1)}, u32[]{:S(2)}, u32[]{:S(2)}) collective-permute-start(bf16[128,2176]{1,0:T(8,128)(2,1)S(1)} %collective-permute-done.12.refs_3_), channel_id=1, source_target_pairs={{0,1},{1,0},{2,3},{3,2},{4,5},{5,4},{6,7},{7,6},{8,9},{9,8},{10,11... | collective-permute-start | bytes 1671176 | tf_op jit(solution)/shard_map/cond/branch_0_fun/ppermute | solution.py:363
  78.2 0.0 collective-permute-done.11.refs_2_
  78.2 4.0 %collective-permute-start.15 = (bf16[128,2176]{1,0:T(8,128)(2,1)S(1)}, bf16[128,2176]{1,0:T(8,128)(2,1)S(1)}, u32[]{:S(2)}, u32[]{:S(2)}) collective-permute-start(bf16[128,2176]{1,0:T(8,128)(2,1)S(1)} %collective-permute-done.11.refs_2_), channel_id=1, source_target_pairs={{0,1},{1,0},{2,3},{3,2},{4,5},{5,4},{6,7},{7,6},{8,9},{9,8},{10,11... | collective-permute-start | bytes 1671176 | tf_op jit(solution)/shard_map/cond/branch_0_fun/ppermute | solution.py:363
  82.3 8.2 %collective-permute-done.10.refs_1_ = bf16[128,2176]{1,0:T(8,128)(2,1)S(1)} collective-permute-done((bf16[128,2176]{1,0:T(8,128)(2,1)S(1)}, bf16[128,2176]{1,0:T(8,128)(2,1)S(1)}, u32[]{:S(2)}, u32[]{:S(2)}) %collective-permute-start.10) | collective-permute-done | bytes 557088 | tf_op jit(solution)/shard_map/cond/branch_0_fun/ppermute | solution.py:356
  90.5 2.8 %collective-permute-start.14 = (bf16[128,2176]{1,0:T(8,128)(2,1)S(1)}, bf16[128,2176]{1,0:T(8,128)(2,1)S(1)}, u32[]{:S(2)}, u32[]{:S(2)}) collective-permute-start(bf16[128,2176]{1,0:T(8,128)(2,1)S(1)} %collective-permute-done.10.refs_1_), channel_id=1, source_target_pairs={{0,1},{1,0},{2,3},{3,2},{4,5},{5,4},{6,7},{7,6},{8,9},{9,8},{10,11... | collective-permute-start | bytes 1671176 | tf_op jit(solution)/shard_map/cond/branch_0_fun/ppermute | solution.py:363
  93.3 0.0 collective-permute-done.13.refs_4_
  93.3 0.0 collective-permute-done.16.refs_7_
  93.3 1.5 %collective-permute-done.14.refs_5_ = bf16[128,2176]{1,0:T(8,128)(2,1)S(1)} collective-permute-done((bf16[128,2176]{1,0:T(8,128)(2,1)S(1)}, bf16[128,2176]{1,0:T(8,128)(2,1)S(1)}, u32[]{:S(2)}, u32[]{:S(2)}) %collective-permute-start.14) | collective-permute-done | bytes 557088 | tf_op jit(solution)/shard_map/cond/branch_0_fun/ppermute | solution.py:363
  94.8 1.5 %project.4 = bf16[192,2048]{1,0:T(8,128)(2,1)S(1)} custom-call(bf16[192,1024]{1,0:T(8,128)(2,1)S(1)} %attend.4.a_ref, bf16[128,2176]{1,0:T(8,128)(2,1)S(1)} %stack.4.refs_0_, bf16[128,2176]{1,0:T(8,128)(2,1)S(1)} %collective-permute-done.10.refs_1_, bf16[128,2176]{1,0:T(8,128)(2,1)S(1)} %collective-permute-done.11.refs_2_, ...), custom_call_target="tpu_custom_call" | custom-call | flops 810000000 | bytes 6000000 | tf_op jit(solution)/shard_map/cond/branch_0_fun/project/pallas_call | solution.py:310
  96.6 0.0 copy-start.4
  96.6 0.9 copy-done.4
  (8 shorter events, 0.1 us)
Async XLA Ops:
  0.0 3.1 %copy-start.5 = (bf16[1,1000,64]{1,2,0:T(8,128)(2,1)S(1)}, bf16[1,1000,64]{1,2,0:T(8,128)(2,1)}, u32[]{:S(2)}) copy-start(bf16[1,1000,64]{1,2,0:T(8,128)(2,1)} %param.16) | copy-start | bytes 384004
  3.1 17.5 %collective-permute-start.1 = (f32[1,256]{1,0:T(1,128)S(1)}, f32[1,256]{1,0:T(1,128)S(1)}, u32[]{:S(2)}, u32[]{:S(2)}) collective-permute-start(f32[1,256]{1,0:T(1,128)S(1)} %get-tuple-element.76.ask_ref.after_ref), channel_id=1, source_target_pairs={{32,0},{64,32},{96,64},{128,96},{160,128},{192,160},{224,192},{256... | collective-permute-start | bytes 3080 | tf_op jit(solution)/shard_map/cond/branch_0_fun/ppermute | solution.py:344
  18.6 16.5 %collective-permute-start = (bf16[32,2048]{1,0:T(8,128)(2,1)}, bf16[32,2048]{1,0:T(8,128)(2,1)S(1)}, u32[]{:S(2)}, u32[]{:S(2)}) collective-permute-start(bf16[32,2048]{1,0:T(8,128)(2,1)} %bitcast.61), channel_id=1, source_target_pairs={{0,32},{32,64},{64,96},{96,128},{128,160},{160,192},{192,224},{224... | collective-permute-start | bytes 393224 | tf_op jit(solution)/shard_map/cond/branch_0_fun/ppermute | solution.py:345
  20.5 4.5 %copy-start = (bf16[1,2,12,16,1024]{4,3,2,1,0:T(8,128)(2,1)S(1)}, bf16[1,2,12,16,1024]{4,3,2,1,0:T(8,128)(2,1)}, u32[]{:S(2)}) copy-start(bf16[1,2,12,16,1024]{4,3,2,1,0:T(8,128)(2,1)} %get-tuple-element.152) | copy-start | bytes 2359300 | tf_op jit(solution)/shard_map/cond
  22.0 13.1 %collective-permute-start.2 = (bf16[32,256]{1,0:T(8,128)(2,1)S(1)}, bf16[32,256]{1,0:T(8,128)(2,1)S(1)}, u32[]{:S(2)}, u32[]{:S(2)}) collective-permute-start(bf16[32,256]{1,0:T(8,128)(2,1)S(1)} %answer.4), channel_id=1, source_target_pairs={{0,32},{32,64},{64,96},{96,128},{128,160},{160,192},{192,224},{224... | collective-permute-start | bytes 49160 | tf_op jit(solution)/shard_map/cond/branch_0_fun/ppermute | solution.py:349
  25.0 10.1 %copy-start.10 = (bf16[1,64,2048]{2,1,0:T(8,128)(2,1)S(1)}, bf16[1,64,2048]{2,1,0:T(8,128)(2,1)}, u32[]{:S(2)}) copy-start(bf16[1,64,2048]{2,1,0:T(8,128)(2,1)} %get-tuple-element.144) | copy-start | bytes 786436 | tf_op jit(solution)/shard_map/cond
  25.0 10.1 %copy-start.14 = (bf16[1,32,2048]{2,1,0:T(8,128)(2,1)S(1)}, bf16[1,32,2048]{2,1,0:T(8,128)(2,1)}, u32[]{:S(2)}) copy-start(bf16[1,32,2048]{2,1,0:T(8,128)(2,1)} %get-tuple-element.140) | copy-start | bytes 393220 | tf_op jit(solution)/shard_map/cond
  25.3 24.0 %collective-permute-start.6 = (bf16[2,48,1024]{2,1,0:T(8,128)(2,1)S(1)}, bf16[2,48,1024]{2,1,0:T(8,128)(2,1)S(1)}, u32[]{:S(2)}, u32[]{:S(2)}) collective-permute-start(bf16[2,48,1024]{2,1,0:T(8,128)(2,1)S(1)} %get-tuple-element.81), channel_id=1, source_target_pairs={{0,8},{8,16},{16,24},{1,9},{9,17},{17,25},{2,10},{10,18},{18,26},{... | collective-permute-start | bytes 589832 | tf_op jit(solution)/shard_map/cond/branch_0_fun/ppermute | solution.py:347
  28.0 21.4 %collective-permute-start.7 = (bf16[2,48,1024]{2,1,0:T(8,128)(2,1)S(1)}, bf16[2,48,1024]{2,1,0:T(8,128)(2,1)S(1)}, u32[]{:S(2)}, u32[]{:S(2)}) collective-permute-start(bf16[2,48,1024]{2,1,0:T(8,128)(2,1)S(1)} %get-tuple-element.82), channel_id=1, source_target_pairs={{8,0},{16,8},{24,16},{9,1},{17,9},{25,17},{10,2},{18,10},{26,18},{... | collective-permute-start | bytes 589832 | tf_op jit(solution)/shard_map/cond/branch_0_fun/ppermute | solution.py:348
  35.3 22.8 %collective-permute-start.5 = (bf16[32,2176]{1,0:T(8,128)(2,1)S(1)}, bf16[32,2176]{1,0:T(8,128)(2,1)S(1)}, u32[]{:S(2)}, u32[]{:S(2)}) collective-permute-start(bf16[32,2176]{1,0:T(8,128)(2,1)S(1)} %mix.4.refs_0_.after_ref), channel_id=1, source_target_pairs={{0,16},{8,24},{16,0},{24,8},{1,17},{9,25},{17,1},{25,9},{2,18},{10... | collective-permute-start | bytes 417800 | tf_op jit(solution)/shard_map/cond/branch_0_fun/ppermute | solution.py:352
  42.0 16.1 %collective-permute-start.4 = (bf16[32,2176]{1,0:T(8,128)(2,1)S(1)}, bf16[32,2176]{1,0:T(8,128)(2,1)S(1)}, u32[]{:S(2)}, u32[]{:S(2)}) collective-permute-start(bf16[32,2176]{1,0:T(8,128)(2,1)S(1)} %mix.4.refs_0_.after_ref), channel_id=1, source_target_pairs={{0,24},{8,16},{16,8},{24,0},{1,25},{9,17},{17,9},{25,1},{2,26},{10... | collective-permute-start | bytes 417800 | tf_op jit(solution)/shard_map/cond/branch_0_fun/ppermute | solution.py:352
  47.4 10.7 %collective-permute-start.3 = (bf16[32,2176]{1,0:T(8,128)(2,1)S(1)}, bf16[32,2176]{1,0:T(8,128)(2,1)S(1)}, u32[]{:S(2)}, u32[]{:S(2)}) collective-permute-start(bf16[32,2176]{1,0:T(8,128)(2,1)S(1)} %mix.4.refs_0_.after_ref), channel_id=1, source_target_pairs={{0,8},{8,0},{16,24},{24,16},{1,9},{9,1},{17,25},{25,17},{2,10},{10... | collective-permute-start | bytes 417800 | tf_op jit(solution)/shard_map/cond/branch_0_fun/ppermute | solution.py:352
  50.0 17.7 %collective-permute-start.8 = (bf16[2,80,1024]{2,1,0:T(8,128)(2,1)S(1)}, bf16[2,80,1024]{2,1,0:T(8,128)(2,1)S(1)}, u32[]{:S(2)}, u32[]{:S(2)}) collective-permute-start(bf16[2,80,1024]{2,1,0:T(8,128)(2,1)S(1)} %get-tuple-element.83), channel_id=1, source_target_pairs={{0,1},{1,0},{2,3},{3,2},{4,5},{5,4},{6,7},{7,6},{8,9},{9,8},{10,11... | collective-permute-start | bytes 983048 | tf_op jit(solution)/shard_map/cond/branch_0_fun/ppermute | solution.py:360
  54.8 13.0 %copy-start.6 = (bf16[1,12,16,1024]{3,2,1,0:T(8,128)(2,1)S(1)}, bf16[1,12,16,1024]{3,2,1,0:T(8,128)(2,1)}, u32[]{:S(2)}) copy-start(bf16[1,12,16,1024]{3,2,1,0:T(8,128)(2,1)} %get-tuple-element.148) | copy-start | bytes 1179652 | tf_op jit(solution)/shard_map/cond
  54.8 13.0 %collective-permute-start.9 = (bf16[2,80,1024]{2,1,0:T(8,128)(2,1)S(1)}, bf16[2,80,1024]{2,1,0:T(8,128)(2,1)S(1)}, u32[]{:S(2)}, u32[]{:S(2)}) collective-permute-start(bf16[2,80,1024]{2,1,0:T(8,128)(2,1)S(1)} %get-tuple-element.84), channel_id=1, source_target_pairs={{1,2},{3,4},{5,6},{2,1},{4,3},{6,5},{9,10},{11,12},{13,14},{10,9},... | collective-permute-start | bytes 983048 | tf_op jit(solution)/shard_map/cond/branch_0_fun/ppermute | solution.py:359
  58.2 17.5 %collective-permute-start.12 = (bf16[128,2176]{1,0:T(8,128)(2,1)S(1)}, bf16[128,2176]{1,0:T(8,128)(2,1)S(1)}, u32[]{:S(2)}, u32[]{:S(2)}) collective-permute-start(bf16[128,2176]{1,0:T(8,128)(2,1)S(1)} %stack.4.refs_0_), channel_id=1, source_target_pairs={{0,6},{1,7},{2,4},{3,5},{4,2},{5,3},{6,0},{7,1},{8,14},{9,15},{10,... | collective-permute-start | bytes 1671176 | tf_op jit(solution)/shard_map/cond/branch_0_fun/ppermute | solution.py:356
  61.2 17.1 %collective-permute-start.11 = (bf16[128,2176]{1,0:T(8,128)(2,1)S(1)}, bf16[128,2176]{1,0:T(8,128)(2,1)S(1)}, u32[]{:S(2)}, u32[]{:S(2)}) collective-permute-start(bf16[128,2176]{1,0:T(8,128)(2,1)S(1)} %stack.4.refs_0_), channel_id=1, source_target_pairs={{0,2},{1,3},{2,0},{3,1},{4,6},{5,7},{6,4},{7,5},{8,10},{9,11},{10,... | collective-permute-start | bytes 1671176 | tf_op jit(solution)/shard_map/cond/branch_0_fun/ppermute | solution.py:356
  64.3 26.2 %collective-permute-start.10 = (bf16[128,2176]{1,0:T(8,128)(2,1)S(1)}, bf16[128,2176]{1,0:T(8,128)(2,1)S(1)}, u32[]{:S(2)}, u32[]{:S(2)}) collective-permute-start(bf16[128,2176]{1,0:T(8,128)(2,1)S(1)} %stack.4.refs_0_), channel_id=1, source_target_pairs={{0,4},{1,5},{2,6},{3,7},{4,0},{5,1},{6,2},{7,3},{8,12},{9,13},{10,... | collective-permute-start | bytes 1671176 | tf_op jit(solution)/shard_map/cond/branch_0_fun/ppermute | solution.py:356
  69.2 24.0 %collective-permute-start.13 = (bf16[128,2176]{1,0:T(8,128)(2,1)S(1)}, bf16[128,2176]{1,0:T(8,128)(2,1)S(1)}, u32[]{:S(2)}, u32[]{:S(2)}) collective-permute-start(bf16[128,2176]{1,0:T(8,128)(2,1)S(1)} %stack.4.refs_0_), channel_id=1, source_target_pairs={{0,1},{1,0},{2,3},{3,2},{4,5},{5,4},{6,7},{7,6},{8,9},{9,8},{10,11... | collective-permute-start | bytes 1671176 | tf_op jit(solution)/shard_map/cond/branch_0_fun/ppermute | solution.py:363
  75.6 17.6 %collective-permute-start.16 = (bf16[128,2176]{1,0:T(8,128)(2,1)S(1)}, bf16[128,2176]{1,0:T(8,128)(2,1)S(1)}, u32[]{:S(2)}, u32[]{:S(2)}) collective-permute-start(bf16[128,2176]{1,0:T(8,128)(2,1)S(1)} %collective-permute-done.12.refs_3_), channel_id=1, source_target_pairs={{0,1},{1,0},{2,3},{3,2},{4,5},{5,4},{6,7},{7,6},{8,9},{9,8},{10,11... | collective-permute-start | bytes 1671176 | tf_op jit(solution)/shard_map/cond/branch_0_fun/ppermute | solution.py:363
  78.2 15.1 %collective-permute-start.15 = (bf16[128,2176]{1,0:T(8,128)(2,1)S(1)}, bf16[128,2176]{1,0:T(8,128)(2,1)S(1)}, u32[]{:S(2)}, u32[]{:S(2)}) collective-permute-start(bf16[128,2176]{1,0:T(8,128)(2,1)S(1)} %collective-permute-done.11.refs_2_), channel_id=1, source_target_pairs={{0,1},{1,0},{2,3},{3,2},{4,5},{5,4},{6,7},{7,6},{8,9},{9,8},{10,11... | collective-permute-start | bytes 1671176 | tf_op jit(solution)/shard_map/cond/branch_0_fun/ppermute | solution.py:363
  90.5 4.3 %collective-permute-start.14 = (bf16[128,2176]{1,0:T(8,128)(2,1)S(1)}, bf16[128,2176]{1,0:T(8,128)(2,1)S(1)}, u32[]{:S(2)}, u32[]{:S(2)}) collective-permute-start(bf16[128,2176]{1,0:T(8,128)(2,1)S(1)} %collective-permute-done.10.refs_1_), channel_id=1, source_target_pairs={{0,1},{1,0},{2,3},{3,2},{4,5},{5,4},{6,7},{7,6},{8,9},{9,8},{10,11... | collective-permute-start | bytes 1671176 | tf_op jit(solution)/shard_map/cond/branch_0_fun/ppermute | solution.py:363
  96.6 0.9 copy-start.4
